TPU v7x, 512 devices: a whole 4x8x8 slice. The times are simulated.
512 devices in a mesh: dp: 16 (over z, core), tensor: 32 (over x, y).
Axes of the slice: x: 4, y: 8, z: 8, core: 2. Of those that a mesh axis runs over, the one named last changes fastest.
Arguments:
- activations: bfloat16 [12288, 4096], P('dp', 'tensor'), may hold values from -6 to 6
- out_grads_t: bfloat16 [5504, 12288], P('tensor', 'dp'), may hold values from -6 to 6
- in_basis: bfloat16 [4096, 4096], P(None, 'tensor'), may hold values from -0.09375 to 0.09375
- out_basis_t: bfloat16 [5504, 5504], P('tensor'), may hold values from -0.078125 to 0.078125
- query_proj: bfloat16 [4, 5504, 4096], P(None, 'tensor', 'dp'), may hold values from -6 to 6
- eigvals: float32 [5504, 4096], P('tensor', 'dp'), may hold values from 0.05 to 5
- damping: float32 [1], replicated, may hold values from 0.05 to 0.2
- lengths: int32 [96], P('dp'), may hold values from 1 to 128, 7680 in all
Outputs:
- scores: float32 [96, 4], P('dp')
Inputs may be any that keep to these rules, and one draw needn't show every extreme that they name: `lengths`: the largest token count is exactly 128.
All inputs are finite; a program needn't handle non-finite values. No bound on the sum of `lengths` on one device may be relied on, other than what follows from the above.
Results may differ from a plain program's by a relative error of at most 0.006.
Values may be sent and summed in bfloat16 or wider, within the bound.
No kernel may reach another device: no remote copies, remote signals or barrier semaphores. Data moves between devices by JAX's collectives and lax.ppermute only.
A program may use at most 128 MiB of HBM per device.

v0:
```python
import jax
import jax.numpy as jnp
from jax import lax
from jax.sharding import PartitionSpec as P


def local(activations, out_grads_t, in_basis, out_basis_t, query_proj, eigvals, damping, lengths):
    full_act = lax.all_gather(activations, "tensor", axis=1, tiled=True)
    act_local = jnp.dot(full_act, in_basis, preferred_element_type=jnp.float32).astype(jnp.bfloat16)
    act_proj = lax.all_gather(act_local, "tensor", axis=1, tiled=True)
    token_rows = full_act.shape[0]
    width = out_basis_t.shape[0]
    grad_full = jnp.dot(
        out_basis_t,
        lax.all_gather(out_grads_t, "tensor", axis=0, tiled=True),
        preferred_element_type=jnp.float32,
    )
    seq_count = lengths.shape[0]
    seq_len = token_rows // seq_count
    position = lax.broadcasted_iota(jnp.int32, (seq_count, seq_len), 1)
    keep = (position < lengths[:, None]).astype(jnp.float32).reshape(1, token_rows)
    grad_proj = (grad_full * keep).astype(jnp.bfloat16)
    scaled = (query_proj.astype(jnp.float32) / (eigvals + damping[0])).astype(jnp.bfloat16)
    projected = jnp.einsum(
        "jst,std->sjd",
        grad_proj.reshape(width, seq_count, seq_len),
        act_proj.reshape(seq_count, seq_len, act_proj.shape[1]),
        preferred_element_type=jnp.float32,
    )
    partial_value = jnp.einsum(
        "sij,qij->sq",
        projected,
        lax.all_gather(scaled, "dp", axis=2, tiled=True).astype(jnp.float32),
    )
    totals = lax.psum(partial_value, "tensor")
    norm_factor = (act_proj.shape[1] * out_basis_t.shape[1] * seq_len) ** (-0.5)
    return totals * norm_factor


def solution(mesh):
    placed = (
        P("dp", "tensor"),
        P("tensor", "dp"),
        P(None, "tensor"),
        P("tensor", None),
        P(None, "tensor", "dp"),
        P("tensor", "dp"),
        P(),
        P("dp"),
    )
    return jax.shard_map(
        local, mesh=mesh, in_specs=placed, out_specs=P("dp", None), check_vma=False
    )
```

profile of v0, /device:TPU:64, one launch (start us, length us, event | category | flops | bytes accessed | tf_op | source)
XLA Modules:
  0.0 474.7 jit_solution(10755105774203012612)
XLA Ops:
  6.5 0.0 copy-start
  6.5 0.0 all-gather.6.cloned.1.call-start
  6.6 0.7 all-gather.6.cloned.1.call-update
  7.3 0.0 all-gather.12.cloned.1.call-start
  7.3 0.7 all-gather.12.cloned.1.call-update
  8.0 0.0 all-gather.8.cloned.1.call-start
  8.1 104.2 %all-gather.6.cloned.1.call-done = bf16[768,4096]{1,0:T(8,128)(2,1)} async-done(((bf16[768,128]{1,0:T(8,128)(2,1)}), bf16[768,4096]{1,0:T(8,128)(2,1)}) %all-gather.6.cloned.1.call-update) | async-done | bytes 6291472 | tf_op jit(solution)/shard_map/all_gather | solution.py:8
  112.3 5.5 %convolution_convert_fusion = bf16[768,128]{1,0:T(8,128)(2,1)} fusion(bf16[768,4096]{1,0:T(8,128)(2,1)} %all-gather.6.cloned.1.call-done, bf16[4096,128]{1,0:T(8,128)(2,1)} %param.10), kind=kOutput, calls=%fused_computation.4 | convolution fusion | flops 805404672 | bytes 7536640 | tf_op jit(solution)/shard_map/dot_general | solution.py:9
  117.8 0.0 all-gather.8.cloned.1.call-update
  117.8 0.0 all-gather.10.cloned.1.call-start
  118.5 0.0 copy-done.2
  118.5 0.9 fusion.6
  119.5 0.0 all-gather.10.cloned.1.call-update
  119.5 0.1 convert_bitcast_fusion
  119.6 100.5 %all-gather.12.cloned.1.call-done = bf16[32,172,768]{2,1,0:T(8,128)(2,1)} async-done(((bf16[1,172,768]{2,1,0:T(8,128)(2,1)}), bf16[32,172,768]{2,1,0:T(8,128)(2,1)}) %all-gather.12.cloned.1.call-update) | async-done | bytes 8454160 | tf_op jit(solution)/shard_map/all_gather | solution.py:15
  220.1 12.5 %reshape.30 = bf16[5504,768]{1,0:T(8,128)(2,1)} reshape(bf16[32,172,768]{2,1,0:T(8,128)(2,1)} %all-gather.12.cloned.1.call-done) | data formatting | bytes 16908288
  232.6 5.2 %fusion.2 = bf16[172,768]{1,0:T(8,128)(2,1)S(1)} fusion(bf16[172,5504]{1,0:T(8,128)(2,1)S(1)} %copy-done, bf16[5504,768]{1,0:T(8,128)(2,1)} %reshape.30, f32[768]{0:T(1024)S(1)} %convert_bitcast_fusion), kind=kOutput, calls=%fused_computation.3 | convolution fusion | flops 1454376960 | bytes 10614784 | tf_op jit(solution)/shard_map/dot_general | solution.py:13
  237.7 0.3 reshape.26
  238.0 80.5 %all-gather.8.cloned.1.call-done = bf16[768,4096]{1,0:T(8,128)(2,1)} async-done(((bf16[768,128]{1,0:T(8,128)(2,1)}), bf16[768,4096]{1,0:T(8,128)(2,1)}) %all-gather.8.cloned.1.call-update) | async-done | bytes 6291472 | tf_op jit(solution)/shard_map/all_gather | solution.py:10
  318.6 8.5 %fusion.7 = bf16[6,172,4096]{2,1,0:T(8,128)(2,1)} fusion(bf16[6,128,4096]{2,1,0:T(8,128)(2,1)} %bitcast.14, bf16[172,6,128]{2,1,0:T(8,128)(2,1)S(1)} %reshape.26), kind=kOutput, calls=%fused_computation.8 | convolution fusion | flops 1082130432 | bytes 15009792 | tf_op jit(solution)/shard_map/jst,std->sjd/dot_general | solution.py:24
  327.1 51.2 %all-gather.10.cloned.1.call-done = bf16[4,172,4096]{2,0,1:T(4,128)(2,1)} async-done(((bf16[4,172,256]{2,0,1:T(4,128)(2,1)}), bf16[4,172,4096]{2,0,1:T(4,128)(2,1)}) %all-gather.10.cloned.1.call-update) | async-done | bytes 5636112 | tf_op jit(solution)/shard_map/all_gather | solution.py:33
  378.3 15.5 %fusion.3 = f32[6,4]{0,1:T(4,128)S(1)} fusion(bf16[4,172,4096]{2,0,1:T(4,128)(2,1)} %all-gather.10.cloned.1.call-done, bf16[6,172,4096]{2,1,0:T(8,128)(2,1)} %fusion.7), kind=kOutput, calls=%fused_computation.5 | convolution fusion | flops 33816576 | bytes 14090336 | tf_op jit(solution)/shard_map/sij,qij->sq/dot_general | solution.py:30
  393.8 73.8 %psum.7 = f32[6,4]{0,1:T(4,128)S(1)} all-reduce(f32[6,4]{0,1:T(4,128)S(1)} %fusion.3), channel_id=1, replica_groups=mesh['dp'=16,'tensor'=32] {'tensor'}, use_global_device_ids=true, to_apply=%region_0.0 | all-reduce | flops 24 | bytes 192 | tf_op jit(solution)/shard_map/psum | solution.py:35
  467.6 0.6 broadcast_multiply_fusion
  (7 shorter events, 0.0 us)
Async XLA Ops:
  6.5 226.0 %copy-start = (bf16[172,5504]{1,0:T(8,128)(2,1)S(1)}, bf16[172,5504]{1,0:T(8,128)(2,1)}, u32[]{:S(2)}) copy-start(bf16[172,5504]{1,0:T(8,128)(2,1)} %param.11) | copy-start | bytes 5680132
  6.5 111.9 %copy-start.2 = (f32[172,256]{1,0:T(8,128)S(1)}, f32[172,256]{1,0:T(8,128)}, u32[]{:S(2)}) copy-start(f32[172,256]{1,0:T(8,128)} %param.13) | copy-start | bytes 528388
  6.5 112.0 %copy-start.1 = (bf16[4,172,256]{2,0,1:T(4,128)(2,1)S(1)}, bf16[4,172,256]{2,0,1:T(4,128)(2,1)}, u32[]{:S(2)}) copy-start(bf16[4,172,256]{2,0,1:T(4,128)(2,1)} %param.12) | copy-start | bytes 1056772
  6.5 112.9 %copy-start.3 = (s32[6]{0:T(128)S(1)}, s32[6]{0:T(128)}, u32[]{:S(2)}) copy-start(s32[6]{0:T(128)} %param.15) | copy-start | bytes 76
  6.5 105.7 %all-gather.6.cloned.1.call-start = ((), (), s32[]{:S(2)}) async-start(), calls=%async_computation | async-start | bytes 6488064 | tf_op jit(solution)/shard_map/all_gather | solution.py:8
  7.3 212.8 %all-gather.12.cloned.1.call-start = ((), (), s32[]{:S(2)}) async-start(), calls=%async_computation.3 | async-start | bytes 8921088 | tf_op jit(solution)/shard_map/all_gather | solution.py:15
  8.0 310.6 %all-gather.8.cloned.1.call-start = ((), (), s32[]{:S(2)}) async-start(), calls=%async_computation.1 | async-start | bytes 6488064 | tf_op jit(solution)/shard_map/all_gather | solution.py:10
  117.8 260.5 %all-gather.10.cloned.1.call-start = ((), (), s32[]{:S(2)}) async-start(), calls=%async_computation.2 | async-start | bytes 5988352 | tf_op jit(solution)/shard_map/all_gather | solution.py:33
Sparse Core Ops, SparseCore 0:
  10.4 101.8 all-gather.5
  115.4 104.6 all-gather.11
  223.1 95.4 all-gather.7
  320.5 57.7 all-gather.9
where the time goes:
time: 475 us
  waiting for transfers between devices  338 us (71%)
  blocking collectives  73.8 us (16%)
  matrix products  34.7 us (7%)
  between operations  13.8 us (3%)
  local copies, waits for them, and re-layouts  12.8 us (3%)
    all_gather x1, waiting for transfers between devices, local(): full_act = lax.all_gather(activations, 'tensor', axis=1, tiled=True)  104 us
    all_gather x1, waiting for transfers between devices, local(): lax.all_gather(out_grads_t, 'tensor', axis=0, tiled=True)  101 us
    all_gather x1, waiting for transfers between devices, local(): act_proj = lax.all_gather(act_local, 'tensor', axis=1, tiled=True)  80.5 us
    psum x1, blocking collectives, local(): totals = lax.psum(partial_value, 'tensor')  73.8 us
    all_gather x1, waiting for transfers between devices, local(): lax.all_gather(scaled, 'dp', axis=2, tiled=True).astype(jnp.float32)  51.2 us
    dot_general x1, matrix products, local(): jnp.einsum('sij,qij->sq', projected, lax.all_gather(scaled, 'dp', axis=2,...  15.5 us
    unnamed x9, local copies, waits for them, and re-layouts  12.5 us
  transfers between devices with their start and end apart: 4, of which 4 were waited for; matrix products, arithmetic and copies ran while one was open for 7% of the time, Pallas kernels for 0%

commit v1 on v0

v1 whole, which is shorter than its diff:
```python
import jax
import jax.numpy as jnp
from jax import lax
from jax.experimental import pallas as pl
from jax.experimental.pallas import tpu as pltpu
from jax.sharding import PartitionSpec as P

NX, NY, NZ = 4, 8, 8
XG = [[x * NY + y for x in range(NX)] for y in range(NY)]
YG = [[x * NY + y for y in range(NY)] for x in range(NX)]
ZG = [[z * 2 + c for z in range(NZ)] for c in range(2)]
CG = [[z * 2 + c for c in range(2)] for z in range(NZ)]
SEQ = 128
PAD = 176


def score_kernel(g_ref, a_ref, s_ref, o_ref, p_ref):
    seqs = g_ref.shape[2] // SEQ
    queries = s_ref.shape[1] // 2

    def block(step, _):
        fx = step // 4
        pair = lax.rem(step, 4)
        high = pair // 2
        core = lax.rem(pair, 2)
        for s in range(seqs):
            tokens = pl.ds(s * SEQ, SEQ)
            rhs = jnp.concatenate([a_ref[2 * pair, tokens, :], a_ref[2 * pair + 1, tokens, :]], axis=1)
            p_ref[s] = jnp.dot(g_ref[fx, :, tokens], rhs, preferred_element_type=jnp.float32)
        for half in range(2):
            lanes = pl.ds(half * 128, 128)
            slots = [lax.rem(2 * q + half - 2 * fx - high + 8, 8) for q in range(queries)]

            def rows(r, acc):
                sl = pl.ds(pl.multiple_of(r * 16, 16), 16)
                w = [s_ref[core, 2 * q + half, slots[q], sl, :].astype(jnp.float32) for q in range(queries)]
                out = []
                for s in range(seqs):
                    p = p_ref[s, sl, lanes]
                    for q in range(queries):
                        t = p * w[q]
                        out.append(acc[s * queries + q] + t[:8] + t[8:])
                return tuple(out)

            zero = tuple(jnp.zeros((8, 128), jnp.float32) for _ in range(seqs * queries))
            acc = lax.fori_loop(0, PAD // 16, rows, zero)
            for n in range(seqs * queries):
                o_ref[n] += acc[n]
        return 0

    o_ref[...] = jnp.zeros_like(o_ref)
    lax.fori_loop(0, 16, block, 0)


def score_tiles(g4, a8, s2):
    seqs = g4.shape[2] // SEQ
    queries = s2.shape[1] // 2
    return pl.pallas_call(
        score_kernel,
        out_shape=jax.ShapeDtypeStruct((seqs * queries, 8, 128), jnp.float32),
        in_specs=[pl.BlockSpec(memory_space=pltpu.VMEM)] * 3,
        out_specs=pl.BlockSpec(memory_space=pltpu.VMEM),
        scratch_shapes=[pltpu.VMEM((seqs, PAD, 256), jnp.float32)],
        compiler_params=pltpu.CompilerParams(vmem_limit_bytes=40 * 1024 * 1024),
        cost_estimate=pl.CostEstimate(flops=2 * 768 * 704 * 1024, bytes_accessed=9_000_000, transcendentals=0),
    )(g4, a8, s2)


def add_parts(parts):
    wide = [parts[n].astype(jnp.float32) for n in range(NX)]
    return (wide[0] + wide[1]) + (wide[2] + wide[3])


def local(activations, out_grads_t, in_basis, out_basis_t, query_proj, eigvals, damping, lengths):
    bf, f32 = jnp.bfloat16, jnp.float32
    tokens, width = activations.shape[0], out_grads_t.shape[0]
    seqs, queries = lengths.shape[0], query_proj.shape[0]
    seq_len = tokens // seqs
    kx = lax.shift_right_logical(lax.axis_index("tensor"), 3)
    kz = lax.shift_right_logical(lax.axis_index("dp"), 1)
    base = 2 * kx + (kz & 1)

    y8 = lax.all_gather(out_grads_t, "tensor", axis_index_groups=YG)
    x8 = lax.all_gather(activations, "tensor", axis_index_groups=YG)

    scaled = (query_proj.astype(f32) / (eigvals + damping[0])).astype(bf)
    scaled = jnp.pad(scaled, ((0, 0), (0, PAD - width), (0, 0)))
    pieces = scaled.reshape(queries, PAD, 2, 128).transpose(0, 2, 1, 3).reshape(8, PAD, 128)
    got = []
    for r in range(8):
        perm = []
        for z in range(NZ):
            for c in range(2):
                for x in range(NX):
                    for y in range(NY):
                        zz = (2 * x + z % 2 + r) % 8
                        perm.append(((z * 2 + c) * 32 + x * NY + y, (zz * 2 + c) * 32 + (z // 2) * NY + y))
        piece = lax.dynamic_index_in_dim(pieces, (base + r) & 7, 0, keepdims=False)
        got.append(lax.ppermute(piece, ("dp", "tensor"), perm))
    s8 = lax.all_gather(jnp.stack(got), "dp", axis_index_groups=ZG)
    s2 = lax.all_gather(s8, "dp", axis_index_groups=CG)

    v4 = out_basis_t.reshape(width, NX, NY * width).transpose(1, 0, 2)
    v4 = lax.all_to_all(v4, "tensor", 0, 0, axis_index_groups=XG)
    u4 = lax.all_to_all(in_basis.reshape(NX, NY * 128, 128), "tensor", 0, 0, axis_index_groups=XG)

    g_part = jnp.einsum("xjk,kt->xjt", v4, y8.reshape(NY * width, tokens), preferred_element_type=f32).astype(bf)
    g_parts = lax.all_to_all(g_part, "tensor", 0, 0, axis_index_groups=XG)
    position = lax.broadcasted_iota(jnp.int32, (seqs, seq_len), 1)
    keep = (position < lengths[:, None]).astype(f32).reshape(1, tokens)
    g = (add_parts(g_parts) * keep).astype(bf)
    g4 = lax.all_gather(jnp.pad(g, ((0, PAD - width), (0, 0))), "tensor", axis_index_groups=XG)

    a_part = jnp.einsum("yte,xyed->xtd", x8, u4.reshape(NX, NY, 128, 128), preferred_element_type=f32).astype(bf)
    a_parts = lax.all_to_all(a_part, "tensor", 0, 0, axis_index_groups=XG)
    a = add_parts(a_parts).astype(bf)
    a8 = lax.all_gather(a, "tensor", axis_index_groups=YG)

    part = score_tiles(g4, a8, s2).sum((1, 2))
    tile = jnp.broadcast_to(jnp.pad(part, (0, 128 - part.shape[0])), (NX * NY, 8, 128))
    totals = lax.all_to_all(tile, "tensor", 0, 0)[:, 0, : part.shape[0]].sum(0)
    norm_factor = (in_basis.shape[0] * out_basis_t.shape[1] * seq_len) ** (-0.5)
    return totals.reshape(seqs, queries) * norm_factor


def solution(mesh):
    placed = (
        P("dp", "tensor"),
        P("tensor", "dp"),
        P(None, "tensor"),
        P("tensor", None),
        P(None, "tensor", "dp"),
        P("tensor", "dp"),
        P(),
        P("dp"),
    )
    return jax.shard_map(
        local, mesh=mesh, in_specs=placed, out_specs=P("dp", None), check_vma=False
    )
```

time: 475 us -> 297 us (0.63)
  the two profiles are of different devices: /device:TPU:64 before, /device:TPU:1 now
where the time goes in v1:
time: 297 us; the launch traced here: 296 us
  waiting for transfers between devices  152 us (51%)
  starting transfers between devices  52.8 us (18%)
  blocking collectives  35.2 us (12%)
  local copies, waits for them, and re-layouts  17 us (6%)
  Pallas kernels  14.5 us (5%)
  between operations  14.4 us (5%)
  matrix products  7.78 us (3%)
    ppermute x8, starting transfers between devices, local(): got.append(lax.ppermute(piece, ('dp', 'tensor'), perm))  41 us
    all_gather x1, waiting for transfers between devices, local(): a8 = lax.all_gather(a, 'tensor', axis_index_groups=YG)  40.7 us
    all_gather x1, waiting for transfers between devices, local(): lax.all_gather(jnp.pad(g, ((0, PAD - width), (0, 0))), 'tensor', axis_ind...  33.5 us
    all_gather x1, waiting for transfers between devices, local(): s2 = lax.all_gather(s8, 'dp', axis_index_groups=CG)  28.9 us
    all_to_all x1, blocking collectives, local(): lax.all_to_all(in_basis.reshape(NX, NY * 128, 128), 'tensor', 0, 0, axis_...  18 us
    all_to_all x1, blocking collectives, local(): totals = lax.all_to_all(tile, 'tensor', 0, 0)[:, 0, :part.shape[0]].sum(0)  17.2 us
    all_gather x1, waiting for transfers between devices, local(): s8 = lax.all_gather(jnp.stack(got), 'dp', axis_index_groups=ZG)  16 us
    pallas_call x1, Pallas kernels, score_tiles(): pl.pallas_call(score_kernel, out_shape=jax.ShapeDtypeStruct((seqs * queri...  14.5 us
  transfers between devices with their start and end apart: 17, of which 10 were waited for; matrix products, arithmetic and copies ran while one was open for 7% of the time, Pallas kernels for 0%

profile of v1, /device:TPU:1, one launch (start us, length us, event | category | flops | bytes accessed | tf_op | source)
XLA Modules:
  0.0 296.0 jit_solution(13875203875147525684)
XLA Ops:
  11.7 4.8 %collective-permute-start.1 = (bf16[176,128]{1,0:T(8,128)(2,1)S(1)}, bf16[176,128]{1,0:T(8,128)(2,1)S(1)}, u32[]{:S(2)}, u32[]{:S(2)}) collective-permute-start(bf16[176,128]{1,0:T(8,128)(2,1)S(1)} %get-tuple-element.11), channel_id=1, source_target_pairs={{0,64},{1,65},{2,66},{3,67},{4,68},{5,69},{6,70},{7,71},{8,192},{9... | collective-permute-start | bytes 135176 | tf_op jit(solution)/shard_map/ppermute | solution.py:99
  16.5 9.1 %collective-permute-start.2 = (bf16[176,128]{1,0:T(8,128)(2,1)S(1)}, bf16[176,128]{1,0:T(8,128)(2,1)S(1)}, u32[]{:S(2)}, u32[]{:S(2)}) collective-permute-start(bf16[176,128]{1,0:T(8,128)(2,1)S(1)} %get-tuple-element.10), channel_id=1, source_target_pairs={{0,128},{1,129},{2,130},{3,131},{4,132},{5,133},{6,134},{7,135},{8... | collective-permute-start | bytes 135176 | tf_op jit(solution)/shard_map/ppermute | solution.py:99
  25.6 4.1 %collective-permute-start.3 = (bf16[176,128]{1,0:T(8,128)(2,1)S(1)}, bf16[176,128]{1,0:T(8,128)(2,1)S(1)}, u32[]{:S(2)}, u32[]{:S(2)}) collective-permute-start(bf16[176,128]{1,0:T(8,128)(2,1)S(1)} %get-tuple-element.9), channel_id=1, source_target_pairs={{0,192},{1,193},{2,194},{3,195},{4,196},{5,197},{6,198},{7,199},{8... | collective-permute-start | bytes 135176 | tf_op jit(solution)/shard_map/ppermute | solution.py:99
  29.7 12.4 %collective-permute-start.4 = (bf16[176,128]{1,0:T(8,128)(2,1)S(1)}, bf16[176,128]{1,0:T(8,128)(2,1)S(1)}, u32[]{:S(2)}, u32[]{:S(2)}) collective-permute-start(bf16[176,128]{1,0:T(8,128)(2,1)S(1)} %get-tuple-element.8), channel_id=1, source_target_pairs={{0,256},{1,257},{2,258},{3,259},{4,260},{5,261},{6,262},{7,263},{8... | collective-permute-start | bytes 135176 | tf_op jit(solution)/shard_map/ppermute | solution.py:99
  42.1 3.7 %collective-permute-start.5 = (bf16[176,128]{1,0:T(8,128)(2,1)S(1)}, bf16[176,128]{1,0:T(8,128)(2,1)S(1)}, u32[]{:S(2)}, u32[]{:S(2)}) collective-permute-start(bf16[176,128]{1,0:T(8,128)(2,1)S(1)} %get-tuple-element.7), channel_id=1, source_target_pairs={{0,320},{1,321},{2,322},{3,323},{4,324},{5,325},{6,326},{7,327},{8... | collective-permute-start | bytes 135176 | tf_op jit(solution)/shard_map/ppermute | solution.py:99
  45.8 4.3 %collective-permute-start.6 = (bf16[176,128]{1,0:T(8,128)(2,1)S(1)}, bf16[176,128]{1,0:T(8,128)(2,1)S(1)}, u32[]{:S(2)}, u32[]{:S(2)}) collective-permute-start(bf16[176,128]{1,0:T(8,128)(2,1)S(1)} %get-tuple-element.6), channel_id=1, source_target_pairs={{0,384},{1,385},{2,386},{3,387},{4,388},{5,389},{6,390},{7,391},{8... | collective-permute-start | bytes 135176 | tf_op jit(solution)/shard_map/ppermute | solution.py:99
  52.9 2.6 collective-permute-done.7
  56.3 18.0 %all_to_all.25 = bf16[4,1024,128]{2,1,0:T(8,128)(2,1)S(1)} all-to-all(bf16[4,1024,128]{2,1,0:T(8,128)(2,1)S(1)} %bitcast.68), channel_id=1, replica_groups={{0,8,16,24},{1,9,17,25},{2,10,18,26},{3,11,19,27},{4,12,20,28},{5,13,21..., dimensions={0} | all-to-all | bytes 2097152 | tf_op jit(solution)/shard_map/all_to_all | solution.py:105
  74.3 3.4 %fusion = bf16[4,768,128]{1,2,0:T(8,128)(2,1)} fusion(bf16[4,8,128,128]{3,2,1,0:T(8,128)(2,1)S(1)} %bitcast.69, bf16[8,768,128,1]{2,1,0,3:T(8,128)(2,1)} %bitcast.71), kind=kOutput, calls=%fused_computation.3 | convolution fusion | flops 805699584 | bytes 3407872 | tf_op jit(solution)/shard_map/yte,xyed->xtd/dot_general | solution.py:114
  77.6 3.5 %all-to-all-start.3 = ((bf16[4,768,128]{1,2,0:T(8,128)(2,1)}), bf16[4,768,128]{1,2,0:T(8,128)(2,1)S(1)}, u32[]{:S(2)}, u32[]{:S(2)}) async-start(bf16[4,768,128]{1,2,0:T(8,128)(2,1)} %fusion), calls=%async_computation.3 | async-start | bytes 1572864 | tf_op jit(solution)/shard_map/all_to_all | solution.py:115
  81.1 4.4 %reshape.46 = bf16[172,4,1376]{2,1,0:T(4,128)(2,1)S(1)} reshape(bf16[172,5504]{1,0:T(8,128)(2,1)} %param.11) | data formatting | bytes 3786752 | tf_op jit(solution)/shard_map/reshape | solution.py:103
  89.5 4.4 %all-to-all-start = ((bf16[4,172,1376]{2,1,0:T(8,128)(2,1)}), bf16[4,172,1376]{2,1,0:T(8,128)(2,1)}, u32[]{:S(2)}, u32[]{:S(2)}) async-start(bf16[4,172,1376]{2,1,0:T(8,128)(2,1)} %bitcast.62), calls=%async_computation | async-start | bytes 3964928 | tf_op jit(solution)/shard_map/all_to_all | solution.py:104
  94.9 3.6 %all-gather.23.cloned.1.call-done = bf16[8,172,768]{2,1,0:T(8,128)(2,1)} async-done(((bf16[1,172,768]{2,1,0:T(8,128)(2,1)}), bf16[8,172,768]{2,1,0:T(8,128)(2,1)}) %all-gather.23.cloned.1.call-update) | async-done | bytes 2113552 | tf_op jit(solution)/shard_map/all_gather | solution.py:83
  101.1 12.0 %all-to-all-done = bf16[4,172,1376]{2,1,0:T(8,128)(2,1)} async-done(((bf16[4,172,1376]{2,1,0:T(8,128)(2,1)}), bf16[4,172,1376]{2,1,0:T(8,128)(2,1)}, u32[]{:S(2)}, u32[]{:S(2)}) %all-to-all-start) | async-done | bytes 1893408 | tf_op jit(solution)/shard_map/all_to_all | solution.py:104
  113.0 4.4 %convolution_convert_fusion = bf16[4,172,768]{2,1,0:T(8,128)(2,1)} fusion(bf16[4,172,1376]{2,1,0:T(8,128)(2,1)} %all-to-all-done, bf16[1376,768,1]{1,0,2:T(8,128)(2,1)S(1)} %reshape.60), kind=kOutput, calls=%fused_computation.2 | convolution fusion | flops 1454641152 | bytes 5063680 | tf_op jit(solution)/shard_map/xjk,kt->xjt/dot_general | solution.py:107
  117.5 3.6 %all-to-all-start.1 = ((bf16[4,172,768]{2,1,0:T(8,128)(2,1)}), bf16[4,172,768]{2,1,0:T(8,128)(2,1)S(1)}, u32[]{:S(2)}, u32[]{:S(2)}) async-start(bf16[4,172,768]{2,1,0:T(8,128)(2,1)} %convolution_convert_fusion), calls=%async_computation.1 | async-start | bytes 2162688 | tf_op jit(solution)/shard_map/all_to_all | solution.py:108
  121.2 9.8 %all-to-all-done.1 = bf16[4,172,768]{2,1,0:T(8,128)(2,1)S(1)} async-done(((bf16[4,172,768]{2,1,0:T(8,128)(2,1)}), bf16[4,172,768]{2,1,0:T(8,128)(2,1)S(1)}, u32[]{:S(2)}, u32[]{:S(2)}) %all-to-all-start.1) | async-done | bytes 1056800 | tf_op jit(solution)/shard_map/all_to_all | solution.py:108
  132.0 16.0 %all-gather.19.cloned.1.call-done = bf16[64,176,128]{2,1,0:T(8,128)(2,1)} async-done(((bf16[8,176,128]{2,1,0:T(8,128)(2,1)}), bf16[64,176,128]{2,1,0:T(8,128)(2,1)}) %all-gather.19.cloned.1.call-update) | async-done | bytes 2883600 | tf_op jit(solution)/shard_map/all_gather | solution.py:100
  148.0 40.7 %all-gather.13.cloned.1.call-done.a_ref = bf16[8,768,128]{2,1,0:T(8,128)(2,1)} async-done(((bf16[1,768,128]{2,1,0:T(8,128)(2,1)}), bf16[8,768,128]{2,1,0:T(8,128)(2,1)}) %all-gather.13.cloned.1.call-update) | async-done | bytes 1572880 | tf_op jit(solution)/shard_map/all_gather | solution.py:117
  188.8 33.5 %all-gather.15.cloned.1.call-done = bf16[704,768]{1,0:T(8,128)(2,1)} async-done(((bf16[176,768]{1,0:T(8,128)(2,1)}), bf16[704,768]{1,0:T(8,128)(2,1)}) %all-gather.15.cloned.1.call-update) | async-done | bytes 1081360 | tf_op jit(solution)/shard_map/all_gather | solution.py:112
  222.2 28.9 %all-gather.21.cloned.1.call-done = bf16[16,8,176,128]{3,2,1,0:T(8,128)(2,1)} async-done(((bf16[8,8,176,128]{3,2,1,0:T(8,128)(2,1)}), bf16[16,8,176,128]{3,2,1,0:T(8,128)(2,1)}) %all-gather.21.cloned.1.call-update) | async-done | bytes 5767184 | tf_op jit(solution)/shard_map/all_gather | solution.py:101
  251.1 2.6 copy-done
  256.4 14.5 %shard_map.82 = f32[24,8,128]{2,1,0:T(8,128)S(1)} custom-call(bf16[4,176,768]{2,1,0:T(8,128)(2,1)S(1)} %bitcast.65, bf16[8,768,128]{2,1,0:T(8,128)(2,1)S(1)} %copy-done.1, bf16[2,8,8,176,128]{4,3,2,1,0:T(8,128)(2,1)S(1)} %bitcast.64), custom_call_target="tpu_custom_call" | custom-call | flops 1107296256 | bytes 9000000 | tf_op jit(solution)/shard_map/pallas_call | solution.py:58
  271.1 17.2 %all_to_all.26 = f32[32,8,128]{2,1,0:T(8,128)S(1)} all-to-all(f32[32,8,128]{2,1,0:T(8,128)S(1)} %broadcast_in_dim.2), channel_id=1, replica_groups=mesh['dp'=16,'tensor'=32] {'tensor'}, dimensions={0} | all-to-all | bytes 262144 | tf_op jit(solution)/shard_map/all_to_all | solution.py:121
  (61 shorter events, 20.1 us)
Async XLA Ops:
  6.5 67.7 %all-gather.17.cloned.1.call-start = ((), (), s32[]{:S(2)}) async-start(), calls=%async_computation.7 | async-start | bytes 1769472 | tf_op jit(solution)/shard_map/all_gather | solution.py:84
  7.3 91.3 %all-gather.23.cloned.1.call-start = ((), (), s32[]{:S(2)}) async-start(), calls=%async_computation.10 | async-start | bytes 2433024 | tf_op jit(solution)/shard_map/all_gather | solution.py:83
  8.0 140.0 %all-gather.19.cloned.1.call-start = ((), (), s32[]{:S(2)}) async-start(), calls=%async_computation.8 | async-start | bytes 3244032 | tf_op jit(solution)/shard_map/all_gather | solution.py:100
  9.7 46.6 %copy-start.3 = (bf16[4096,128]{1,0:T(8,128)(2,1)S(1)}, bf16[4096,128]{1,0:T(8,128)(2,1)}, u32[]{:S(2)}) copy-start(bf16[4096,128]{1,0:T(8,128)(2,1)} %param.10) | copy-start | bytes 3145732
  11.0 31.2 %collective-permute-start = (bf16[176,128]{1,0:T(8,128)(2,1)S(1)}, bf16[176,128]{1,0:T(8,128)(2,1)S(1)}, u32[]{:S(2)}, u32[]{:S(2)}) collective-permute-start(bf16[176,128]{1,0:T(8,128)(2,1)S(1)} %get-tuple-element.12), channel_id=1, source_target_pairs={{0,0},{1,1},{2,2},{3,3},{4,4},{5,5},{6,6},{7,7},{8,128},{9,129},{1... | collective-permute-start | bytes 135176 | tf_op jit(solution)/shard_map/ppermute | solution.py:99
  11.7 34.2 %collective-permute-start.1 = (bf16[176,128]{1,0:T(8,128)(2,1)S(1)}, bf16[176,128]{1,0:T(8,128)(2,1)S(1)}, u32[]{:S(2)}, u32[]{:S(2)}) collective-permute-start(bf16[176,128]{1,0:T(8,128)(2,1)S(1)} %get-tuple-element.11), channel_id=1, source_target_pairs={{0,64},{1,65},{2,66},{3,67},{4,68},{5,69},{6,70},{7,71},{8,192},{9... | collective-permute-start | bytes 135176 | tf_op jit(solution)/shard_map/ppermute | solution.py:99
  16.5 33.6 %collective-permute-start.2 = (bf16[176,128]{1,0:T(8,128)(2,1)S(1)}, bf16[176,128]{1,0:T(8,128)(2,1)S(1)}, u32[]{:S(2)}, u32[]{:S(2)}) collective-permute-start(bf16[176,128]{1,0:T(8,128)(2,1)S(1)} %get-tuple-element.10), channel_id=1, source_target_pairs={{0,128},{1,129},{2,130},{3,131},{4,132},{5,133},{6,134},{7,135},{8... | collective-permute-start | bytes 135176 | tf_op jit(solution)/shard_map/ppermute | solution.py:99
  25.6 26.5 %collective-permute-start.3 = (bf16[176,128]{1,0:T(8,128)(2,1)S(1)}, bf16[176,128]{1,0:T(8,128)(2,1)S(1)}, u32[]{:S(2)}, u32[]{:S(2)}) collective-permute-start(bf16[176,128]{1,0:T(8,128)(2,1)S(1)} %get-tuple-element.9), channel_id=1, source_target_pairs={{0,192},{1,193},{2,194},{3,195},{4,196},{5,197},{6,198},{7,199},{8... | collective-permute-start | bytes 135176 | tf_op jit(solution)/shard_map/ppermute | solution.py:99
  29.7 22.5 %collective-permute-start.4 = (bf16[176,128]{1,0:T(8,128)(2,1)S(1)}, bf16[176,128]{1,0:T(8,128)(2,1)S(1)}, u32[]{:S(2)}, u32[]{:S(2)}) collective-permute-start(bf16[176,128]{1,0:T(8,128)(2,1)S(1)} %get-tuple-element.8), channel_id=1, source_target_pairs={{0,256},{1,257},{2,258},{3,259},{4,260},{5,261},{6,262},{7,263},{8... | collective-permute-start | bytes 135176 | tf_op jit(solution)/shard_map/ppermute | solution.py:99
  42.1 10.1 %collective-permute-start.5 = (bf16[176,128]{1,0:T(8,128)(2,1)S(1)}, bf16[176,128]{1,0:T(8,128)(2,1)S(1)}, u32[]{:S(2)}, u32[]{:S(2)}) collective-permute-start(bf16[176,128]{1,0:T(8,128)(2,1)S(1)} %get-tuple-element.7), channel_id=1, source_target_pairs={{0,320},{1,321},{2,322},{3,323},{4,324},{5,325},{6,326},{7,327},{8... | collective-permute-start | bytes 135176 | tf_op jit(solution)/shard_map/ppermute | solution.py:99
  45.8 7.0 %collective-permute-start.6 = (bf16[176,128]{1,0:T(8,128)(2,1)S(1)}, bf16[176,128]{1,0:T(8,128)(2,1)S(1)}, u32[]{:S(2)}, u32[]{:S(2)}) collective-permute-start(bf16[176,128]{1,0:T(8,128)(2,1)S(1)} %get-tuple-element.6), channel_id=1, source_target_pairs={{0,384},{1,385},{2,386},{3,387},{4,388},{5,389},{6,390},{7,391},{8... | collective-permute-start | bytes 135176 | tf_op jit(solution)/shard_map/ppermute | solution.py:99
  50.1 5.4 %collective-permute-start.7 = (bf16[176,128]{1,0:T(8,128)(2,1)S(1)}, bf16[176,128]{1,0:T(8,128)(2,1)S(1)}, u32[]{:S(2)}, u32[]{:S(2)}) collective-permute-start(bf16[176,128]{1,0:T(8,128)(2,1)S(1)} %get-tuple-element.5), channel_id=1, source_target_pairs={{0,448},{1,449},{2,450},{3,451},{4,452},{5,453},{6,454},{7,455},{8... | collective-permute-start | bytes 135176 | tf_op jit(solution)/shard_map/ppermute | solution.py:99
  55.5 0.7 copy-start.4
  77.6 11.9 %all-to-all-start.3 = ((bf16[4,768,128]{1,2,0:T(8,128)(2,1)}), bf16[4,768,128]{1,2,0:T(8,128)(2,1)S(1)}, u32[]{:S(2)}, u32[]{:S(2)}) async-start(bf16[4,768,128]{1,2,0:T(8,128)(2,1)} %fusion), calls=%async_computation.3 | async-start | bytes 1572864 | tf_op jit(solution)/shard_map/all_to_all | solution.py:115
  89.5 23.5 %all-to-all-start = ((bf16[4,172,1376]{2,1,0:T(8,128)(2,1)}), bf16[4,172,1376]{2,1,0:T(8,128)(2,1)}, u32[]{:S(2)}, u32[]{:S(2)}) async-start(bf16[4,172,1376]{2,1,0:T(8,128)(2,1)} %bitcast.62), calls=%async_computation | async-start | bytes 3964928 | tf_op jit(solution)/shard_map/all_to_all | solution.py:104
  93.9 94.8 %all-gather.13.cloned.1.call-start = ((), (), s32[]{:S(2)}) async-start(), calls=%async_computation.5 | async-start | bytes 1769472 | tf_op jit(solution)/shard_map/all_gather | solution.py:117
  117.4 3.7 %copy-start.5 = (s32[6]{0:T(128)S(1)}, s32[6]{0:T(128)}, u32[]{:S(2)}) copy-start(s32[6]{0:T(128)} %param.15) | copy-start | bytes 76
  117.5 13.6 %all-to-all-start.1 = ((bf16[4,172,768]{2,1,0:T(8,128)(2,1)}), bf16[4,172,768]{2,1,0:T(8,128)(2,1)S(1)}, u32[]{:S(2)}, u32[]{:S(2)}) async-start(bf16[4,172,768]{2,1,0:T(8,128)(2,1)} %convolution_convert_fusion), calls=%async_computation.1 | async-start | bytes 2162688 | tf_op jit(solution)/shard_map/all_to_all | solution.py:108
  121.1 101.1 %all-gather.15.cloned.1.call-start = ((), (), s32[]{:S(2)}) async-start(), calls=%async_computation.6 | async-start | bytes 1351680 | tf_op jit(solution)/shard_map/all_gather | solution.py:112
  132.0 119.1 %all-gather.21.cloned.1.call-start = ((), (), s32[]{:S(2)}) async-start(), calls=%async_computation.9 | async-start | bytes 8650752 | tf_op jit(solution)/shard_map/all_gather | solution.py:101
  251.1 2.6 copy-start
  253.7 1.4 copy-start.1
  255.1 1.2 copy-start.2
Sparse Core Ops, SparseCore 0:
  9.4 43.9 all-gather.16
  55.5 43.0 all-gather.22
  100.6 47.3 all-gather.18
  150.0 38.7 all-gather.12
  190.7 31.4 all-gather.14
  224.1 26.9 all-gather.20

commit v2 on v1

v2 whole, which is shorter than its diff:
```python
import jax
import jax.numpy as jnp
from jax import lax
from jax.experimental import pallas as pl
from jax.experimental.pallas import tpu as pltpu
from jax.sharding import PartitionSpec as P

NX, NY, NZ = 4, 8, 8
XG = [[x * NY + y for x in range(NX)] for y in range(NY)]
YG = [[x * NY + y for y in range(NY)] for x in range(NX)]
ZG = [[z * 2 + c for z in range(NZ)] for c in range(2)]
SEQ = 128
PAD = 176


def shift_x(array, by):
    perm = [(x * NY + y, (x + by) % NX * NY + y) for x in range(NX) for y in range(NY)]
    return lax.ppermute(array, "tensor", perm)


def score_kernel(where_ref, g0_ref, g1_ref, g2_ref, g3_ref, a_ref, own_ref, other_ref, o_ref, at_ref, sum_ref):
    core, kx = where_ref[0], where_ref[1]
    tokens = g0_ref.shape[1]
    queries = own_ref.shape[0] // 2
    row = 0
    for high in range(2):
        for c in (core, 1 - core):
            for half in range(2):
                at_ref[pl.ds(row, 128), :] = a_ref[4 * high + 2 * c + half]
                row += 128
    sum_ref[...] = jnp.zeros_like(sum_ref)
    for d, g_ref in enumerate((g0_ref, g1_ref, g2_ref, g3_ref)):
        fx = (kx - d) & (NX - 1)

        def one(q, _):
            tiles = []
            for high in range(2):
                for s_ref in (own_ref, other_ref):
                    for half in range(2):
                        p = 2 * q + half
                        tiles.append(s_ref[p, (p - 2 * fx - high) & 7])
            lhs = jnp.concatenate(tiles, axis=1)
            t = jnp.dot(lhs, at_ref[...], preferred_element_type=jnp.float32)
            t = t * g_ref[...].astype(jnp.float32)
            sum_ref[q] += t.reshape(PAD // 8, 8, tokens).sum(0)
            return 0

        lax.fori_loop(0, queries, one, 0)
    lane = lax.broadcasted_iota(jnp.int32, (1, 128), 1)
    out = jnp.zeros((1, 128), jnp.float32)
    for q in range(queries):
        per_token = jnp.sum(sum_ref[q], axis=0, keepdims=True)
        for s in range(tokens // SEQ):
            value = jnp.sum(per_token[:, s * SEQ : (s + 1) * SEQ], axis=1, keepdims=True)
            out = jnp.where(lane == s * queries + q, value, out)
    o_ref[...] = jnp.broadcast_to(out, o_ref.shape)


def score_tiles(where, gs, at, own, other):
    tokens = at.shape[2]
    queries = own.shape[0] // 2
    return pl.pallas_call(
        score_kernel,
        out_shape=jax.ShapeDtypeStruct((NX * NY, 128), jnp.float32),
        in_specs=[pl.BlockSpec(memory_space=pltpu.SMEM)] + [pl.BlockSpec(memory_space=pltpu.VMEM)] * 7,
        out_specs=pl.BlockSpec(memory_space=pltpu.VMEM),
        scratch_shapes=[
            pltpu.VMEM((NY * 128, tokens), jnp.bfloat16),
            pltpu.VMEM((queries, 8, tokens), jnp.float32),
        ],
        compiler_params=pltpu.CompilerParams(vmem_limit_bytes=40 * 1024 * 1024),
        cost_estimate=pl.CostEstimate(
            flops=2 * NX * queries * PAD * NY * 128 * tokens, bytes_accessed=9_000_000, transcendentals=0
        ),
    )(where, *gs, at, own, other)


def add_parts(parts):
    wide = [parts[n].astype(jnp.float32) for n in range(NX)]
    return (wide[0] + wide[1]) + (wide[2] + wide[3])


def local(activations, out_grads_t, in_basis, out_basis_t, query_proj, eigvals, damping, lengths):
    bf, f32 = jnp.bfloat16, jnp.float32
    tokens, width = activations.shape[0], out_grads_t.shape[0]
    seqs, queries = lengths.shape[0], query_proj.shape[0]
    seq_len = tokens // seqs
    kx = lax.shift_right_logical(lax.axis_index("tensor"), 3)
    dp = lax.axis_index("dp")
    base = 2 * kx + (lax.shift_right_logical(dp, 1) & 1)

    grads = jnp.pad(out_grads_t.reshape(width, seqs, seq_len).transpose(1, 0, 2), ((0, 0), (0, PAD - width), (0, 0)))
    both = jnp.concatenate([activations, grads.reshape(seqs * PAD, seq_len)], axis=0)
    both = lax.all_gather(both, "tensor", axis_index_groups=YG)
    x8 = both[:, :tokens]
    y8 = both[:, tokens:].reshape(NY, seqs, PAD, seq_len)[:, :, :width]

    scaled = (query_proj.astype(f32) / (eigvals + damping[0])).astype(bf)
    scaled = jnp.pad(scaled, ((0, 0), (0, PAD - width), (0, 0)))
    pieces = scaled.reshape(queries, PAD, 2, 128).transpose(0, 2, 1, 3).reshape(8, PAD, 128)
    got = []
    for r in range(8):
        perm = []
        for z in range(NZ):
            for c in range(2):
                for x in range(NX):
                    for y in range(NY):
                        zz = (2 * x + z % 2 + r) % 8
                        perm.append(((z * 2 + c) * 32 + x * NY + y, (zz * 2 + c) * 32 + (z // 2) * NY + y))
        piece = lax.dynamic_index_in_dim(pieces, (base + r) & 7, 0, keepdims=False)
        got.append(lax.ppermute(piece, ("dp", "tensor"), perm))
    own = lax.all_gather(jnp.stack(got), "dp", axis_index_groups=ZG)
    other = lax.ppermute(own, "dp", [(n, n ^ 1) for n in range(16)])

    v4 = out_basis_t.reshape(width, NX, NY * width).transpose(1, 0, 2)
    v4 = lax.all_to_all(v4, "tensor", 0, 0, axis_index_groups=XG)
    u4 = lax.all_to_all(in_basis.reshape(NX, NY * 128, 128), "tensor", 0, 0, axis_index_groups=XG)

    a_part = jnp.einsum("xyed,yte->xdt", u4.reshape(NX, NY, 128, 128), x8, preferred_element_type=f32).astype(bf)
    a_parts = lax.all_to_all(a_part, "tensor", 0, 0, axis_index_groups=XG)
    at = lax.all_gather(add_parts(a_parts).astype(bf), "tensor", axis_index_groups=YG)

    y8 = y8.transpose(0, 2, 1, 3).reshape(NY * width, tokens)
    g_part = jnp.einsum("xjk,kt->xjt", v4, y8, preferred_element_type=f32).astype(bf)
    g_parts = lax.all_to_all(g_part, "tensor", 0, 0, axis_index_groups=XG)
    position = lax.broadcasted_iota(jnp.int32, (seqs, seq_len), 1)
    keep = (position < lengths[:, None]).astype(f32).reshape(1, tokens)
    g = (add_parts(g_parts) * keep).astype(bf)
    g = jnp.pad(g, ((0, PAD - width), (0, 0)))
    gs = [g] + [shift_x(g, d) for d in range(1, NX)]

    where = jnp.stack([dp & 1, kx]).astype(jnp.int32)
    tile = score_tiles(where, gs, at, own, other)
    totals = lax.all_to_all(tile, "tensor", 0, 0, tiled=True).sum(0)[: seqs * queries]
    norm_factor = (in_basis.shape[0] * out_basis_t.shape[1] * seq_len) ** (-0.5)
    return totals.reshape(seqs, queries) * norm_factor


def solution(mesh):
    placed = (
        P("dp", "tensor"),
        P("tensor", "dp"),
        P(None, "tensor"),
        P("tensor", None),
        P(None, "tensor", "dp"),
        P("tensor", "dp"),
        P(),
        P("dp"),
    )
    return jax.shard_map(
        local, mesh=mesh, in_specs=placed, out_specs=P("dp", None), check_vma=False
    )
```

time: 297 us -> 209 us (0.70)
  waiting for transfers between devices: 152 us -> 52.1 us
  starting transfers between devices: 52.8 us -> 66.7 us
  Pallas kernels: 14.5 us -> 9.78 us
    all_gather x6 -> x3, waiting for transfers between devices: 123 us -> 20.6 us  [the longest x1 20.5 us: local(): own = lax.all_gather(jnp.stack(got), 'dp', axis_index_groups=ZG)]
    ppermute x0 -> x4, starting transfers between devices: none -> 13.1 us  [the longest x3 8.42 us: shift_x(): return lax.ppermute(array, 'tensor', perm)]
    all_to_all x1, waiting for transfers between devices: 12 us -> 0.01 us  [local(): v4 = lax.all_to_all(v4, 'tensor', 0, 0, axis_index_groups=XG)]
    ppermute x0 -> x4, waiting for transfers between devices: none -> 10.2 us  [the longest x3 10.2 us: shift_x(): return lax.ppermute(array, 'tensor', perm)]
    all_to_all x1, waiting for transfers between devices: 9.8 us -> 15.5 us  [local(): g_parts = lax.all_to_all(g_part, 'tensor', 0, 0, axis_index_groups=XG)]
    unnamed x20 -> x23, local copies, waits for them, and re-layouts: 8.62 us -> 3 us
    reshape x0 -> x2, local copies, waits for them, and re-layouts: none -> 4.78 us  [the longest x1 3.45 us: local(): y8 = y8.transpose(0, 2, 1, 3).reshape(NY * width, tokens)]
    pallas_call x1, Pallas kernels: 14.5 us -> 9.78 us  [score_tiles(): pl.pallas_call(score_kernel, out_shape=jax.ShapeDtypeStruct((NX * NY, 128...]
  transfers between devices with their start and end apart: 17 -> 18, of which waited for: 10 -> 8; matrix products, arithmetic and copies ran while one was open for 7% -> 11% of each run, Pallas kernels for 0% -> 0%
where the time goes in v2:
time: 209 us; the launch traced here: 208 us
  starting transfers between devices  66.7 us (32%)
  waiting for transfers between devices  52.1 us (25%)
  blocking collectives  36.2 us (17%)
  local copies, waits for them, and re-layouts  17.4 us (8%)
  between operations  14.1 us (7%)
  Pallas kernels  9.78 us (5%)
  matrix products  8.31 us (4%)
  other arithmetic  3.51 us (2%)
    ppermute x8, starting transfers between devices, local(): got.append(lax.ppermute(piece, ('dp', 'tensor'), perm))  41.1 us
    all_gather x1, waiting for transfers between devices, local(): own = lax.all_gather(jnp.stack(got), 'dp', axis_index_groups=ZG)  20.5 us
    all_to_all x1, blocking collectives, local(): lax.all_to_all(tile, 'tensor', 0, 0, tiled=True).sum(0)[:seqs * queries]  18.5 us
    all_to_all x1, blocking collectives, local(): lax.all_to_all(in_basis.reshape(NX, NY * 128, 128), 'tensor', 0, 0, axis_...  17.7 us
    all_to_all x1, waiting for transfers between devices, local(): g_parts = lax.all_to_all(g_part, 'tensor', 0, 0, axis_index_groups=XG)  15.5 us
    ppermute x3, waiting for transfers between devices, shift_x(): return lax.ppermute(array, 'tensor', perm)  10.2 us
    pallas_call x1, Pallas kernels, score_tiles(): pl.pallas_call(score_kernel, out_shape=jax.ShapeDtypeStruct((NX * NY, 128...  9.78 us
    ppermute x3, starting transfers between devices, shift_x(): return lax.ppermute(array, 'tensor', perm)  8.42 us
  transfers between devices with their start and end apart: 18, of which 8 were waited for; matrix products, arithmetic and copies ran while one was open for 11% of the time, Pallas kernels for 0%

profile of v2, /device:TPU:1, one launch (start us, length us, event | category | flops | bytes accessed | tf_op | source)
XLA Modules:
  0.0 208.2 jit_solution(7319817734032342353)
XLA Ops:
  11.5 4.8 %collective-permute-start.4 = (bf16[176,128]{1,0:T(8,128)(2,1)S(1)}, bf16[176,128]{1,0:T(8,128)(2,1)S(1)}, u32[]{:S(2)}, u32[]{:S(2)}) collective-permute-start(bf16[176,128]{1,0:T(8,128)(2,1)S(1)} %get-tuple-element.11), channel_id=1, source_target_pairs={{0,64},{1,65},{2,66},{3,67},{4,68},{5,69},{6,70},{7,71},{8,192},{9... | collective-permute-start | bytes 135176 | tf_op jit(solution)/shard_map/ppermute | solution.py:111
  16.4 9.1 %collective-permute-start.5 = (bf16[176,128]{1,0:T(8,128)(2,1)S(1)}, bf16[176,128]{1,0:T(8,128)(2,1)S(1)}, u32[]{:S(2)}, u32[]{:S(2)}) collective-permute-start(bf16[176,128]{1,0:T(8,128)(2,1)S(1)} %get-tuple-element.10), channel_id=1, source_target_pairs={{0,128},{1,129},{2,130},{3,131},{4,132},{5,133},{6,134},{7,135},{8... | collective-permute-start | bytes 135176 | tf_op jit(solution)/shard_map/ppermute | solution.py:111
  25.5 4.1 %collective-permute-start.6 = (bf16[176,128]{1,0:T(8,128)(2,1)S(1)}, bf16[176,128]{1,0:T(8,128)(2,1)S(1)}, u32[]{:S(2)}, u32[]{:S(2)}) collective-permute-start(bf16[176,128]{1,0:T(8,128)(2,1)S(1)} %get-tuple-element.9), channel_id=1, source_target_pairs={{0,192},{1,193},{2,194},{3,195},{4,196},{5,197},{6,198},{7,199},{8... | collective-permute-start | bytes 135176 | tf_op jit(solution)/shard_map/ppermute | solution.py:111
  29.6 12.4 %collective-permute-start.7 = (bf16[176,128]{1,0:T(8,128)(2,1)S(1)}, bf16[176,128]{1,0:T(8,128)(2,1)S(1)}, u32[]{:S(2)}, u32[]{:S(2)}) collective-permute-start(bf16[176,128]{1,0:T(8,128)(2,1)S(1)} %get-tuple-element.8), channel_id=1, source_target_pairs={{0,256},{1,257},{2,258},{3,259},{4,260},{5,261},{6,262},{7,263},{8... | collective-permute-start | bytes 135176 | tf_op jit(solution)/shard_map/ppermute | solution.py:111
  42.0 3.7 %collective-permute-start.8 = (bf16[176,128]{1,0:T(8,128)(2,1)S(1)}, bf16[176,128]{1,0:T(8,128)(2,1)S(1)}, u32[]{:S(2)}, u32[]{:S(2)}) collective-permute-start(bf16[176,128]{1,0:T(8,128)(2,1)S(1)} %get-tuple-element.7), channel_id=1, source_target_pairs={{0,320},{1,321},{2,322},{3,323},{4,324},{5,325},{6,326},{7,327},{8... | collective-permute-start | bytes 135176 | tf_op jit(solution)/shard_map/ppermute | solution.py:111
  45.7 4.3 %collective-permute-start.9 = (bf16[176,128]{1,0:T(8,128)(2,1)S(1)}, bf16[176,128]{1,0:T(8,128)(2,1)S(1)}, u32[]{:S(2)}, u32[]{:S(2)}) collective-permute-start(bf16[176,128]{1,0:T(8,128)(2,1)S(1)} %get-tuple-element.6), channel_id=1, source_target_pairs={{0,384},{1,385},{2,386},{3,387},{4,388},{5,389},{6,390},{7,391},{8... | collective-permute-start | bytes 135176 | tf_op jit(solution)/shard_map/ppermute | solution.py:111
  52.8 2.8 %collective-permute-done.10 = bf16[176,128]{1,0:T(8,128)(2,1)S(1)} collective-permute-done((bf16[176,128]{1,0:T(8,128)(2,1)S(1)}, bf16[176,128]{1,0:T(8,128)(2,1)S(1)}, u32[]{:S(2)}, u32[]{:S(2)}) %collective-permute-start.10) | collective-permute-done | bytes 45088 | tf_op jit(solution)/shard_map/ppermute | solution.py:111
  56.4 17.7 %all_to_all.29 = bf16[4,1024,128]{2,1,0:T(8,128)(2,1)S(1)} all-to-all(bf16[4,1024,128]{2,1,0:T(8,128)(2,1)S(1)} %bitcast.89), channel_id=1, replica_groups={{0,8,16,24},{1,9,17,25},{2,10,18,26},{3,11,19,27},{4,12,20,28},{5,13,21..., dimensions={0} | all-to-all | bytes 2097152 | tf_op jit(solution)/shard_map/all_to_all | solution.py:117
  74.1 3.3 %fusion.2 = bf16[4,128,768]{1,2,0:T(8,128)(2,1)} fusion(bf16[4,8,128,128]{3,2,1,0:T(8,128)(2,1)S(1)} %bitcast.90, bf16[8,1824,128]{2,1,0:T(8,128)(2,1)} %bitcast.86), kind=kOutput, calls=%fused_computation.7 | convolution fusion | flops 805699584 | bytes 3407872 | tf_op jit(solution)/shard_map/xyed,yte->xdt/dot_general | solution.py:119
  77.3 3.5 %all-to-all-start.3 = ((bf16[4,128,768]{1,2,0:T(8,128)(2,1)}), bf16[4,128,768]{1,2,0:T(8,128)(2,1)S(1)}, u32[]{:S(2)}, u32[]{:S(2)}) async-start(bf16[4,128,768]{1,2,0:T(8,128)(2,1)} %fusion.2), calls=%async_computation.3 | async-start | bytes 1572864 | tf_op jit(solution)/shard_map/all_to_all | solution.py:120
  80.8 4.5 %reshape.69 = bf16[172,4,1376]{2,1,0:T(4,128)(2,1)S(1)} reshape(bf16[172,5504]{1,0:T(8,128)(2,1)} %param.11) | data formatting | bytes 3786752 | tf_op jit(solution)/shard_map/reshape | solution.py:115
  89.2 4.4 %all-to-all-start = ((bf16[4,172,1376]{2,1,0:T(8,128)(2,1)}), bf16[4,172,1376]{2,1,0:T(8,128)(2,1)}, u32[]{:S(2)}, u32[]{:S(2)}) async-start(bf16[4,172,1376]{2,1,0:T(8,128)(2,1)} %bitcast.76), calls=%async_computation | async-start | bytes 3964928 | tf_op jit(solution)/shard_map/all_to_all | solution.py:116
  93.6 20.5 %all-gather.10.cloned.1.call-done = bf16[64,176,128]{2,1,0:T(8,128)(2,1)} async-done(((bf16[8,176,128]{2,1,0:T(8,128)(2,1)}), bf16[64,176,128]{2,1,0:T(8,128)(2,1)}) %all-gather.10.cloned.1.call-update) | async-done | bytes 2883600 | tf_op jit(solution)/shard_map/all_gather | solution.py:112
  114.2 4.7 %collective-permute-start.11 = (bf16[8,8,176,128]{3,2,1,0:T(8,128)(2,1)}, bf16[8,8,176,128]{3,2,1,0:T(8,128)(2,1)}, u32[]{:S(2)}, u32[]{:S(2)}) collective-permute-start(bf16[8,8,176,128]{3,2,1,0:T(8,128)(2,1)} %bitcast.80), channel_id=1, source_target_pairs={{0,32},{32,0},{64,96},{96,64},{128,160},{160,128},{192,224},{224,1... | collective-permute-start | bytes 8650760 | tf_op jit(solution)/shard_map/ppermute | solution.py:113
  122.3 3.5 %reshape.76 = bf16[1376,768,1]{1,0,2:T(8,128)(2,1)} reshape(bf16[8,172,6,128]{3,2,1,0:T(8,128)(2,1)S(1)} %bitcast.82) | data formatting | bytes 4227072 | tf_op jit(solution)/shard_map/reshape | solution.py:123
  125.8 5.1 %fusion.1 = bf16[4,172,768]{2,1,0:T(8,128)(2,1)} fusion(bf16[1376,768,1]{1,0,2:T(8,128)(2,1)} %reshape.76, bf16[4,172,1376]{2,1,0:T(8,128)(2,1)} %all-to-all-done), kind=kOutput, calls=%fused_computation.6 | convolution fusion | flops 1454641152 | bytes 5063680 | tf_op jit(solution)/shard_map/xjk,kt->xjt/dot_general | solution.py:124
  130.8 4.5 %all-to-all-start.1 = ((bf16[4,172,768]{2,1,0:T(8,128)(2,1)}), bf16[4,172,768]{2,1,0:T(8,128)(2,1)}, u32[]{:S(2)}, u32[]{:S(2)}) async-start(bf16[4,172,768]{2,1,0:T(8,128)(2,1)} %fusion.1), calls=%async_computation.1 | async-start | bytes 2162688 | tf_op jit(solution)/shard_map/all_to_all | solution.py:125
  135.4 15.5 %all-to-all-done.1 = bf16[4,172,768]{2,1,0:T(8,128)(2,1)} async-done(((bf16[4,172,768]{2,1,0:T(8,128)(2,1)}), bf16[4,172,768]{2,1,0:T(8,128)(2,1)}, u32[]{:S(2)}, u32[]{:S(2)}) %all-to-all-start.1) | async-done | bytes 1056800 | tf_op jit(solution)/shard_map/all_to_all | solution.py:125
  154.6 3.7 %collective-permute-start.1 = (bf16[176,768]{1,0:T(8,128)(2,1)S(1)}, bf16[176,768]{1,0:T(8,128)(2,1)}, u32[]{:S(2)}, u32[]{:S(2)}) collective-permute-start(bf16[176,768]{1,0:T(8,128)(2,1)S(1)} %pad.13.g0_ref), channel_id=1, source_target_pairs={{0,16},{1,17},{2,18},{3,19},{4,20},{5,21},{6,22},{7,23},{8,24},{9,... | collective-permute-start | bytes 811016 | tf_op jit(solution)/shard_map/ppermute | solution.py:18
  158.3 2.5 %collective-permute-start.2 = (bf16[176,768]{1,0:T(8,128)(2,1)S(1)}, bf16[176,768]{1,0:T(8,128)(2,1)}, u32[]{:S(2)}, u32[]{:S(2)}) collective-permute-start(bf16[176,768]{1,0:T(8,128)(2,1)S(1)} %pad.13.g0_ref), channel_id=1, source_target_pairs={{0,24},{1,25},{2,26},{3,27},{4,28},{5,29},{6,30},{7,31},{8,0},{9,1... | collective-permute-start | bytes 811016 | tf_op jit(solution)/shard_map/ppermute | solution.py:18
  163.2 4.8 %collective-permute-done.1.g2_ref = bf16[176,768]{1,0:T(8,128)(2,1)} collective-permute-done((bf16[176,768]{1,0:T(8,128)(2,1)S(1)}, bf16[176,768]{1,0:T(8,128)(2,1)}, u32[]{:S(2)}, u32[]{:S(2)}) %collective-permute-start.1) | collective-permute-done | bytes 270368 | tf_op jit(solution)/shard_map/ppermute | solution.py:18
  168.0 3.1 %collective-permute-done.2.g3_ref = bf16[176,768]{1,0:T(8,128)(2,1)} collective-permute-done((bf16[176,768]{1,0:T(8,128)(2,1)S(1)}, bf16[176,768]{1,0:T(8,128)(2,1)}, u32[]{:S(2)}, u32[]{:S(2)}) %collective-permute-start.2) | collective-permute-done | bytes 270368 | tf_op jit(solution)/shard_map/ppermute | solution.py:18
  172.6 9.8 %shard_map.82 = f32[32,128]{1,0:T(8,128)S(1)} custom-call(s32[2]{0:T(128)S(1)} %pad_add_fusion.where_ref, bf16[176,768]{1,0:T(8,128)(2,1)S(1)} %pad.13.g0_ref, bf16[176,768]{1,0:T(8,128)(2,1)S(1)} %collective-permute-done.g1_ref, bf16[176,768]{1,0:T(8,128)(2,1)} %collective-permute-done.1.g2_ref, bf16[176,768]{1,0:T(8,128)(2,1)} %collective-permute-done.2.g3_ref, ...), custom_call_target="tpu_custom_call" | custom-call | flops 4429185024 | bytes 9000000 | tf_op jit(solution)/shard_map/pallas_call | solution.py:62
  182.4 18.5 %all_to_all.30 = f32[32,1,128]{2,1,0:T(1,128)S(1)} all-to-all(f32[32,1,128]{2,1,0:T(1,128)S(1)} %bitcast.79), channel_id=1, replica_groups=mesh['dp'=16,'tensor'=32] {'tensor'}, dimensions={0} | all-to-all | bytes 32768 | tf_op jit(solution)/shard_map/all_to_all | solution.py:134
  (66 shorter events, 23.3 us)
Async XLA Ops:
  6.5 3.9 %copy-start.5 = (f32[172,256]{1,0:T(8,128)S(1)}, f32[172,256]{1,0:T(8,128)}, u32[]{:S(2)}) copy-start(f32[172,256]{1,0:T(8,128)} %param.13) | copy-start | bytes 528388
  6.5 3.9 %copy-start.4 = (bf16[4,172,256]{2,0,1:T(4,128)(2,1)S(1)}, bf16[4,172,256]{2,0,1:T(4,128)(2,1)}, u32[]{:S(2)}) copy-start(bf16[4,172,256]{2,0,1:T(4,128)(2,1)} %param.12) | copy-start | bytes 1056772
  6.5 67.6 %all-gather.8.cloned.1.call-start = ((), (), s32[]{:S(2)}) async-start(), calls=%async_computation.6 | async-start | bytes 4202496 | tf_op jit(solution)/shard_map/all_gather | solution.py:94
  9.7 104.5 %all-gather.10.cloned.1.call-start = ((), (), s32[]{:S(2)}) async-start(), calls=%async_computation.7 | async-start | bytes 3244032 | tf_op jit(solution)/shard_map/all_gather | solution.py:112
  10.5 45.9 %copy-start.2 = (bf16[4096,128]{1,0:T(8,128)(2,1)S(1)}, bf16[4096,128]{1,0:T(8,128)(2,1)}, u32[]{:S(2)}) copy-start(bf16[4096,128]{1,0:T(8,128)(2,1)} %param.10) | copy-start | bytes 3145732
  10.7 31.3 %collective-permute-start.3 = (bf16[176,128]{1,0:T(8,128)(2,1)S(1)}, bf16[176,128]{1,0:T(8,128)(2,1)S(1)}, u32[]{:S(2)}, u32[]{:S(2)}) collective-permute-start(bf16[176,128]{1,0:T(8,128)(2,1)S(1)} %get-tuple-element.12), channel_id=1, source_target_pairs={{0,0},{1,1},{2,2},{3,3},{4,4},{5,5},{6,6},{7,7},{8,128},{9,129},{1... | collective-permute-start | bytes 135176 | tf_op jit(solution)/shard_map/ppermute | solution.py:111
  11.5 34.2 %collective-permute-start.4 = (bf16[176,128]{1,0:T(8,128)(2,1)S(1)}, bf16[176,128]{1,0:T(8,128)(2,1)S(1)}, u32[]{:S(2)}, u32[]{:S(2)}) collective-permute-start(bf16[176,128]{1,0:T(8,128)(2,1)S(1)} %get-tuple-element.11), channel_id=1, source_target_pairs={{0,64},{1,65},{2,66},{3,67},{4,68},{5,69},{6,70},{7,71},{8,192},{9... | collective-permute-start | bytes 135176 | tf_op jit(solution)/shard_map/ppermute | solution.py:111
  16.4 33.6 %collective-permute-start.5 = (bf16[176,128]{1,0:T(8,128)(2,1)S(1)}, bf16[176,128]{1,0:T(8,128)(2,1)S(1)}, u32[]{:S(2)}, u32[]{:S(2)}) collective-permute-start(bf16[176,128]{1,0:T(8,128)(2,1)S(1)} %get-tuple-element.10), channel_id=1, source_target_pairs={{0,128},{1,129},{2,130},{3,131},{4,132},{5,133},{6,134},{7,135},{8... | collective-permute-start | bytes 135176 | tf_op jit(solution)/shard_map/ppermute | solution.py:111
  25.5 26.5 %collective-permute-start.6 = (bf16[176,128]{1,0:T(8,128)(2,1)S(1)}, bf16[176,128]{1,0:T(8,128)(2,1)S(1)}, u32[]{:S(2)}, u32[]{:S(2)}) collective-permute-start(bf16[176,128]{1,0:T(8,128)(2,1)S(1)} %get-tuple-element.9), channel_id=1, source_target_pairs={{0,192},{1,193},{2,194},{3,195},{4,196},{5,197},{6,198},{7,199},{8... | collective-permute-start | bytes 135176 | tf_op jit(solution)/shard_map/ppermute | solution.py:111
  29.6 22.5 %collective-permute-start.7 = (bf16[176,128]{1,0:T(8,128)(2,1)S(1)}, bf16[176,128]{1,0:T(8,128)(2,1)S(1)}, u32[]{:S(2)}, u32[]{:S(2)}) collective-permute-start(bf16[176,128]{1,0:T(8,128)(2,1)S(1)} %get-tuple-element.8), channel_id=1, source_target_pairs={{0,256},{1,257},{2,258},{3,259},{4,260},{5,261},{6,262},{7,263},{8... | collective-permute-start | bytes 135176 | tf_op jit(solution)/shard_map/ppermute | solution.py:111
  42.0 10.1 %collective-permute-start.8 = (bf16[176,128]{1,0:T(8,128)(2,1)S(1)}, bf16[176,128]{1,0:T(8,128)(2,1)S(1)}, u32[]{:S(2)}, u32[]{:S(2)}) collective-permute-start(bf16[176,128]{1,0:T(8,128)(2,1)S(1)} %get-tuple-element.7), channel_id=1, source_target_pairs={{0,320},{1,321},{2,322},{3,323},{4,324},{5,325},{6,326},{7,327},{8... | collective-permute-start | bytes 135176 | tf_op jit(solution)/shard_map/ppermute | solution.py:111
  45.7 7.0 %collective-permute-start.9 = (bf16[176,128]{1,0:T(8,128)(2,1)S(1)}, bf16[176,128]{1,0:T(8,128)(2,1)S(1)}, u32[]{:S(2)}, u32[]{:S(2)}) collective-permute-start(bf16[176,128]{1,0:T(8,128)(2,1)S(1)} %get-tuple-element.6), channel_id=1, source_target_pairs={{0,384},{1,385},{2,386},{3,387},{4,388},{5,389},{6,390},{7,391},{8... | collective-permute-start | bytes 135176 | tf_op jit(solution)/shard_map/ppermute | solution.py:111
  50.0 5.6 %collective-permute-start.10 = (bf16[176,128]{1,0:T(8,128)(2,1)S(1)}, bf16[176,128]{1,0:T(8,128)(2,1)S(1)}, u32[]{:S(2)}, u32[]{:S(2)}) collective-permute-start(bf16[176,128]{1,0:T(8,128)(2,1)S(1)} %get-tuple-element.5), channel_id=1, source_target_pairs={{0,448},{1,449},{2,450},{3,451},{4,452},{5,453},{6,454},{7,455},{8... | collective-permute-start | bytes 135176 | tf_op jit(solution)/shard_map/ppermute | solution.py:111
  77.3 11.8 %all-to-all-start.3 = ((bf16[4,128,768]{1,2,0:T(8,128)(2,1)}), bf16[4,128,768]{1,2,0:T(8,128)(2,1)S(1)}, u32[]{:S(2)}, u32[]{:S(2)}) async-start(bf16[4,128,768]{1,2,0:T(8,128)(2,1)} %fusion.2), calls=%async_computation.3 | async-start | bytes 1572864 | tf_op jit(solution)/shard_map/all_to_all | solution.py:120
  89.2 36.6 %all-to-all-start = ((bf16[4,172,1376]{2,1,0:T(8,128)(2,1)}), bf16[4,172,1376]{2,1,0:T(8,128)(2,1)}, u32[]{:S(2)}, u32[]{:S(2)}) async-start(bf16[4,172,1376]{2,1,0:T(8,128)(2,1)} %bitcast.76), calls=%async_computation | async-start | bytes 3964928 | tf_op jit(solution)/shard_map/all_to_all | solution.py:116
  93.6 77.6 %all-gather.6.cloned.1.call-start = ((), (), s32[]{:S(2)}) async-start(), calls=%async_computation.5 | async-start | bytes 1769472 | tf_op jit(solution)/shard_map/all_gather | solution.py:121
  114.2 57.0 %collective-permute-start.11 = (bf16[8,8,176,128]{3,2,1,0:T(8,128)(2,1)}, bf16[8,8,176,128]{3,2,1,0:T(8,128)(2,1)}, u32[]{:S(2)}, u32[]{:S(2)}) collective-permute-start(bf16[8,8,176,128]{3,2,1,0:T(8,128)(2,1)} %bitcast.80), channel_id=1, source_target_pairs={{0,32},{32,0},{64,96},{96,64},{128,160},{160,128},{192,224},{224,1... | collective-permute-start | bytes 8650760 | tf_op jit(solution)/shard_map/ppermute | solution.py:113
  125.8 9.6 %copy-start.6 = (s32[6]{0:T(128)S(1)}, s32[6]{0:T(128)}, u32[]{:S(2)}) copy-start(s32[6]{0:T(128)} %param.15) | copy-start | bytes 76
  130.8 40.3 %copy-start = (bf16[64,176,128]{2,1,0:T(8,128)(2,1)S(1)}, bf16[64,176,128]{2,1,0:T(8,128)(2,1)}, u32[]{:S(2)}) copy-start(bf16[64,176,128]{2,1,0:T(8,128)(2,1)} %all-gather.10.cloned.1.call-done) | copy-start | bytes 8650756
  130.8 20.1 %all-to-all-start.1 = ((bf16[4,172,768]{2,1,0:T(8,128)(2,1)}), bf16[4,172,768]{2,1,0:T(8,128)(2,1)}, u32[]{:S(2)}, u32[]{:S(2)}) async-start(bf16[4,172,768]{2,1,0:T(8,128)(2,1)} %fusion.1), calls=%async_computation.1 | async-start | bytes 2162688 | tf_op jit(solution)/shard_map/all_to_all | solution.py:125
  152.4 10.8 %collective-permute-start = (bf16[176,768]{1,0:T(8,128)(2,1)S(1)}, bf16[176,768]{1,0:T(8,128)(2,1)S(1)}, u32[]{:S(2)}, u32[]{:S(2)}) collective-permute-start(bf16[176,768]{1,0:T(8,128)(2,1)S(1)} %pad.13.g0_ref), channel_id=1, source_target_pairs={{0,8},{1,9},{2,10},{3,11},{4,12},{5,13},{6,14},{7,15},{8,16},{9,17... | collective-permute-start | bytes 811016 | tf_op jit(solution)/shard_map/ppermute | solution.py:18
  154.6 13.4 %collective-permute-start.1 = (bf16[176,768]{1,0:T(8,128)(2,1)S(1)}, bf16[176,768]{1,0:T(8,128)(2,1)}, u32[]{:S(2)}, u32[]{:S(2)}) collective-permute-start(bf16[176,768]{1,0:T(8,128)(2,1)S(1)} %pad.13.g0_ref), channel_id=1, source_target_pairs={{0,16},{1,17},{2,18},{3,19},{4,20},{5,21},{6,22},{7,23},{8,24},{9,... | collective-permute-start | bytes 811016 | tf_op jit(solution)/shard_map/ppermute | solution.py:18
  158.3 12.9 %collective-permute-start.2 = (bf16[176,768]{1,0:T(8,128)(2,1)S(1)}, bf16[176,768]{1,0:T(8,128)(2,1)}, u32[]{:S(2)}, u32[]{:S(2)}) collective-permute-start(bf16[176,768]{1,0:T(8,128)(2,1)S(1)} %pad.13.g0_ref), channel_id=1, source_target_pairs={{0,24},{1,25},{2,26},{3,27},{4,28},{5,29},{6,30},{7,31},{8,0},{9,1... | collective-permute-start | bytes 811016 | tf_op jit(solution)/shard_map/ppermute | solution.py:18
  171.2 1.4 copy-start.1
  (1 other events, 0.7 us)
Sparse Core Ops, SparseCore 0:
  9.8 58.3 all-gather.7
  70.2 43.8 all-gather.9
  119.9 36.0 all-gather.5

commit v3 on v2

v3 whole, which is shorter than its diff:
```python
import jax
import jax.numpy as jnp
from jax import lax
from jax.experimental import pallas as pl
from jax.experimental.pallas import tpu as pltpu
from jax.sharding import PartitionSpec as P

NX, NY, NZ = 4, 8, 8
XG = [[x * NY + y for x in range(NX)] for y in range(NY)]
YG = [[x * NY + y for y in range(NY)] for x in range(NX)]
ZG = [[z * 2 + c for z in range(NZ)] for c in range(2)]
SEQ = 128
PAD = 176


def shift_x(array, by):
    perm = [(x * NY + y, (x + by) % NX * NY + y) for x in range(NX) for y in range(NY)]
    return lax.ppermute(array, "tensor", perm)


def score_kernel(kx_ref, g0_ref, g1_ref, g2_ref, g3_ref, a_ref, s_ref, o_ref):
    q = pl.program_id(0)
    queries = pl.num_programs(0)
    tokens = g0_ref.shape[1]
    acc = jnp.zeros((8, tokens), jnp.float32)
    for d, g_ref in enumerate((g0_ref, g1_ref, g2_ref, g3_ref)):
        fx = (kx_ref[0] - d) & (NX - 1)
        tiles = [s_ref[half, core, fx, high] for high in range(2) for core in range(2) for half in range(2)]
        t = jnp.dot(jnp.concatenate(tiles, axis=1), a_ref[...], preferred_element_type=jnp.float32)
        acc += (t * g_ref[...].astype(jnp.float32)).reshape(PAD // 8, 8, tokens).sum(0)
    per_token = jnp.sum(acc, axis=0, keepdims=True)
    lane = lax.broadcasted_iota(jnp.int32, o_ref.shape, 1)

    @pl.when(q == 0)
    def _():
        o_ref[...] = jnp.zeros_like(o_ref)

    out = o_ref[...]
    for s in range(tokens // SEQ):
        value = jnp.sum(per_token[:, s * SEQ : (s + 1) * SEQ], axis=1, keepdims=True)
        out = jnp.where(lane == s * queries + q, value, out)
    o_ref[...] = out


def score_tiles(kx, gs, at, tiles):
    tokens = at.shape[1]
    queries = tiles.shape[0] // 2
    whole = lambda q: (0, 0)
    return pl.pallas_call(
        score_kernel,
        grid=(queries,),
        out_shape=jax.ShapeDtypeStruct((NX * NY, 128), jnp.float32),
        in_specs=[pl.BlockSpec(memory_space=pltpu.SMEM)]
        + [pl.BlockSpec((PAD, tokens), whole)] * NX
        + [pl.BlockSpec(at.shape, whole), pl.BlockSpec((2,) + tiles.shape[1:], lambda q: (q, 0, 0, 0, 0, 0))],
        out_specs=pl.BlockSpec((NX * NY, 128), whole),
        compiler_params=pltpu.CompilerParams(vmem_limit_bytes=48 * 1024 * 1024),
        cost_estimate=pl.CostEstimate(
            flops=2 * NX * queries * PAD * NY * 128 * tokens, bytes_accessed=9_000_000, transcendentals=0
        ),
    )(kx, *gs, at, tiles)


def add_parts(parts):
    wide = [parts[n].astype(jnp.float32) for n in range(NX)]
    return (wide[0] + wide[1]) + (wide[2] + wide[3])


def local(activations, out_grads_t, in_basis, out_basis_t, query_proj, eigvals, damping, lengths):
    bf, f32 = jnp.bfloat16, jnp.float32
    tokens, width = activations.shape[0], out_grads_t.shape[0]
    seqs, queries = lengths.shape[0], query_proj.shape[0]
    seq_len = tokens // seqs
    kx = lax.shift_right_logical(lax.axis_index("tensor"), 3)

    grads = jnp.pad(out_grads_t.reshape(width, seqs, seq_len).transpose(1, 0, 2), ((0, 0), (0, PAD - width), (0, 0)))
    both = jnp.concatenate([activations, grads.reshape(seqs * PAD, seq_len)], axis=0)
    both = lax.all_gather(both, "tensor", axis_index_groups=YG)
    x8 = both[:, :tokens]
    y8 = both[:, tokens:].reshape(NY, seqs, PAD, seq_len)[:, :, :width]

    scaled = (query_proj.astype(f32) / (eigvals + damping[0])).astype(bf)
    scaled = jnp.pad(scaled, ((0, 0), (0, PAD - width), (0, 0)))
    pieces = scaled.reshape(queries, PAD, 2, 128).transpose(0, 2, 1, 3).reshape(8, PAD, 128)
    pieces = lax.all_to_all(pieces, "dp", 0, 0, axis_index_groups=ZG)
    pieces = lax.all_to_all(pieces.reshape(NX, 2, PAD, 128), "tensor", 0, 0, axis_index_groups=XG)
    tiles = lax.all_gather(pieces, "dp").reshape(NZ, 2, NX, 2, PAD, 128)

    v4 = out_basis_t.reshape(width, NX, NY * width).transpose(1, 0, 2)
    vs = [lax.dynamic_index_in_dim(v4, (kx + d) & (NX - 1), 0, keepdims=False) for d in range(NX)]
    vs = [vs[0]] + [shift_x(vs[d], d) for d in range(1, NX)]
    u4 = lax.all_to_all(in_basis.reshape(NX, NY * 128, 128), "tensor", 0, 0, axis_index_groups=XG)

    tie = (vs[1][:1, :1] + vs[2][:1, :1] + vs[3][:1, :1]) * 0
    u4 = lax.dynamic_update_slice(u4, u4[:1, :1, :1] + tie[None], (0, 0, 0))
    a_part = jnp.einsum("xyed,yte->xdt", u4.reshape(NX, NY, 128, 128), x8, preferred_element_type=f32).astype(bf)
    a_parts = lax.all_to_all(a_part, "tensor", 0, 0, axis_index_groups=XG)
    at = jnp.broadcast_to(add_parts(a_parts).astype(bf), (NY, 128, tokens))
    at = lax.all_to_all(at, "tensor", 0, 0, axis_index_groups=YG)

    y8 = y8.transpose(0, 2, 1, 3).reshape(NY * width, tokens)
    g_parts = [jnp.dot(v, y8, preferred_element_type=f32).astype(bf) for v in vs]
    g_parts = [g_parts[0]] + [shift_x(g_parts[d], -d) for d in range(1, NX)]
    position = lax.broadcasted_iota(jnp.int32, (seqs, seq_len), 1)
    keep = (position < lengths[:, None]).astype(f32).reshape(1, tokens)
    g = (add_parts(g_parts) * keep).astype(bf)
    g = jnp.pad(g, ((0, PAD - width), (0, 0)))
    gs = [g] + [shift_x(g, d) for d in range(1, NX)]

    tile = score_tiles(kx.reshape(1), gs, at.reshape(NY * 128, tokens), tiles)
    totals = lax.all_to_all(tile, "tensor", 0, 0, tiled=True).sum(0)[: seqs * queries]
    norm_factor = (in_basis.shape[0] * out_basis_t.shape[1] * seq_len) ** (-0.5)
    return totals.reshape(seqs, queries) * norm_factor


def solution(mesh):
    placed = (
        P("dp", "tensor"),
        P("tensor", "dp"),
        P(None, "tensor"),
        P("tensor", None),
        P(None, "tensor", "dp"),
        P("tensor", "dp"),
        P(),
        P("dp"),
    )
    return jax.shard_map(
        local, mesh=mesh, in_specs=placed, out_specs=P("dp", None), check_vma=False
    )
```

time: 209 us -> 190 us (0.909)
  blocking collectives: 36.2 us -> 68.6 us
  starting transfers between devices: 66.7 us -> 38 us
  waiting for transfers between devices: 52.1 us -> 33.3 us
  matrix products: 8.31 us -> 4.86 us
  between operations: 14.1 us -> 16.8 us
  Pallas kernels: 9.78 us -> 7.15 us
    ppermute x9 -> x0, starting transfers between devices: 45.8 us -> none  [the longest x8 41.1 us: local(): got.append(lax.ppermute(piece, ('dp', 'tensor'), perm))]
    all_to_all x1 -> x3, blocking collectives: 17.7 us -> 50 us  [the longest x1 23.6 us: local(): pieces = lax.all_to_all(pieces, 'dp', 0, 0, axis_index_groups=ZG)]
    ppermute x3 -> x9, waiting for transfers between devices: 10.2 us -> 33.2 us  [shift_x(): return lax.ppermute(array, 'tensor', perm)]
    all_gather x2 -> x1, waiting for transfers between devices: 20.6 us -> 0.01 us  [local(): tiles = lax.all_gather(pieces, 'dp').reshape(NZ, 2, NX, 2, PAD, 128)]
    ppermute x3 -> x9, starting transfers between devices: 8.42 us -> 27.6 us  [shift_x(): return lax.ppermute(array, 'tensor', perm)]
    all_to_all x3 -> x2, waiting for transfers between devices: 17.8 us -> 0.01 us  [the longest x1 0.01 us: local(): lax.all_to_all(in_basis.reshape(NX, NY * 128, 128), 'tensor', 0, 0, axis_...]
    another operation x1, local copies, waits for them, and re-layouts: 0.01 us -> 4.81 us  [local(): own = lax.all_gather(jnp.stack(got), 'dp', axis_index_groups=ZG)]
    ppermute x9 -> x0, waiting for transfers between devices: 3.51 us -> none  [the longest x8 3.51 us: local(): got.append(lax.ppermute(piece, ('dp', 'tensor'), perm))]
  transfers between devices with their start and end apart: 18 -> 13, of which waited for: 8 -> 8; matrix products, arithmetic and copies ran while one was open for 11% -> 11% of each run, Pallas kernels for 0% -> 0%
where the time goes in v3:
time: 190 us; the launch traced here: 188 us
  blocking collectives  68.6 us (36%)
  starting transfers between devices  38 us (20%)
  waiting for transfers between devices  33.3 us (18%)
  local copies, waits for them, and re-layouts  17.6 us (9%)
  between operations  16.8 us (9%)
  Pallas kernels  7.15 us (4%)
  matrix products  4.86 us (3%)
  other arithmetic  2.23 us (1%)
    ppermute x9, waiting for transfers between devices, shift_x(): return lax.ppermute(array, 'tensor', perm)  33.2 us
    ppermute x9, starting transfers between devices, shift_x(): return lax.ppermute(array, 'tensor', perm)  27.6 us
    all_to_all x1, blocking collectives, local(): pieces = lax.all_to_all(pieces, 'dp', 0, 0, axis_index_groups=ZG)  23.6 us
    all_to_all x1, blocking collectives, local(): lax.all_to_all(tile, 'tensor', 0, 0, tiled=True).sum(0)[:seqs * queries]  18.6 us
    all_to_all x1, blocking collectives, local(): a_parts = lax.all_to_all(a_part, 'tensor', 0, 0, axis_index_groups=XG)  16.4 us
    all_to_all x1, blocking collectives, local(): lax.all_to_all(pieces.reshape(NX, 2, PAD, 128), 'tensor', 0, 0, axis_inde...  9.96 us
    pallas_call x1, Pallas kernels, score_tiles(): pl.pallas_call(score_kernel, grid=(queries,), out_shape=jax.ShapeDtypeStr...  7.15 us
    all_to_all x1, starting transfers between devices, local(): at = lax.all_to_all(at, 'tensor', 0, 0, axis_index_groups=YG)  6.77 us
  transfers between devices with their start and end apart: 13, of which 8 were waited for; matrix products, arithmetic and copies ran while one was open for 11% of the time, Pallas kernels for 0%

profile of v3, /device:TPU:1, one launch (start us, length us, event | category | flops | bytes accessed | tf_op | source)
XLA Modules:
  0.0 188.5 jit_solution(11809745001150894058)
XLA Ops:
  10.6 23.6 %all_to_all.34 = bf16[8,176,128]{2,1,0:T(8,128)(2,1)S(1)} all-to-all(bf16[8,176,128]{2,1,0:T(8,128)(2,1)S(1)} %bitcast.75), channel_id=1, replica_groups={{0,64,128,192,256,320,384,448},{32,96,160,224,288,352,416,480},{1,65,12..., dimensions={0} | all-to-all | bytes 720896 | tf_op jit(solution)/shard_map/all_to_all | solution.py:85
  34.2 10.0 %all_to_all.35 = bf16[4,2,176,128]{3,2,1,0:T(8,128)(2,1)} all-to-all(bf16[4,2,176,128]{3,2,1,0:T(8,128)(2,1)S(1)} %bitcast.76), channel_id=1, replica_groups={{0,8,16,24},{1,9,17,25},{2,10,18,26},{3,11,19,27},{4,12,20,28},{5,13,21..., dimensions={0} | all-to-all | bytes 720896 | tf_op jit(solution)/shard_map/all_to_all | solution.py:86
  44.2 3.5 %all-to-all-start = ((bf16[4,1024,128]{2,1,0:T(8,128)(2,1)}), bf16[4,1024,128]{2,1,0:T(8,128)(2,1)S(1)}, u32[]{:S(2)}, u32[]{:S(2)}) async-start(bf16[4,1024,128]{2,1,0:T(8,128)(2,1)} %bitcast.7), calls=%async_computation | async-start | bytes 2097152 | tf_op jit(solution)/shard_map/all_to_all | solution.py:92
  47.8 4.4 %reshape.87 = bf16[172,4,1376]{2,1,0:T(4,128)(2,1)S(1)} reshape(bf16[172,5504]{1,0:T(8,128)(2,1)} %param.11) | data formatting | bytes 3786752 | tf_op jit(solution)/shard_map/reshape | solution.py:89
  52.2 4.8 %constant_dynamic-slice_fusion.2 = (bf16[172,1,1376]{2,1,0:T(2,128)(2,1)S(1)}, bf16[172,1,1376]{2,1,0:T(2,128)(2,1)S(1)}, bf16[172,1,1376]{2,1,0:T(2,128)(2,1)S(1)}, bf16[172,1,1376]{2,1,0:T(2,128)(2,1)}) fusion(bf16[172,4,1376]{2,1,0:T(4,128)(2,1)S(1)} %reshape.87, s32[]{:T(128)S(6)} %select_n.14, s32[]{:T(128)S(6)} %select_n.16, s32[]{:T(128)S(6)} %select_n.15, ...), kind=kLoop, calls=%fused_computation.38 | loop fusion | bytes 3786768 | tf_op jit(solution)/shard_map/dynamic-slice.1
  57.1 3.3 %collective-permute-start = (bf16[172,1376]{1,0:T(8,128)(2,1)S(1)}, bf16[172,1376]{1,0:T(8,128)(2,1)S(1)}, u32[]{:S(2)}, u32[]{:S(2)}) collective-permute-start(bf16[172,1376]{1,0:T(8,128)(2,1)S(1)} %bitcast.83), channel_id=1, source_target_pairs={{0,8},{1,9},{2,10},{3,11},{4,12},{5,13},{6,14},{7,15},{8,16},{9,17... | collective-permute-start | bytes 1420040 | tf_op jit(solution)/shard_map/ppermute | solution.py:18
  60.5 4.3 %collective-permute-start.2 = (bf16[172,1376]{1,0:T(8,128)(2,1)S(1)}, bf16[172,1376]{1,0:T(8,128)(2,1)S(1)}, u32[]{:S(2)}, u32[]{:S(2)}) collective-permute-start(bf16[172,1376]{1,0:T(8,128)(2,1)S(1)} %bitcast.84), channel_id=1, source_target_pairs={{0,16},{1,17},{2,18},{3,19},{4,20},{5,21},{6,22},{7,23},{8,24},{9,... | collective-permute-start | bytes 1420040 | tf_op jit(solution)/shard_map/ppermute | solution.py:18
  64.9 3.1 %collective-permute-start.4 = (bf16[172,1376]{1,0:T(8,128)(2,1)S(1)}, bf16[172,1376]{1,0:T(8,128)(2,1)S(1)}, u32[]{:S(2)}, u32[]{:S(2)}) collective-permute-start(bf16[172,1376]{1,0:T(8,128)(2,1)S(1)} %bitcast.82), channel_id=1, source_target_pairs={{0,24},{1,25},{2,26},{3,27},{4,28},{5,29},{6,30},{7,31},{8,0},{9,1... | collective-permute-start | bytes 1420040 | tf_op jit(solution)/shard_map/ppermute | solution.py:18
  67.9 2.7 %collective-permute-done = bf16[172,1376]{1,0:T(8,128)(2,1)S(1)} collective-permute-done((bf16[172,1376]{1,0:T(8,128)(2,1)S(1)}, bf16[172,1376]{1,0:T(8,128)(2,1)S(1)}, u32[]{:S(2)}, u32[]{:S(2)}) %collective-permute-start) | collective-permute-done | bytes 473376 | tf_op jit(solution)/shard_map/ppermute | solution.py:18
  71.2 9.8 %collective-permute-done.2 = bf16[172,1376]{1,0:T(8,128)(2,1)S(1)} collective-permute-done((bf16[172,1376]{1,0:T(8,128)(2,1)S(1)}, bf16[172,1376]{1,0:T(8,128)(2,1)S(1)}, u32[]{:S(2)}, u32[]{:S(2)}) %collective-permute-start.2) | collective-permute-done | bytes 473376 | tf_op jit(solution)/shard_map/ppermute | solution.py:18
  86.7 2.5 %bitcast_convert_fusion = bf16[4,128,768]{2,1,0:T(8,128)(2,1)S(1)} fusion(bf16[4,8,128,128]{3,2,1,0:T(8,128)(2,1)S(1)} %bitcast.81, bf16[8,1824,128]{2,1,0:T(8,128)(2,1)} %bitcast.78), kind=kOutput, calls=%fused_computation.10 | convolution fusion | flops 805699584 | bytes 3407872 | tf_op jit(solution)/shard_map/xyed,yte->xdt/dot_general | solution.py:96
  89.2 16.4 %all_to_all.36 = bf16[4,128,768]{2,1,0:T(8,128)(2,1)S(1)} all-to-all(bf16[4,128,768]{2,1,0:T(8,128)(2,1)S(1)} %bitcast_convert_fusion), channel_id=1, replica_groups={{0,8,16,24},{1,9,17,25},{2,10,18,26},{3,11,19,27},{4,12,20,28},{5,13,21..., dimensions={0} | all-to-all | bytes 1572864 | tf_op jit(solution)/shard_map/all_to_all | solution.py:97
  107.0 6.8 %all-to-all-start.2 = ((bf16[8,128,768]{2,1,0:T(8,128)(2,1)}), bf16[8,128,768]{2,1,0:T(8,128)(2,1)S(1)}, u32[]{:S(2)}, u32[]{:S(2)}) async-start(bf16[8,128,768]{2,1,0:T(8,128)(2,1)} %broadcast_in_dim.9), calls=%async_computation.2 | async-start | bytes 3145728 | tf_op jit(solution)/shard_map/all_to_all | solution.py:99
  117.0 2.9 %collective-permute-start.1 = (bf16[172,768]{1,0:T(8,128)(2,1)S(1)}, bf16[172,768]{1,0:T(8,128)(2,1)S(1)}, u32[]{:S(2)}, u32[]{:S(2)}) collective-permute-start(bf16[172,768]{1,0:T(8,128)(2,1)S(1)} %fusion.15), channel_id=1, source_target_pairs={{0,24},{1,25},{2,26},{3,27},{4,28},{5,29},{6,30},{7,31},{8,0},{9,1... | collective-permute-start | bytes 792584 | tf_op jit(solution)/shard_map/ppermute | solution.py:18
  120.5 3.6 %collective-permute-start.3 = (bf16[172,768]{1,0:T(8,128)(2,1)S(1)}, bf16[172,768]{1,0:T(8,128)(2,1)S(1)}, u32[]{:S(2)}, u32[]{:S(2)}) collective-permute-start(bf16[172,768]{1,0:T(8,128)(2,1)S(1)} %fusion.18), channel_id=1, source_target_pairs={{0,16},{1,17},{2,18},{3,19},{4,20},{5,21},{6,22},{7,23},{8,24},{9,... | collective-permute-start | bytes 792584 | tf_op jit(solution)/shard_map/ppermute | solution.py:18
  124.7 1.9 %collective-permute-start.5 = (bf16[172,768]{1,0:T(8,128)(2,1)S(1)}, bf16[172,768]{1,0:T(8,128)(2,1)S(1)}, u32[]{:S(2)}, u32[]{:S(2)}) collective-permute-start(bf16[172,768]{1,0:T(8,128)(2,1)S(1)} %fusion.21), channel_id=1, source_target_pairs={{0,8},{1,9},{2,10},{3,11},{4,12},{5,13},{6,14},{7,15},{8,16},{9,17... | collective-permute-start | bytes 792584 | tf_op jit(solution)/shard_map/ppermute | solution.py:18
  127.3 2.4 %collective-permute-done.3 = bf16[172,768]{1,0:T(8,128)(2,1)S(1)} collective-permute-done((bf16[172,768]{1,0:T(8,128)(2,1)S(1)}, bf16[172,768]{1,0:T(8,128)(2,1)S(1)}, u32[]{:S(2)}, u32[]{:S(2)}) %collective-permute-start.3) | collective-permute-done | bytes 264224 | tf_op jit(solution)/shard_map/ppermute | solution.py:18
  129.7 7.6 %collective-permute-done.5 = bf16[172,768]{1,0:T(8,128)(2,1)S(1)} collective-permute-done((bf16[172,768]{1,0:T(8,128)(2,1)S(1)}, bf16[172,768]{1,0:T(8,128)(2,1)S(1)}, u32[]{:S(2)}, u32[]{:S(2)}) %collective-permute-start.5) | collective-permute-done | bytes 264224 | tf_op jit(solution)/shard_map/ppermute | solution.py:18
  139.3 2.6 %collective-permute-start.7 = (bf16[176,768]{1,0:T(8,128)(2,1)S(1)}, bf16[176,768]{1,0:T(8,128)(2,1)S(1)}, u32[]{:S(2)}, u32[]{:S(2)}) collective-permute-start(bf16[176,768]{1,0:T(8,128)(2,1)S(1)} %pad.13.g0_ref), channel_id=1, source_target_pairs={{0,16},{1,17},{2,18},{3,19},{4,20},{5,21},{6,22},{7,23},{8,24},{9,... | collective-permute-start | bytes 811016 | tf_op jit(solution)/shard_map/ppermute | solution.py:18
  142.0 4.0 %collective-permute-start.8 = (bf16[176,768]{1,0:T(8,128)(2,1)S(1)}, bf16[176,768]{1,0:T(8,128)(2,1)S(1)}, u32[]{:S(2)}, u32[]{:S(2)}) collective-permute-start(bf16[176,768]{1,0:T(8,128)(2,1)S(1)} %pad.13.g0_ref), channel_id=1, source_target_pairs={{0,24},{1,25},{2,26},{3,27},{4,28},{5,29},{6,30},{7,31},{8,0},{9,1... | collective-permute-start | bytes 811016 | tf_op jit(solution)/shard_map/ppermute | solution.py:18
  147.6 3.6 %collective-permute-done.7.g2_ref = bf16[176,768]{1,0:T(8,128)(2,1)S(1)} collective-permute-done((bf16[176,768]{1,0:T(8,128)(2,1)S(1)}, bf16[176,768]{1,0:T(8,128)(2,1)S(1)}, u32[]{:S(2)}, u32[]{:S(2)}) %collective-permute-start.7) | collective-permute-done | bytes 270368 | tf_op jit(solution)/shard_map/ppermute | solution.py:18
  151.2 3.9 %collective-permute-done.8.g3_ref = bf16[176,768]{1,0:T(8,128)(2,1)S(1)} collective-permute-done((bf16[176,768]{1,0:T(8,128)(2,1)S(1)}, bf16[176,768]{1,0:T(8,128)(2,1)S(1)}, u32[]{:S(2)}, u32[]{:S(2)}) %collective-permute-start.8) | collective-permute-done | bytes 270368 | tf_op jit(solution)/shard_map/ppermute | solution.py:18
  155.1 7.2 %shard_map.82 = f32[32,128]{1,0:T(8,128)S(1)} custom-call(s32[1]{0:T(128)} %bitcast.kx_ref, bf16[176,768]{1,0:T(8,128)(2,1)S(1)} %pad.13.g0_ref, bf16[176,768]{1,0:T(8,128)(2,1)S(1)} %collective-permute-done.6.g1_ref, bf16[176,768]{1,0:T(8,128)(2,1)S(1)} %collective-permute-done.7.g2_ref, bf16[176,768]{1,0:T(8,128)(2,1)S(1)} %collective-permute-done.8.g3_ref, ...), custom_call_target="tpu_custom_call" | custom-call | flops 4429185024 | bytes 9000000 | tf_op jit(solution)/shard_map/pallas_call | solution.py:49
  162.2 18.6 %all_to_all.37 = f32[32,1,128]{2,1,0:T(1,128)S(1)} all-to-all(f32[32,1,128]{2,1,0:T(1,128)S(1)} %bitcast.69), channel_id=1, replica_groups=mesh['dp'=16,'tensor'=32] {'tensor'}, dimensions={0} | all-to-all | bytes 32768 | tf_op jit(solution)/shard_map/all_to_all | solution.py:111
  (59 shorter events, 18.3 us)
Async XLA Ops:
  6.5 3.9 %copy-start.2 = (f32[172,256]{1,0:T(8,128)S(1)}, f32[172,256]{1,0:T(8,128)}, u32[]{:S(2)}) copy-start(f32[172,256]{1,0:T(8,128)} %param.13) | copy-start | bytes 528388
  6.5 3.9 %copy-start.1 = (bf16[4,172,256]{2,0,1:T(4,128)(2,1)S(1)}, bf16[4,172,256]{2,0,1:T(4,128)(2,1)}, u32[]{:S(2)}) copy-start(bf16[4,172,256]{2,0,1:T(4,128)(2,1)} %param.12) | copy-start | bytes 1056772
  6.5 80.2 %all-gather.5.cloned.1.call-start = ((), (), s32[]{:S(2)}) async-start(), calls=%async_computation.6 | async-start | bytes 4202496 | tf_op jit(solution)/shard_map/all_gather | solution.py:78
  9.7 145.4 %all-gather.7.cloned.1.call-start = ((), (), s32[]{:S(2)}) async-start(), calls=%async_computation.7 | async-start | bytes 6127616 | tf_op jit(solution)/shard_map/all_gather | solution.py:87
  44.2 41.3 %all-to-all-start = ((bf16[4,1024,128]{2,1,0:T(8,128)(2,1)}), bf16[4,1024,128]{2,1,0:T(8,128)(2,1)S(1)}, u32[]{:S(2)}, u32[]{:S(2)}) async-start(bf16[4,1024,128]{2,1,0:T(8,128)(2,1)} %bitcast.7), calls=%async_computation | async-start | bytes 2097152 | tf_op jit(solution)/shard_map/all_to_all | solution.py:92
  57.1 13.6 %collective-permute-start = (bf16[172,1376]{1,0:T(8,128)(2,1)S(1)}, bf16[172,1376]{1,0:T(8,128)(2,1)S(1)}, u32[]{:S(2)}, u32[]{:S(2)}) collective-permute-start(bf16[172,1376]{1,0:T(8,128)(2,1)S(1)} %bitcast.83), channel_id=1, source_target_pairs={{0,8},{1,9},{2,10},{3,11},{4,12},{5,13},{6,14},{7,15},{8,16},{9,17... | collective-permute-start | bytes 1420040 | tf_op jit(solution)/shard_map/ppermute | solution.py:18
  60.5 20.6 %collective-permute-start.2 = (bf16[172,1376]{1,0:T(8,128)(2,1)S(1)}, bf16[172,1376]{1,0:T(8,128)(2,1)S(1)}, u32[]{:S(2)}, u32[]{:S(2)}) collective-permute-start(bf16[172,1376]{1,0:T(8,128)(2,1)S(1)} %bitcast.84), channel_id=1, source_target_pairs={{0,16},{1,17},{2,18},{3,19},{4,20},{5,21},{6,22},{7,23},{8,24},{9,... | collective-permute-start | bytes 1420040 | tf_op jit(solution)/shard_map/ppermute | solution.py:18
  64.9 19.6 %collective-permute-start.4 = (bf16[172,1376]{1,0:T(8,128)(2,1)S(1)}, bf16[172,1376]{1,0:T(8,128)(2,1)S(1)}, u32[]{:S(2)}, u32[]{:S(2)}) collective-permute-start(bf16[172,1376]{1,0:T(8,128)(2,1)S(1)} %bitcast.82), channel_id=1, source_target_pairs={{0,24},{1,25},{2,26},{3,27},{4,28},{5,29},{6,30},{7,31},{8,0},{9,1... | collective-permute-start | bytes 1420040 | tf_op jit(solution)/shard_map/ppermute | solution.py:18
  81.0 4.5 %copy-start.4 = (bf16[172,1376]{1,0:T(8,128)(2,1)}, bf16[172,1376]{1,0:T(8,128)(2,1)S(1)}, u32[]{:S(2)}) copy-start(bf16[172,1376]{1,0:T(8,128)(2,1)S(1)} %collective-permute-done.2) | copy-start | bytes 1420036
  84.4 1.1 copy-start.6
  105.7 8.0 %copy-start.3 = (s32[6]{0:T(128)S(1)}, s32[6]{0:T(128)}, u32[]{:S(2)}) copy-start(s32[6]{0:T(128)} %param.15) | copy-start | bytes 76
  107.0 48.1 %all-to-all-start.2 = ((bf16[8,128,768]{2,1,0:T(8,128)(2,1)}), bf16[8,128,768]{2,1,0:T(8,128)(2,1)S(1)}, u32[]{:S(2)}, u32[]{:S(2)}) async-start(bf16[8,128,768]{2,1,0:T(8,128)(2,1)} %broadcast_in_dim.9), calls=%async_computation.2 | async-start | bytes 3145728 | tf_op jit(solution)/shard_map/all_to_all | solution.py:99
  116.4 3.5 %copy-start.5 = (bf16[172,1376]{1,0:T(8,128)(2,1)S(1)}, bf16[172,1376]{1,0:T(8,128)(2,1)}, u32[]{:S(2)}) copy-start(bf16[172,1376]{1,0:T(8,128)(2,1)} %copy-done.4) | copy-start | bytes 1420036
  117.0 7.1 %copy-start.7 = (bf16[172,1376]{1,0:T(8,128)(2,1)S(1)}, bf16[172,1376]{1,0:T(8,128)(2,1)}, u32[]{:S(2)}) copy-start(bf16[172,1376]{1,0:T(8,128)(2,1)} %copy-done.6) | copy-start | bytes 1420036
  117.0 10.3 %collective-permute-start.1 = (bf16[172,768]{1,0:T(8,128)(2,1)S(1)}, bf16[172,768]{1,0:T(8,128)(2,1)S(1)}, u32[]{:S(2)}, u32[]{:S(2)}) collective-permute-start(bf16[172,768]{1,0:T(8,128)(2,1)S(1)} %fusion.15), channel_id=1, source_target_pairs={{0,24},{1,25},{2,26},{3,27},{4,28},{5,29},{6,30},{7,31},{8,0},{9,1... | collective-permute-start | bytes 792584 | tf_op jit(solution)/shard_map/ppermute | solution.py:18
  120.5 6.2 %copy-start = (bf16[172,1,1376]{2,1,0:T(2,128)(2,1)S(1)}, bf16[172,1,1376]{2,1,0:T(2,128)(2,1)}, u32[]{:S(2)}) copy-start(bf16[172,1,1376]{2,1,0:T(2,128)(2,1)} %get-tuple-element.8) | copy-start | bytes 1420036
  120.5 9.1 %collective-permute-start.3 = (bf16[172,768]{1,0:T(8,128)(2,1)S(1)}, bf16[172,768]{1,0:T(8,128)(2,1)S(1)}, u32[]{:S(2)}, u32[]{:S(2)}) collective-permute-start(bf16[172,768]{1,0:T(8,128)(2,1)S(1)} %fusion.18), channel_id=1, source_target_pairs={{0,16},{1,17},{2,18},{3,19},{4,20},{5,21},{6,22},{7,23},{8,24},{9,... | collective-permute-start | bytes 792584 | tf_op jit(solution)/shard_map/ppermute | solution.py:18
  124.7 12.5 %collective-permute-start.5 = (bf16[172,768]{1,0:T(8,128)(2,1)S(1)}, bf16[172,768]{1,0:T(8,128)(2,1)S(1)}, u32[]{:S(2)}, u32[]{:S(2)}) collective-permute-start(bf16[172,768]{1,0:T(8,128)(2,1)S(1)} %fusion.21), channel_id=1, source_target_pairs={{0,8},{1,9},{2,10},{3,11},{4,12},{5,13},{6,14},{7,15},{8,16},{9,17... | collective-permute-start | bytes 792584 | tf_op jit(solution)/shard_map/ppermute | solution.py:18
  137.4 10.2 %collective-permute-start.6 = (bf16[176,768]{1,0:T(8,128)(2,1)S(1)}, bf16[176,768]{1,0:T(8,128)(2,1)S(1)}, u32[]{:S(2)}, u32[]{:S(2)}) collective-permute-start(bf16[176,768]{1,0:T(8,128)(2,1)S(1)} %pad.13.g0_ref), channel_id=1, source_target_pairs={{0,8},{1,9},{2,10},{3,11},{4,12},{5,13},{6,14},{7,15},{8,16},{9,17... | collective-permute-start | bytes 811016 | tf_op jit(solution)/shard_map/ppermute | solution.py:18
  139.3 11.9 %collective-permute-start.7 = (bf16[176,768]{1,0:T(8,128)(2,1)S(1)}, bf16[176,768]{1,0:T(8,128)(2,1)S(1)}, u32[]{:S(2)}, u32[]{:S(2)}) collective-permute-start(bf16[176,768]{1,0:T(8,128)(2,1)S(1)} %pad.13.g0_ref), channel_id=1, source_target_pairs={{0,16},{1,17},{2,18},{3,19},{4,20},{5,21},{6,22},{7,23},{8,24},{9,... | collective-permute-start | bytes 811016 | tf_op jit(solution)/shard_map/ppermute | solution.py:18
  142.0 13.1 %collective-permute-start.8 = (bf16[176,768]{1,0:T(8,128)(2,1)S(1)}, bf16[176,768]{1,0:T(8,128)(2,1)S(1)}, u32[]{:S(2)}, u32[]{:S(2)}) collective-permute-start(bf16[176,768]{1,0:T(8,128)(2,1)S(1)} %pad.13.g0_ref), channel_id=1, source_target_pairs={{0,24},{1,25},{2,26},{3,27},{4,28},{5,29},{6,30},{7,31},{8,0},{9,1... | collective-permute-start | bytes 811016 | tf_op jit(solution)/shard_map/ppermute | solution.py:18
Sparse Core Ops, SparseCore 0:
  9.8 58.3 all-gather.4
  70.3 47.4 all-gather.6

commit v4 on v3

--- a/solution.py
+++ b/solution.py
@@ -16,6 +16,37 @@
 def shift_x(array, by):
     perm = [(x * NY + y, (x + by) % NX * NY + y) for x in range(NX) for y in range(NY)]
     return lax.ppermute(array, "tensor", perm)
+
+
+def columns_kernel(kx_ref, v_ref, o0_ref, o1_ref, o2_ref, o3_ref, all_ref):
+    rows, columns = v_ref.shape
+    width = columns // (NX * NY)
+    for x in range(NX):
+        for y in range(NY):
+            first = (x * NY + y) * width
+            if first + PAD <= columns:
+                block = v_ref[:, first : first + PAD]
+            else:
+                block = jnp.concatenate(
+                    [v_ref[:, first:], jnp.zeros((rows, first + PAD - columns), v_ref.dtype)], axis=1
+                )
+            all_ref[x, :, y * PAD : (y + 1) * PAD] = block
+    for d, o_ref in enumerate((o0_ref, o1_ref, o2_ref, o3_ref)):
+        o_ref[...] = all_ref[(kx_ref[0] + d) & (NX - 1)]
+
+
+def column_blocks(kx, v):
+    one = jax.ShapeDtypeStruct((v.shape[0], NY * PAD), v.dtype)
+    vmem = pl.BlockSpec(memory_space=pltpu.VMEM)
+    return pl.pallas_call(
+        columns_kernel,
+        out_shape=[one] * NX,
+        in_specs=[pl.BlockSpec(memory_space=pltpu.SMEM), vmem],
+        out_specs=[vmem] * NX,
+        scratch_shapes=[pltpu.VMEM((NX,) + one.shape, v.dtype)],
+        compiler_params=pltpu.CompilerParams(vmem_limit_bytes=24 * 1024 * 1024),
+        cost_estimate=pl.CostEstimate(flops=0, bytes_accessed=4_000_000, transcendentals=0),
+    )(kx, v)
 
 
 def score_kernel(kx_ref, g0_ref, g1_ref, g2_ref, g3_ref, a_ref, s_ref, o_ref):
@@ -77,28 +108,29 @@
     both = jnp.concatenate([activations, grads.reshape(seqs * PAD, seq_len)], axis=0)
     both = lax.all_gather(both, "tensor", axis_index_groups=YG)
     x8 = both[:, :tokens]
-    y8 = both[:, tokens:].reshape(NY, seqs, PAD, seq_len)[:, :, :width]
+    y8 = both[:, tokens:].reshape(NY, seqs, PAD, seq_len)
 
     scaled = (query_proj.astype(f32) / (eigvals + damping[0])).astype(bf)
     scaled = jnp.pad(scaled, ((0, 0), (0, PAD - width), (0, 0)))
     pieces = scaled.reshape(queries, PAD, 2, 128).transpose(0, 2, 1, 3).reshape(8, PAD, 128)
+    blocks = column_blocks(kx.reshape(1), out_basis_t)
+    vs = [blocks[0]] + [shift_x(blocks[d], d) for d in range(1, NX)]
     pieces = lax.all_to_all(pieces, "dp", 0, 0, axis_index_groups=ZG)
-    pieces = lax.all_to_all(pieces.reshape(NX, 2, PAD, 128), "tensor", 0, 0, axis_index_groups=XG)
+    rows = NY * 128
+    mixed = jnp.concatenate([in_basis.reshape(NX, rows, 128), pieces.reshape(NX, 2 * PAD, 128)], axis=1)
+    tie = (vs[1][:1, :1] + vs[2][:1, :1] + vs[3][:1, :1]) * 0
+    mixed = lax.dynamic_update_slice(mixed, mixed[:1, :1, :1] + tie[None], (0, 0, 0))
+    mixed = lax.all_to_all(mixed, "tensor", 0, 0, axis_index_groups=XG)
+    u4 = mixed[:, :rows]
+    pieces = mixed[:, rows:].reshape(NX, 2, PAD, 128)
     tiles = lax.all_gather(pieces, "dp").reshape(NZ, 2, NX, 2, PAD, 128)
 
-    v4 = out_basis_t.reshape(width, NX, NY * width).transpose(1, 0, 2)
-    vs = [lax.dynamic_index_in_dim(v4, (kx + d) & (NX - 1), 0, keepdims=False) for d in range(NX)]
-    vs = [vs[0]] + [shift_x(vs[d], d) for d in range(1, NX)]
-    u4 = lax.all_to_all(in_basis.reshape(NX, NY * 128, 128), "tensor", 0, 0, axis_index_groups=XG)
-
-    tie = (vs[1][:1, :1] + vs[2][:1, :1] + vs[3][:1, :1]) * 0
-    u4 = lax.dynamic_update_slice(u4, u4[:1, :1, :1] + tie[None], (0, 0, 0))
     a_part = jnp.einsum("xyed,yte->xdt", u4.reshape(NX, NY, 128, 128), x8, preferred_element_type=f32).astype(bf)
     a_parts = lax.all_to_all(a_part, "tensor", 0, 0, axis_index_groups=XG)
     at = jnp.broadcast_to(add_parts(a_parts).astype(bf), (NY, 128, tokens))
     at = lax.all_to_all(at, "tensor", 0, 0, axis_index_groups=YG)
 
-    y8 = y8.transpose(0, 2, 1, 3).reshape(NY * width, tokens)
+    y8 = y8.transpose(0, 2, 1, 3).reshape(NY * PAD, tokens)
     g_parts = [jnp.dot(v, y8, preferred_element_type=f32).astype(bf) for v in vs]
     g_parts = [g_parts[0]] + [shift_x(g_parts[d], -d) for d in range(1, NX)]
     position = lax.broadcasted_iota(jnp.int32, (seqs, seq_len), 1)

time: 190 us -> 177 us (0.932)
  the two profiles are of different devices: /device:TPU:1 before, /device:TPU:64 now
where the time goes in v4:
time: 177 us; the launch traced here: 176 us
  blocking collectives  54.3 us (31%)
  starting transfers between devices  46.3 us (26%)
  waiting for transfers between devices  29.6 us (17%)
  between operations  17.2 us (10%)
  local copies, waits for them, and re-layouts  11.1 us (6%)
  Pallas kernels  8.46 us (5%)
  matrix products  4.84 us (3%)
  other arithmetic  4.45 us (3%)
    ppermute x9, waiting for transfers between devices, shift_x(): return lax.ppermute(array, 'tensor', perm)  29.6 us
    ppermute x9, starting transfers between devices, shift_x(): return lax.ppermute(array, 'tensor', perm)  29.2 us
    all_to_all x1, blocking collectives, local(): mixed = lax.all_to_all(mixed, 'tensor', 0, 0, axis_index_groups=XG)  22.6 us
    all_to_all x1, blocking collectives, local(): lax.all_to_all(tile, 'tensor', 0, 0, tiled=True).sum(0)[:seqs * queries]  18.3 us
    all_to_all x1, blocking collectives, local(): a_parts = lax.all_to_all(a_part, 'tensor', 0, 0, axis_index_groups=XG)  13.4 us
    all_to_all x1, starting transfers between devices, local(): pieces = lax.all_to_all(pieces, 'dp', 0, 0, axis_index_groups=ZG)  9.96 us
    pallas_call x1, Pallas kernels, score_tiles(): pl.pallas_call(score_kernel, grid=(queries,), out_shape=jax.ShapeDtypeStr...  7.15 us
    all_to_all x1, starting transfers between devices, local(): at = lax.all_to_all(at, 'tensor', 0, 0, axis_index_groups=YG)  7.11 us
  transfers between devices with their start and end apart: 13, of which 6 were waited for; matrix products, arithmetic and copies ran while one was open for 9% of the time, Pallas kernels for 1%

profile of v4, /device:TPU:64, one launch (start us, length us, event | category | flops | bytes accessed | tf_op | source)
XLA Modules:
  0.0 176.2 jit_solution(995919933219482773)
XLA Ops:
  7.9 1.7 pad_maximum_fusion.1
  11.5 10.0 %all-to-all-start = ((bf16[8,176,128]{2,1,0:T(8,128)(2,1)}), bf16[8,176,128]{2,1,0:T(8,128)(2,1)S(1)}, u32[]{:S(2)}, u32[]{:S(2)}) async-start(bf16[8,176,128]{2,1,0:T(8,128)(2,1)} %bitcast.9), calls=%async_computation | async-start | bytes 720896 | tf_op jit(solution)/shard_map/all_to_all | solution.py:118
  22.8 3.4 %collective-permute-start = (bf16[172,1408]{1,0:T(8,128)(2,1)S(1)}, bf16[172,1408]{1,0:T(8,128)(2,1)S(1)}, u32[]{:S(2)}, u32[]{:S(2)}) collective-permute-start(bf16[172,1408]{1,0:T(8,128)(2,1)S(1)} %get-tuple-element.10), channel_id=1, source_target_pairs={{0,8},{1,9},{2,10},{3,11},{4,12},{5,13},{6,14},{7,15},{8,16},{9,17... | collective-permute-start | bytes 1453064 | tf_op jit(solution)/shard_map/ppermute | solution.py:18
  26.2 4.6 %collective-permute-start.2 = (bf16[172,1408]{1,0:T(8,128)(2,1)S(1)}, bf16[172,1408]{1,0:T(8,128)(2,1)S(1)}, u32[]{:S(2)}, u32[]{:S(2)}) collective-permute-start(bf16[172,1408]{1,0:T(8,128)(2,1)S(1)} %get-tuple-element.11), channel_id=1, source_target_pairs={{0,16},{1,17},{2,18},{3,19},{4,20},{5,21},{6,22},{7,23},{8,24},{9,... | collective-permute-start | bytes 1453064 | tf_op jit(solution)/shard_map/ppermute | solution.py:18
  30.8 3.3 %collective-permute-start.4 = (bf16[172,1408]{1,0:T(8,128)(2,1)S(1)}, bf16[172,1408]{1,0:T(8,128)(2,1)S(1)}, u32[]{:S(2)}, u32[]{:S(2)}) collective-permute-start(bf16[172,1408]{1,0:T(8,128)(2,1)S(1)} %get-tuple-element.12), channel_id=1, source_target_pairs={{0,24},{1,25},{2,26},{3,27},{4,28},{5,29},{6,30},{7,31},{8,0},{9,1... | collective-permute-start | bytes 1453064 | tf_op jit(solution)/shard_map/ppermute | solution.py:18
  35.4 3.7 %collective-permute-done = bf16[172,1408]{1,0:T(8,128)(2,1)S(1)} collective-permute-done((bf16[172,1408]{1,0:T(8,128)(2,1)S(1)}, bf16[172,1408]{1,0:T(8,128)(2,1)S(1)}, u32[]{:S(2)}, u32[]{:S(2)}) %collective-permute-start) | collective-permute-done | bytes 484384 | tf_op jit(solution)/shard_map/ppermute | solution.py:18
  39.8 10.2 %collective-permute-done.2 = bf16[172,1408]{1,0:T(8,128)(2,1)S(1)} collective-permute-done((bf16[172,1408]{1,0:T(8,128)(2,1)S(1)}, bf16[172,1408]{1,0:T(8,128)(2,1)S(1)}, u32[]{:S(2)}, u32[]{:S(2)}) %collective-permute-start.2) | collective-permute-done | bytes 484384 | tf_op jit(solution)/shard_map/ppermute | solution.py:18
  56.2 22.6 %all_to_all.29 = bf16[4,1376,128]{2,1,0:T(8,128)(2,1)S(1)} all-to-all(bf16[4,1376,128]{2,1,0:T(8,128)(2,1)S(1)} %dynamic_update_slice.3), channel_id=1, replica_groups={{0,8,16,24},{1,9,17,25},{2,10,18,26},{3,11,19,27},{4,12,20,28},{5,13,21..., dimensions={0} | all-to-all | bytes 2818048 | tf_op jit(solution)/shard_map/all_to_all | solution.py:123
  79.7 2.5 %bitcast_convert_fusion = bf16[4,128,768]{2,1,0:T(8,128)(2,1)S(1)} fusion(bf16[4,8,128,128]{3,2,1,0:T(8,128)(2,1)S(1)} %bitcast.70, bf16[8,1824,128]{2,1,0:T(8,128)(2,1)} %bitcast.67), kind=kOutput, calls=%fused_computation.10 | convolution fusion | flops 805699584 | bytes 3407872 | tf_op jit(solution)/shard_map/xyed,yte->xdt/dot_general | solution.py:128
  82.1 13.4 %all_to_all.30 = bf16[4,128,768]{2,1,0:T(8,128)(2,1)S(1)} all-to-all(bf16[4,128,768]{2,1,0:T(8,128)(2,1)S(1)} %bitcast_convert_fusion), channel_id=1, replica_groups={{0,8,16,24},{1,9,17,25},{2,10,18,26},{3,11,19,27},{4,12,20,28},{5,13,21..., dimensions={0} | all-to-all | bytes 1572864 | tf_op jit(solution)/shard_map/all_to_all | solution.py:129
  96.9 7.1 %all-to-all-start.3 = ((bf16[8,128,768]{2,1,0:T(8,128)(2,1)}), bf16[8,128,768]{2,1,0:T(8,128)(2,1)S(1)}, u32[]{:S(2)}, u32[]{:S(2)}) async-start(bf16[8,128,768]{2,1,0:T(8,128)(2,1)} %broadcast_in_dim.9), calls=%async_computation.3 | async-start | bytes 3145728 | tf_op jit(solution)/shard_map/all_to_all | solution.py:131
  104.0 1.8 %slice.68 = bf16[8,1056,128]{2,1,0:T(8,128)(2,1)S(1)} slice(bf16[8,1824,128]{2,1,0:T(8,128)(2,1)} %bitcast.68), slice={[0:8], [768:1824], [0:128]} | slice | bytes 4325376 | tf_op jit(solution)/shard_map/slice | solution.py:111
  107.5 3.2 %collective-permute-start.1 = (bf16[172,768]{1,0:T(8,128)(2,1)S(1)}, bf16[172,768]{1,0:T(8,128)(2,1)S(1)}, u32[]{:S(2)}, u32[]{:S(2)}) collective-permute-start(bf16[172,768]{1,0:T(8,128)(2,1)S(1)} %fusion.15), channel_id=1, source_target_pairs={{0,24},{1,25},{2,26},{3,27},{4,28},{5,29},{6,30},{7,31},{8,0},{9,1... | collective-permute-start | bytes 792584 | tf_op jit(solution)/shard_map/ppermute | solution.py:18
  111.3 3.5 %collective-permute-start.3 = (bf16[172,768]{1,0:T(8,128)(2,1)S(1)}, bf16[172,768]{1,0:T(8,128)(2,1)S(1)}, u32[]{:S(2)}, u32[]{:S(2)}) collective-permute-start(bf16[172,768]{1,0:T(8,128)(2,1)S(1)} %fusion.18), channel_id=1, source_target_pairs={{0,16},{1,17},{2,18},{3,19},{4,20},{5,21},{6,22},{7,23},{8,24},{9,... | collective-permute-start | bytes 792584 | tf_op jit(solution)/shard_map/ppermute | solution.py:18
  115.4 1.9 %collective-permute-start.5 = (bf16[172,768]{1,0:T(8,128)(2,1)S(1)}, bf16[172,768]{1,0:T(8,128)(2,1)S(1)}, u32[]{:S(2)}, u32[]{:S(2)}) collective-permute-start(bf16[172,768]{1,0:T(8,128)(2,1)S(1)} %fusion.21), channel_id=1, source_target_pairs={{0,8},{1,9},{2,10},{3,11},{4,12},{5,13},{6,14},{7,15},{8,16},{9,17... | collective-permute-start | bytes 792584 | tf_op jit(solution)/shard_map/ppermute | solution.py:18
  117.9 5.7 %collective-permute-done.3 = bf16[172,768]{1,0:T(8,128)(2,1)S(1)} collective-permute-done((bf16[172,768]{1,0:T(8,128)(2,1)S(1)}, bf16[172,768]{1,0:T(8,128)(2,1)S(1)}, u32[]{:S(2)}, u32[]{:S(2)}) %collective-permute-start.3) | collective-permute-done | bytes 264224 | tf_op jit(solution)/shard_map/ppermute | solution.py:18
  123.6 2.6 %collective-permute-done.5 = bf16[172,768]{1,0:T(8,128)(2,1)S(1)} collective-permute-done((bf16[172,768]{1,0:T(8,128)(2,1)S(1)}, bf16[172,768]{1,0:T(8,128)(2,1)S(1)}, u32[]{:S(2)}, u32[]{:S(2)}) %collective-permute-start.5) | collective-permute-done | bytes 264224 | tf_op jit(solution)/shard_map/ppermute | solution.py:18
  126.3 1.9 %collective-permute-start.6 = (bf16[176,768]{1,0:T(8,128)(2,1)S(1)}, bf16[176,768]{1,0:T(8,128)(2,1)S(1)}, u32[]{:S(2)}, u32[]{:S(2)}) collective-permute-start(bf16[176,768]{1,0:T(8,128)(2,1)S(1)} %pad.13.g0_ref), channel_id=1, source_target_pairs={{0,8},{1,9},{2,10},{3,11},{4,12},{5,13},{6,14},{7,15},{8,16},{9,17... | collective-permute-start | bytes 811016 | tf_op jit(solution)/shard_map/ppermute | solution.py:18
  128.3 4.2 %collective-permute-start.7 = (bf16[176,768]{1,0:T(8,128)(2,1)S(1)}, bf16[176,768]{1,0:T(8,128)(2,1)S(1)}, u32[]{:S(2)}, u32[]{:S(2)}) collective-permute-start(bf16[176,768]{1,0:T(8,128)(2,1)S(1)} %pad.13.g0_ref), channel_id=1, source_target_pairs={{0,16},{1,17},{2,18},{3,19},{4,20},{5,21},{6,22},{7,23},{8,24},{9,... | collective-permute-start | bytes 811016 | tf_op jit(solution)/shard_map/ppermute | solution.py:18
  132.5 3.2 %collective-permute-start.8 = (bf16[176,768]{1,0:T(8,128)(2,1)S(1)}, bf16[176,768]{1,0:T(8,128)(2,1)S(1)}, u32[]{:S(2)}, u32[]{:S(2)}) collective-permute-start(bf16[176,768]{1,0:T(8,128)(2,1)S(1)} %pad.13.g0_ref), channel_id=1, source_target_pairs={{0,24},{1,25},{2,26},{3,27},{4,28},{5,29},{6,30},{7,31},{8,0},{9,1... | collective-permute-start | bytes 811016 | tf_op jit(solution)/shard_map/ppermute | solution.py:18
  135.7 4.8 %collective-permute-done.6.g1_ref = bf16[176,768]{1,0:T(8,128)(2,1)S(1)} collective-permute-done((bf16[176,768]{1,0:T(8,128)(2,1)S(1)}, bf16[176,768]{1,0:T(8,128)(2,1)S(1)}, u32[]{:S(2)}, u32[]{:S(2)}) %collective-permute-start.6) | collective-permute-done | bytes 270368 | tf_op jit(solution)/shard_map/ppermute | solution.py:18
  140.5 2.5 %collective-permute-done.8.g3_ref = bf16[176,768]{1,0:T(8,128)(2,1)S(1)} collective-permute-done((bf16[176,768]{1,0:T(8,128)(2,1)S(1)}, bf16[176,768]{1,0:T(8,128)(2,1)S(1)}, u32[]{:S(2)}, u32[]{:S(2)}) %collective-permute-start.8) | collective-permute-done | bytes 270368 | tf_op jit(solution)/shard_map/ppermute | solution.py:18
  143.0 7.2 %shard_map.83 = f32[32,128]{1,0:T(8,128)S(1)} custom-call(s32[1]{0:T(128)} %bitcast.kx_ref, bf16[176,768]{1,0:T(8,128)(2,1)S(1)} %pad.13.g0_ref, bf16[176,768]{1,0:T(8,128)(2,1)S(1)} %collective-permute-done.6.g1_ref, bf16[176,768]{1,0:T(8,128)(2,1)S(1)} %collective-permute-done.7.g2_ref, bf16[176,768]{1,0:T(8,128)(2,1)S(1)} %collective-permute-done.8.g3_ref, ...), custom_call_target="tpu_custom_call" | custom-call | flops 4429185024 | bytes 9000000 | tf_op jit(solution)/shard_map/pallas_call | solution.py:80
  150.2 18.3 %all_to_all.31 = f32[32,1,128]{2,1,0:T(1,128)S(1)} all-to-all(f32[32,1,128]{2,1,0:T(1,128)S(1)} %bitcast.58), channel_id=1, replica_groups=mesh['dp'=16,'tensor'=32] {'tensor'}, dimensions={0} | all-to-all | bytes 32768 | tf_op jit(solution)/shard_map/all_to_all | solution.py:143
  (63 shorter events, 15.7 us)
Async XLA Ops:
  6.5 4.0 %copy-start.3 = (f32[172,256]{1,0:T(8,128)S(1)}, f32[172,256]{1,0:T(8,128)}, u32[]{:S(2)}) copy-start(f32[172,256]{1,0:T(8,128)} %param.13) | copy-start | bytes 528388
  6.5 4.0 %copy-start.2 = (bf16[4,172,256]{2,0,1:T(4,128)(2,1)S(1)}, bf16[4,172,256]{2,0,1:T(4,128)(2,1)}, u32[]{:S(2)}) copy-start(bf16[4,172,256]{2,0,1:T(4,128)(2,1)} %param.12) | copy-start | bytes 1056772
  6.5 73.1 %all-gather.6.cloned.1.call-start = ((), (), s32[]{:S(2)}) async-start(), calls=%async_computation.6 | async-start | bytes 4202496 | tf_op jit(solution)/shard_map/all_gather | solution.py:109
  9.7 11.8 %copy-start = (bf16[172,5504]{1,0:T(8,128)(2,1)S(1)}, bf16[172,5504]{1,0:T(8,128)(2,1)}, u32[]{:S(2)}) copy-start(bf16[172,5504]{1,0:T(8,128)(2,1)} %v_ref.1) | copy-start | bytes 5680132
  11.5 42.4 %all-to-all-start = ((bf16[8,176,128]{2,1,0:T(8,128)(2,1)}), bf16[8,176,128]{2,1,0:T(8,128)(2,1)S(1)}, u32[]{:S(2)}, u32[]{:S(2)}) async-start(bf16[8,176,128]{2,1,0:T(8,128)(2,1)} %bitcast.9), calls=%async_computation | async-start | bytes 720896 | tf_op jit(solution)/shard_map/all_to_all | solution.py:118
  21.5 121.6 %all-gather.4.cloned.1.call-start = ((), (), s32[]{:S(2)}) async-start(), calls=%async_computation.5 | async-start | bytes 6127616 | tf_op jit(solution)/shard_map/all_gather | solution.py:126
  22.8 16.4 %collective-permute-start = (bf16[172,1408]{1,0:T(8,128)(2,1)S(1)}, bf16[172,1408]{1,0:T(8,128)(2,1)S(1)}, u32[]{:S(2)}, u32[]{:S(2)}) collective-permute-start(bf16[172,1408]{1,0:T(8,128)(2,1)S(1)} %get-tuple-element.10), channel_id=1, source_target_pairs={{0,8},{1,9},{2,10},{3,11},{4,12},{5,13},{6,14},{7,15},{8,16},{9,17... | collective-permute-start | bytes 1453064 | tf_op jit(solution)/shard_map/ppermute | solution.py:18
  26.2 23.8 %collective-permute-start.2 = (bf16[172,1408]{1,0:T(8,128)(2,1)S(1)}, bf16[172,1408]{1,0:T(8,128)(2,1)S(1)}, u32[]{:S(2)}, u32[]{:S(2)}) collective-permute-start(bf16[172,1408]{1,0:T(8,128)(2,1)S(1)} %get-tuple-element.11), channel_id=1, source_target_pairs={{0,16},{1,17},{2,18},{3,19},{4,20},{5,21},{6,22},{7,23},{8,24},{9,... | collective-permute-start | bytes 1453064 | tf_op jit(solution)/shard_map/ppermute | solution.py:18
  30.8 21.1 %collective-permute-start.4 = (bf16[172,1408]{1,0:T(8,128)(2,1)S(1)}, bf16[172,1408]{1,0:T(8,128)(2,1)S(1)}, u32[]{:S(2)}, u32[]{:S(2)}) collective-permute-start(bf16[172,1408]{1,0:T(8,128)(2,1)S(1)} %get-tuple-element.12), channel_id=1, source_target_pairs={{0,24},{1,25},{2,26},{3,27},{4,28},{5,29},{6,30},{7,31},{8,0},{9,1... | collective-permute-start | bytes 1453064 | tf_op jit(solution)/shard_map/ppermute | solution.py:18
  39.1 14.1 %copy-start.9 = (bf16[172,1408]{1,0:T(8,128)(2,1)}, bf16[172,1408]{1,0:T(8,128)(2,1)S(1)}, u32[]{:S(2)}) copy-start(bf16[172,1408]{1,0:T(8,128)(2,1)S(1)} %collective-permute-done) | copy-start | bytes 1453060
  50.0 3.3 %copy-start.7 = (bf16[172,1408]{1,0:T(8,128)(2,1)}, bf16[172,1408]{1,0:T(8,128)(2,1)S(1)}, u32[]{:S(2)}) copy-start(bf16[172,1408]{1,0:T(8,128)(2,1)S(1)} %collective-permute-done.2) | copy-start | bytes 1453060
  51.9 1.4 copy-start.5
  53.9 0.8 copy-start.1
  95.6 8.4 %copy-start.4 = (s32[6]{0:T(128)S(1)}, s32[6]{0:T(128)}, u32[]{:S(2)}) copy-start(s32[6]{0:T(128)} %param.15) | copy-start | bytes 76
  96.9 46.2 %all-to-all-start.3 = ((bf16[8,128,768]{2,1,0:T(8,128)(2,1)}), bf16[8,128,768]{2,1,0:T(8,128)(2,1)S(1)}, u32[]{:S(2)}, u32[]{:S(2)}) async-start(bf16[8,128,768]{2,1,0:T(8,128)(2,1)} %broadcast_in_dim.9), calls=%async_computation.3 | async-start | bytes 3145728 | tf_op jit(solution)/shard_map/all_to_all | solution.py:131
  105.9 1.0 copy-start.10
  106.6 4.1 %copy-start.8 = (bf16[172,1408]{1,0:T(8,128)(2,1)S(1)}, bf16[172,1408]{1,0:T(8,128)(2,1)}, u32[]{:S(2)}) copy-start(bf16[172,1408]{1,0:T(8,128)(2,1)} %copy-done.7) | copy-start | bytes 1453060
  107.5 7.3 %copy-start.6 = (bf16[172,1408]{1,0:T(8,128)(2,1)S(1)}, bf16[172,1408]{1,0:T(8,128)(2,1)}, u32[]{:S(2)}) copy-start(bf16[172,1408]{1,0:T(8,128)(2,1)} %copy-done.5) | copy-start | bytes 1453060
  107.5 10.4 %collective-permute-start.1 = (bf16[172,768]{1,0:T(8,128)(2,1)S(1)}, bf16[172,768]{1,0:T(8,128)(2,1)S(1)}, u32[]{:S(2)}, u32[]{:S(2)}) collective-permute-start(bf16[172,768]{1,0:T(8,128)(2,1)S(1)} %fusion.15), channel_id=1, source_target_pairs={{0,24},{1,25},{2,26},{3,27},{4,28},{5,29},{6,30},{7,31},{8,0},{9,1... | collective-permute-start | bytes 792584 | tf_op jit(solution)/shard_map/ppermute | solution.py:18
  111.3 12.3 %collective-permute-start.3 = (bf16[172,768]{1,0:T(8,128)(2,1)S(1)}, bf16[172,768]{1,0:T(8,128)(2,1)S(1)}, u32[]{:S(2)}, u32[]{:S(2)}) collective-permute-start(bf16[172,768]{1,0:T(8,128)(2,1)S(1)} %fusion.18), channel_id=1, source_target_pairs={{0,16},{1,17},{2,18},{3,19},{4,20},{5,21},{6,22},{7,23},{8,24},{9,... | collective-permute-start | bytes 792584 | tf_op jit(solution)/shard_map/ppermute | solution.py:18
  115.4 10.8 %collective-permute-start.5 = (bf16[172,768]{1,0:T(8,128)(2,1)S(1)}, bf16[172,768]{1,0:T(8,128)(2,1)S(1)}, u32[]{:S(2)}, u32[]{:S(2)}) collective-permute-start(bf16[172,768]{1,0:T(8,128)(2,1)S(1)} %fusion.21), channel_id=1, source_target_pairs={{0,8},{1,9},{2,10},{3,11},{4,12},{5,13},{6,14},{7,15},{8,16},{9,17... | collective-permute-start | bytes 792584 | tf_op jit(solution)/shard_map/ppermute | solution.py:18
  126.3 14.2 %collective-permute-start.6 = (bf16[176,768]{1,0:T(8,128)(2,1)S(1)}, bf16[176,768]{1,0:T(8,128)(2,1)S(1)}, u32[]{:S(2)}, u32[]{:S(2)}) collective-permute-start(bf16[176,768]{1,0:T(8,128)(2,1)S(1)} %pad.13.g0_ref), channel_id=1, source_target_pairs={{0,8},{1,9},{2,10},{3,11},{4,12},{5,13},{6,14},{7,15},{8,16},{9,17... | collective-permute-start | bytes 811016 | tf_op jit(solution)/shard_map/ppermute | solution.py:18
  128.3 12.2 %collective-permute-start.7 = (bf16[176,768]{1,0:T(8,128)(2,1)S(1)}, bf16[176,768]{1,0:T(8,128)(2,1)S(1)}, u32[]{:S(2)}, u32[]{:S(2)}) collective-permute-start(bf16[176,768]{1,0:T(8,128)(2,1)S(1)} %pad.13.g0_ref), channel_id=1, source_target_pairs={{0,16},{1,17},{2,18},{3,19},{4,20},{5,21},{6,22},{7,23},{8,24},{9,... | collective-permute-start | bytes 811016 | tf_op jit(solution)/shard_map/ppermute | solution.py:18
  132.5 10.6 %collective-permute-start.8 = (bf16[176,768]{1,0:T(8,128)(2,1)S(1)}, bf16[176,768]{1,0:T(8,128)(2,1)S(1)}, u32[]{:S(2)}, u32[]{:S(2)}) collective-permute-start(bf16[176,768]{1,0:T(8,128)(2,1)S(1)} %pad.13.g0_ref), channel_id=1, source_target_pairs={{0,24},{1,25},{2,26},{3,27},{4,28},{5,29},{6,30},{7,31},{8,0},{9,1... | collective-permute-start | bytes 811016 | tf_op jit(solution)/shard_map/ppermute | solution.py:18
Sparse Core Ops, SparseCore 0:
  9.8 56.7 all-gather.5
  79.7 47.0 all-gather.3

commit v5 on v4

--- a/solution.py
+++ b/solution.py
@@ -16,6 +16,27 @@
 def shift_x(array, by):
     perm = [(x * NY + y, (x + by) % NX * NY + y) for x in range(NX) for y in range(NY)]
     return lax.ppermute(array, "tensor", perm)
+
+
+def pack_kernel(x_ref, y_ref, o_ref):
+    tokens = x_ref.shape[0]
+    width = y_ref.shape[0]
+    o_ref[:tokens] = x_ref[...]
+    for s in range(y_ref.shape[1] // SEQ):
+        block = y_ref[:, s * SEQ : (s + 1) * SEQ]
+        first = tokens + s * PAD
+        o_ref[first : first + PAD] = jnp.concatenate([block, jnp.zeros((PAD - width, SEQ), block.dtype)], axis=0)
+
+
+def packed(x, y):
+    vmem = pl.BlockSpec(memory_space=pltpu.VMEM)
+    return pl.pallas_call(
+        pack_kernel,
+        out_shape=jax.ShapeDtypeStruct((x.shape[0] + y.shape[1] // SEQ * PAD, SEQ), x.dtype),
+        in_specs=[vmem] * 2,
+        out_specs=vmem,
+        cost_estimate=pl.CostEstimate(flops=0, bytes_accessed=1_000_000, transcendentals=0),
+    )(x, y)
 
 
 def columns_kernel(kx_ref, v_ref, o0_ref, o1_ref, o2_ref, o3_ref, all_ref):
@@ -49,16 +70,19 @@
     )(kx, v)
 
 
-def score_kernel(kx_ref, g0_ref, g1_ref, g2_ref, g3_ref, a_ref, s_ref, o_ref):
+def score_kernel(kx_ref, g0_ref, g1_ref, g2_ref, g3_ref, a_ref, s_ref, o_ref, lhs_ref):
     q = pl.program_id(0)
     queries = pl.num_programs(0)
     tokens = g0_ref.shape[1]
+    for d in range(NX):
+        fx = (kx_ref[0] - d) & (NX - 1)
+        for y in range(NY):
+            lhs_ref[d * PAD : (d + 1) * PAD, y * 128 : (y + 1) * 128] = s_ref[y % 2, y // 2 % 2, fx, y // 4]
+    t = jnp.dot(lhs_ref[...], a_ref[...], preferred_element_type=jnp.float32)
     acc = jnp.zeros((8, tokens), jnp.float32)
     for d, g_ref in enumerate((g0_ref, g1_ref, g2_ref, g3_ref)):
-        fx = (kx_ref[0] - d) & (NX - 1)
-        tiles = [s_ref[half, core, fx, high] for high in range(2) for core in range(2) for half in range(2)]
-        t = jnp.dot(jnp.concatenate(tiles, axis=1), a_ref[...], preferred_element_type=jnp.float32)
-        acc += (t * g_ref[...].astype(jnp.float32)).reshape(PAD // 8, 8, tokens).sum(0)
+        part = t[d * PAD : (d + 1) * PAD] * g_ref[...].astype(jnp.float32)
+        acc += part.reshape(PAD // 8, 8, tokens).sum(0)
     per_token = jnp.sum(acc, axis=0, keepdims=True)
     lane = lax.broadcasted_iota(jnp.int32, o_ref.shape, 1)
 
@@ -85,6 +109,7 @@
         + [pl.BlockSpec((PAD, tokens), whole)] * NX
         + [pl.BlockSpec(at.shape, whole), pl.BlockSpec((2,) + tiles.shape[1:], lambda q: (q, 0, 0, 0, 0, 0))],
         out_specs=pl.BlockSpec((NX * NY, 128), whole),
+        scratch_shapes=[pltpu.VMEM((NX * PAD, NY * 128), jnp.bfloat16)],
         compiler_params=pltpu.CompilerParams(vmem_limit_bytes=48 * 1024 * 1024),
         cost_estimate=pl.CostEstimate(
             flops=2 * NX * queries * PAD * NY * 128 * tokens, bytes_accessed=9_000_000, transcendentals=0
@@ -97,6 +122,12 @@
     return (wide[0] + wide[1]) + (wide[2] + wide[3])
 
 
+def after(array, zero):
+    first = (0,) * array.ndim
+    corner = lax.slice(array, first, (1,) * array.ndim)
+    return lax.dynamic_update_slice(array, corner + zero.reshape(corner.shape), first)
+
+
 def local(activations, out_grads_t, in_basis, out_basis_t, query_proj, eigvals, damping, lengths):
     bf, f32 = jnp.bfloat16, jnp.float32
     tokens, width = activations.shape[0], out_grads_t.shape[0]
@@ -104,8 +135,7 @@
     seq_len = tokens // seqs
     kx = lax.shift_right_logical(lax.axis_index("tensor"), 3)
 
-    grads = jnp.pad(out_grads_t.reshape(width, seqs, seq_len).transpose(1, 0, 2), ((0, 0), (0, PAD - width), (0, 0)))
-    both = jnp.concatenate([activations, grads.reshape(seqs * PAD, seq_len)], axis=0)
+    both = packed(activations, out_grads_t)
     both = lax.all_gather(both, "tensor", axis_index_groups=YG)
     x8 = both[:, :tokens]
     y8 = both[:, tokens:].reshape(NY, seqs, PAD, seq_len)
@@ -118,21 +148,24 @@
     pieces = lax.all_to_all(pieces, "dp", 0, 0, axis_index_groups=ZG)
     rows = NY * 128
     mixed = jnp.concatenate([in_basis.reshape(NX, rows, 128), pieces.reshape(NX, 2 * PAD, 128)], axis=1)
-    tie = (vs[1][:1, :1] + vs[2][:1, :1] + vs[3][:1, :1]) * 0
-    mixed = lax.dynamic_update_slice(mixed, mixed[:1, :1, :1] + tie[None], (0, 0, 0))
     mixed = lax.all_to_all(mixed, "tensor", 0, 0, axis_index_groups=XG)
     u4 = mixed[:, :rows]
-    pieces = mixed[:, rows:].reshape(NX, 2, PAD, 128)
+    tie = (vs[1][:1, :1] + vs[2][:1, :1] + vs[3][:1, :1]) * 0
+    pieces = after(mixed[:, rows:].reshape(NX, 2, PAD, 128), tie)
     tiles = lax.all_gather(pieces, "dp").reshape(NZ, 2, NX, 2, PAD, 128)
 
     a_part = jnp.einsum("xyed,yte->xdt", u4.reshape(NX, NY, 128, 128), x8, preferred_element_type=f32).astype(bf)
     a_parts = lax.all_to_all(a_part, "tensor", 0, 0, axis_index_groups=XG)
-    at = jnp.broadcast_to(add_parts(a_parts).astype(bf), (NY, 128, tokens))
-    at = lax.all_to_all(at, "tensor", 0, 0, axis_index_groups=YG)
 
     y8 = y8.transpose(0, 2, 1, 3).reshape(NY * PAD, tokens)
     g_parts = [jnp.dot(v, y8, preferred_element_type=f32).astype(bf) for v in vs]
+    tie = (g_parts[0][:1, :1] + g_parts[1][:1, :1] + g_parts[2][:1, :1] + g_parts[3][:1, :1]) * 0
     g_parts = [g_parts[0]] + [shift_x(g_parts[d], -d) for d in range(1, NX)]
+
+    at = after(add_parts(a_parts).astype(bf), tie)
+    at = jnp.broadcast_to(at, (NY, 128, tokens))
+    at = lax.all_to_all(at, "tensor", 0, 0, axis_index_groups=YG)
+
     position = lax.broadcasted_iota(jnp.int32, (seqs, seq_len), 1)
     keep = (position < lengths[:, None]).astype(f32).reshape(1, tokens)
     g = (add_parts(g_parts) * keep).astype(bf)

time: 177 us -> 183 us (1.034)
  the two profiles are of different devices: /device:TPU:64 before, /device:TPU:1 now
where the time goes in v5:
time: 183 us; the launch traced here: 180 us
  waiting for transfers between devices  47.7 us (26%)
  starting transfers between devices  41.1 us (22%)
  blocking collectives  36.9 us (20%)
  between operations  20.2 us (11%)
  local copies, waits for them, and re-layouts  13.9 us (8%)
  Pallas kernels  10.4 us (6%)
  matrix products  5.73 us (3%)
  other arithmetic  3.61 us (2%)
    ppermute x9, waiting for transfers between devices, shift_x(): return lax.ppermute(array, 'tensor', perm)  40.9 us
    ppermute x9, starting transfers between devices, shift_x(): return lax.ppermute(array, 'tensor', perm)  26.4 us
    all_to_all x1, blocking collectives, local(): pieces = lax.all_to_all(pieces, 'dp', 0, 0, axis_index_groups=ZG)  23.6 us
    all_to_all x1, blocking collectives, local(): lax.all_to_all(tile, 'tensor', 0, 0, tiled=True).sum(0)[:seqs * queries]  13.3 us
    pallas_call x1, Pallas kernels, score_tiles(): pl.pallas_call(score_kernel, grid=(queries,), out_shape=jax.ShapeDtypeStr...  7.16 us
    all_to_all x1, starting transfers between devices, local(): at = lax.all_to_all(at, 'tensor', 0, 0, axis_index_groups=YG)  6.8 us
    all_to_all x1, waiting for transfers between devices, local(): at = lax.all_to_all(at, 'tensor', 0, 0, axis_index_groups=YG)  5.81 us
    all_to_all x1, starting transfers between devices, local(): mixed = lax.all_to_all(mixed, 'tensor', 0, 0, axis_index_groups=XG)  4.32 us
  transfers between devices with their start and end apart: 14, of which 9 were waited for; matrix products, arithmetic and copies ran while one was open for 12% of the time, Pallas kernels for 1%

profile of v5, /device:TPU:1, one launch (start us, length us, event | category | flops | bytes accessed | tf_op | source)
XLA Modules:
  0.0 179.6 jit_solution(12497585525943799343)
XLA Ops:
  11.3 23.6 %all_to_all.29 = bf16[8,176,128]{2,1,0:T(8,128)(2,1)S(1)} all-to-all(bf16[8,176,128]{2,1,0:T(8,128)(2,1)S(1)} %bitcast.64), channel_id=1, replica_groups={{0,64,128,192,256,320,384,448},{32,96,160,224,288,352,416,480},{1,65,12..., dimensions={0} | all-to-all | bytes 720896 | tf_op jit(solution)/shard_map/all_to_all | solution.py:148
  36.1 4.3 %all-to-all-start.1 = ((bf16[4,1376,128]{2,1,0:T(8,128)(2,1)}), bf16[4,1376,128]{2,1,0:T(8,128)(2,1)}, u32[]{:S(2)}, u32[]{:S(2)}) async-start(bf16[4,1376,128]{2,1,0:T(8,128)(2,1)} %pad_maximum_fusion), calls=%async_computation.1 | async-start | bytes 2818048 | tf_op jit(solution)/shard_map/all_to_all | solution.py:151
  41.8 3.3 %collective-permute-start = (bf16[172,1408]{1,0:T(8,128)(2,1)S(1)}, bf16[172,1408]{1,0:T(8,128)(2,1)S(1)}, u32[]{:S(2)}, u32[]{:S(2)}) collective-permute-start(bf16[172,1408]{1,0:T(8,128)(2,1)S(1)} %get-tuple-element.10), channel_id=1, source_target_pairs={{0,8},{1,9},{2,10},{3,11},{4,12},{5,13},{6,14},{7,15},{8,16},{9,17... | collective-permute-start | bytes 1453064 | tf_op jit(solution)/shard_map/ppermute | solution.py:18
  45.1 4.3 %collective-permute-start.2 = (bf16[172,1408]{1,0:T(8,128)(2,1)S(1)}, bf16[172,1408]{1,0:T(8,128)(2,1)S(1)}, u32[]{:S(2)}, u32[]{:S(2)}) collective-permute-start(bf16[172,1408]{1,0:T(8,128)(2,1)S(1)} %get-tuple-element.11), channel_id=1, source_target_pairs={{0,16},{1,17},{2,18},{3,19},{4,20},{5,21},{6,22},{7,23},{8,24},{9,... | collective-permute-start | bytes 1453064 | tf_op jit(solution)/shard_map/ppermute | solution.py:18
  49.4 3.1 %collective-permute-start.4 = (bf16[172,1408]{1,0:T(8,128)(2,1)S(1)}, bf16[172,1408]{1,0:T(8,128)(2,1)S(1)}, u32[]{:S(2)}, u32[]{:S(2)}) collective-permute-start(bf16[172,1408]{1,0:T(8,128)(2,1)S(1)} %get-tuple-element.12), channel_id=1, source_target_pairs={{0,24},{1,25},{2,26},{3,27},{4,28},{5,29},{6,30},{7,31},{8,0},{9,1... | collective-permute-start | bytes 1453064 | tf_op jit(solution)/shard_map/ppermute | solution.py:18
  52.5 15.2 %collective-permute-done = bf16[172,1408]{1,0:T(8,128)(2,1)S(1)} collective-permute-done((bf16[172,1408]{1,0:T(8,128)(2,1)S(1)}, bf16[172,1408]{1,0:T(8,128)(2,1)S(1)}, u32[]{:S(2)}, u32[]{:S(2)}) %collective-permute-start) | collective-permute-done | bytes 484384 | tf_op jit(solution)/shard_map/ppermute | solution.py:18
  68.3 10.3 %collective-permute-done.2 = bf16[172,1408]{1,0:T(8,128)(2,1)S(1)} collective-permute-done((bf16[172,1408]{1,0:T(8,128)(2,1)S(1)}, bf16[172,1408]{1,0:T(8,128)(2,1)S(1)}, u32[]{:S(2)}, u32[]{:S(2)}) %collective-permute-start.2) | collective-permute-done | bytes 484384 | tf_op jit(solution)/shard_map/ppermute | solution.py:18
  84.9 2.3 %slice.89 = bf16[4,1024,128]{2,1,0:T(8,128)(2,1)} slice(bf16[4,1376,128]{2,1,0:T(8,128)(2,1)} %all-to-all-done.1), slice={[0:4], [0:1024], [0:128]} | slice | bytes 2097152 | tf_op jit(solution)/shard_map/slice | solution.py:152
  89.0 3.3 %bitcast_convert_fusion = bf16[4,128,768]{2,1,0:T(8,128)(2,1)} fusion(bf16[4,8,128,128]{3,2,1,0:T(8,128)(2,1)S(1)} %bitcast.68, bf16[8,1824,128]{2,1,0:T(8,128)(2,1)} %bitcast.67), kind=kOutput, calls=%fused_computation.10 | convolution fusion | flops 805699584 | bytes 3407872 | tf_op jit(solution)/shard_map/xyed,yte->xdt/dot_general | solution.py:157
  92.4 3.5 %all-to-all-start.2 = ((bf16[4,128,768]{2,1,0:T(8,128)(2,1)}), bf16[4,128,768]{2,1,0:T(8,128)(2,1)S(1)}, u32[]{:S(2)}, u32[]{:S(2)}) async-start(bf16[4,128,768]{2,1,0:T(8,128)(2,1)} %bitcast_convert_fusion), calls=%async_computation.2 | async-start | bytes 1572864 | tf_op jit(solution)/shard_map/all_to_all | solution.py:158
  107.4 6.8 %all-to-all-start.3 = ((bf16[8,128,768]{2,1,0:T(8,128)(2,1)}), bf16[8,128,768]{2,1,0:T(8,128)(2,1)S(1)}, u32[]{:S(2)}, u32[]{:S(2)}) async-start(bf16[8,128,768]{2,1,0:T(8,128)(2,1)} %broadcast_in_dim.2), calls=%async_computation.3 | async-start | bytes 3145728 | tf_op jit(solution)/shard_map/all_to_all | solution.py:167
  114.2 3.6 %collective-permute-start.1 = (bf16[172,768]{1,0:T(8,128)(2,1)S(1)}, bf16[172,768]{1,0:T(8,128)(2,1)S(1)}, u32[]{:S(2)}, u32[]{:S(2)}) collective-permute-start(bf16[172,768]{1,0:T(8,128)(2,1)S(1)} %fusion.12), channel_id=1, source_target_pairs={{0,24},{1,25},{2,26},{3,27},{4,28},{5,29},{6,30},{7,31},{8,0},{9,1... | collective-permute-start | bytes 792584 | tf_op jit(solution)/shard_map/ppermute | solution.py:18
  117.8 2.7 %collective-permute-start.3 = (bf16[172,768]{1,0:T(8,128)(2,1)S(1)}, bf16[172,768]{1,0:T(8,128)(2,1)S(1)}, u32[]{:S(2)}, u32[]{:S(2)}) collective-permute-start(bf16[172,768]{1,0:T(8,128)(2,1)S(1)} %fusion.15), channel_id=1, source_target_pairs={{0,16},{1,17},{2,18},{3,19},{4,20},{5,21},{6,22},{7,23},{8,24},{9,... | collective-permute-start | bytes 792584 | tf_op jit(solution)/shard_map/ppermute | solution.py:18
  120.5 2.3 %collective-permute-start.5 = (bf16[172,768]{1,0:T(8,128)(2,1)S(1)}, bf16[172,768]{1,0:T(8,128)(2,1)S(1)}, u32[]{:S(2)}, u32[]{:S(2)}) collective-permute-start(bf16[172,768]{1,0:T(8,128)(2,1)S(1)} %fusion.18), channel_id=1, source_target_pairs={{0,8},{1,9},{2,10},{3,11},{4,12},{5,13},{6,14},{7,15},{8,16},{9,17... | collective-permute-start | bytes 792584 | tf_op jit(solution)/shard_map/ppermute | solution.py:18
  122.9 3.9 %collective-permute-done.3 = bf16[172,768]{1,0:T(8,128)(2,1)S(1)} collective-permute-done((bf16[172,768]{1,0:T(8,128)(2,1)S(1)}, bf16[172,768]{1,0:T(8,128)(2,1)S(1)}, u32[]{:S(2)}, u32[]{:S(2)}) %collective-permute-start.3) | collective-permute-done | bytes 264224 | tf_op jit(solution)/shard_map/ppermute | solution.py:18
  126.8 4.2 %collective-permute-done.5 = bf16[172,768]{1,0:T(8,128)(2,1)S(1)} collective-permute-done((bf16[172,768]{1,0:T(8,128)(2,1)S(1)}, bf16[172,768]{1,0:T(8,128)(2,1)S(1)}, u32[]{:S(2)}, u32[]{:S(2)}) %collective-permute-start.5) | collective-permute-done | bytes 264224 | tf_op jit(solution)/shard_map/ppermute | solution.py:18
  131.2 2.3 %collective-permute-start.8 = (bf16[176,768]{1,0:T(8,128)(2,1)S(1)}, bf16[176,768]{1,0:T(8,128)(2,1)S(1)}, u32[]{:S(2)}, u32[]{:S(2)}) collective-permute-start(bf16[176,768]{1,0:T(8,128)(2,1)S(1)} %pad.8.g0_ref), channel_id=1, source_target_pairs={{0,24},{1,25},{2,26},{3,27},{4,28},{5,29},{6,30},{7,31},{8,0},{9,1... | collective-permute-start | bytes 811016 | tf_op jit(solution)/shard_map/ppermute | solution.py:18
  133.5 2.3 %collective-permute-start.7 = (bf16[176,768]{1,0:T(8,128)(2,1)S(1)}, bf16[176,768]{1,0:T(8,128)(2,1)S(1)}, u32[]{:S(2)}, u32[]{:S(2)}) collective-permute-start(bf16[176,768]{1,0:T(8,128)(2,1)S(1)} %pad.8.g0_ref), channel_id=1, source_target_pairs={{0,16},{1,17},{2,18},{3,19},{4,20},{5,21},{6,22},{7,23},{8,24},{9,... | collective-permute-start | bytes 811016 | tf_op jit(solution)/shard_map/ppermute | solution.py:18
  135.9 2.6 %collective-permute-start.6 = (bf16[176,768]{1,0:T(8,128)(2,1)S(1)}, bf16[176,768]{1,0:T(8,128)(2,1)S(1)}, u32[]{:S(2)}, u32[]{:S(2)}) collective-permute-start(bf16[176,768]{1,0:T(8,128)(2,1)S(1)} %pad.8.g0_ref), channel_id=1, source_target_pairs={{0,8},{1,9},{2,10},{3,11},{4,12},{5,13},{6,14},{7,15},{8,16},{9,17... | collective-permute-start | bytes 811016 | tf_op jit(solution)/shard_map/ppermute | solution.py:18
  138.7 3.8 %collective-permute-done.7.g2_ref = bf16[176,768]{1,0:T(8,128)(2,1)S(1)} collective-permute-done((bf16[176,768]{1,0:T(8,128)(2,1)S(1)}, bf16[176,768]{1,0:T(8,128)(2,1)S(1)}, u32[]{:S(2)}, u32[]{:S(2)}) %collective-permute-start.7) | collective-permute-done | bytes 270368 | tf_op jit(solution)/shard_map/ppermute | solution.py:18
  142.5 3.1 %collective-permute-done.6.g1_ref = bf16[176,768]{1,0:T(8,128)(2,1)S(1)} collective-permute-done((bf16[176,768]{1,0:T(8,128)(2,1)S(1)}, bf16[176,768]{1,0:T(8,128)(2,1)S(1)}, u32[]{:S(2)}, u32[]{:S(2)}) %collective-permute-start.6) | collective-permute-done | bytes 270368 | tf_op jit(solution)/shard_map/ppermute | solution.py:18
  145.6 5.8 %all-to-all-done.3 = bf16[8,128,768]{2,1,0:T(8,128)(2,1)S(1)} async-done(((bf16[8,128,768]{2,1,0:T(8,128)(2,1)}), bf16[8,128,768]{2,1,0:T(8,128)(2,1)S(1)}, u32[]{:S(2)}, u32[]{:S(2)}) %all-to-all-start.3) | async-done | bytes 1572896 | tf_op jit(solution)/shard_map/all_to_all | solution.py:167
  151.4 7.2 %shard_map.84 = f32[32,128]{1,0:T(8,128)S(1)} custom-call(s32[1]{0:T(128)} %bitcast.kx_ref, bf16[176,768]{1,0:T(8,128)(2,1)S(1)} %pad.8.g0_ref, bf16[176,768]{1,0:T(8,128)(2,1)S(1)} %collective-permute-done.6.g1_ref, bf16[176,768]{1,0:T(8,128)(2,1)S(1)} %collective-permute-done.7.g2_ref, bf16[176,768]{1,0:T(8,128)(2,1)S(1)} %collective-permute-done.8.g3_ref, ...), custom_call_target="tpu_custom_call" | custom-call | flops 4429185024 | bytes 9000000 | tf_op jit(solution)/shard_map/pallas_call | solution.py:104
  158.6 13.3 %all_to_all.30 = f32[32,1,128]{2,1,0:T(1,128)S(1)} all-to-all(f32[32,1,128]{2,1,0:T(1,128)S(1)} %bitcast.56), channel_id=1, replica_groups=mesh['dp'=16,'tensor'=32] {'tensor'}, dimensions={0} | all-to-all | bytes 32768 | tf_op jit(solution)/shard_map/all_to_all | solution.py:176
  (67 shorter events, 22.2 us)
Async XLA Ops:
  6.5 80.6 %all-gather.6.cloned.1.call-start = ((), (), s32[]{:S(2)}) async-start(), calls=%async_computation.6 | async-start | bytes 4202496 | tf_op jit(solution)/shard_map/all_gather | solution.py:139
  8.5 26.5 %copy-start.3 = (bf16[4096,128]{1,0:T(8,128)(2,1)S(1)}, bf16[4096,128]{1,0:T(8,128)(2,1)}, u32[]{:S(2)}) copy-start(bf16[4096,128]{1,0:T(8,128)(2,1)} %param.10) | copy-start | bytes 3145732
  34.9 5.6 %copy-start = (bf16[172,5504]{1,0:T(8,128)(2,1)S(1)}, bf16[172,5504]{1,0:T(8,128)(2,1)}, u32[]{:S(2)}) copy-start(bf16[172,5504]{1,0:T(8,128)(2,1)} %v_ref.1) | copy-start | bytes 5680132
  36.1 45.7 %all-to-all-start.1 = ((bf16[4,1376,128]{2,1,0:T(8,128)(2,1)}), bf16[4,1376,128]{2,1,0:T(8,128)(2,1)}, u32[]{:S(2)}, u32[]{:S(2)}) async-start(bf16[4,1376,128]{2,1,0:T(8,128)(2,1)} %pad_maximum_fusion), calls=%async_computation.1 | async-start | bytes 2818048 | tf_op jit(solution)/shard_map/all_to_all | solution.py:151
  40.4 111.0 %all-gather.4.cloned.1.call-start = ((), (), s32[]{:S(2)}) async-start(), calls=%async_computation.5 | async-start | bytes 6127616 | tf_op jit(solution)/shard_map/all_gather | solution.py:155
  41.8 25.9 %collective-permute-start = (bf16[172,1408]{1,0:T(8,128)(2,1)S(1)}, bf16[172,1408]{1,0:T(8,128)(2,1)S(1)}, u32[]{:S(2)}, u32[]{:S(2)}) collective-permute-start(bf16[172,1408]{1,0:T(8,128)(2,1)S(1)} %get-tuple-element.10), channel_id=1, source_target_pairs={{0,8},{1,9},{2,10},{3,11},{4,12},{5,13},{6,14},{7,15},{8,16},{9,17... | collective-permute-start | bytes 1453064 | tf_op jit(solution)/shard_map/ppermute | solution.py:18
  45.1 33.6 %collective-permute-start.2 = (bf16[172,1408]{1,0:T(8,128)(2,1)S(1)}, bf16[172,1408]{1,0:T(8,128)(2,1)S(1)}, u32[]{:S(2)}, u32[]{:S(2)}) collective-permute-start(bf16[172,1408]{1,0:T(8,128)(2,1)S(1)} %get-tuple-element.11), channel_id=1, source_target_pairs={{0,16},{1,17},{2,18},{3,19},{4,20},{5,21},{6,22},{7,23},{8,24},{9,... | collective-permute-start | bytes 1453064 | tf_op jit(solution)/shard_map/ppermute | solution.py:18
  49.4 31.1 %collective-permute-start.4 = (bf16[172,1408]{1,0:T(8,128)(2,1)S(1)}, bf16[172,1408]{1,0:T(8,128)(2,1)S(1)}, u32[]{:S(2)}, u32[]{:S(2)}) collective-permute-start(bf16[172,1408]{1,0:T(8,128)(2,1)S(1)} %get-tuple-element.12), channel_id=1, source_target_pairs={{0,24},{1,25},{2,26},{3,27},{4,28},{5,29},{6,30},{7,31},{8,0},{9,1... | collective-permute-start | bytes 1453064 | tf_op jit(solution)/shard_map/ppermute | solution.py:18
  67.7 12.8 %copy-start.5 = (bf16[172,1408]{1,0:T(8,128)(2,1)}, bf16[172,1408]{1,0:T(8,128)(2,1)S(1)}, u32[]{:S(2)}) copy-start(bf16[172,1408]{1,0:T(8,128)(2,1)S(1)} %collective-permute-done) | copy-start | bytes 1453060
  78.7 2.5 %copy-start.7 = (bf16[172,1408]{1,0:T(8,128)(2,1)}, bf16[172,1408]{1,0:T(8,128)(2,1)S(1)}, u32[]{:S(2)}) copy-start(bf16[172,1408]{1,0:T(8,128)(2,1)S(1)} %collective-permute-done.2) | copy-start | bytes 1453060
  80.5 1.3 copy-start.9
  87.1 1.9 %copy-start.2 = (bf16[4,1024,128]{2,1,0:T(8,128)(2,1)S(1)}, bf16[4,1024,128]{2,1,0:T(8,128)(2,1)}, u32[]{:S(2)}) copy-start(bf16[4,1024,128]{2,1,0:T(8,128)(2,1)} %slice.89) | copy-start | bytes 3145732
  92.4 12.6 %all-to-all-start.2 = ((bf16[4,128,768]{2,1,0:T(8,128)(2,1)}), bf16[4,128,768]{2,1,0:T(8,128)(2,1)S(1)}, u32[]{:S(2)}, u32[]{:S(2)}) async-start(bf16[4,128,768]{2,1,0:T(8,128)(2,1)} %bitcast_convert_fusion), calls=%async_computation.2 | async-start | bytes 1572864 | tf_op jit(solution)/shard_map/all_to_all | solution.py:158
  96.6 1.2 copy-start.6
  97.2 1.8 copy-start.8
  98.4 1.8 copy-start.10
  106.2 16.6 %copy-start.4 = (s32[6]{0:T(128)S(1)}, s32[6]{0:T(128)}, u32[]{:S(2)}) copy-start(s32[6]{0:T(128)} %param.15) | copy-start | bytes 76
  107.4 44.0 %all-to-all-start.3 = ((bf16[8,128,768]{2,1,0:T(8,128)(2,1)}), bf16[8,128,768]{2,1,0:T(8,128)(2,1)S(1)}, u32[]{:S(2)}, u32[]{:S(2)}) async-start(bf16[8,128,768]{2,1,0:T(8,128)(2,1)} %broadcast_in_dim.2), calls=%async_computation.3 | async-start | bytes 3145728 | tf_op jit(solution)/shard_map/all_to_all | solution.py:167
  114.2 8.7 %collective-permute-start.1 = (bf16[172,768]{1,0:T(8,128)(2,1)S(1)}, bf16[172,768]{1,0:T(8,128)(2,1)S(1)}, u32[]{:S(2)}, u32[]{:S(2)}) collective-permute-start(bf16[172,768]{1,0:T(8,128)(2,1)S(1)} %fusion.12), channel_id=1, source_target_pairs={{0,24},{1,25},{2,26},{3,27},{4,28},{5,29},{6,30},{7,31},{8,0},{9,1... | collective-permute-start | bytes 792584 | tf_op jit(solution)/shard_map/ppermute | solution.py:18
  117.8 9.0 %collective-permute-start.3 = (bf16[172,768]{1,0:T(8,128)(2,1)S(1)}, bf16[172,768]{1,0:T(8,128)(2,1)S(1)}, u32[]{:S(2)}, u32[]{:S(2)}) collective-permute-start(bf16[172,768]{1,0:T(8,128)(2,1)S(1)} %fusion.15), channel_id=1, source_target_pairs={{0,16},{1,17},{2,18},{3,19},{4,20},{5,21},{6,22},{7,23},{8,24},{9,... | collective-permute-start | bytes 792584 | tf_op jit(solution)/shard_map/ppermute | solution.py:18
  120.5 10.5 %collective-permute-start.5 = (bf16[172,768]{1,0:T(8,128)(2,1)S(1)}, bf16[172,768]{1,0:T(8,128)(2,1)S(1)}, u32[]{:S(2)}, u32[]{:S(2)}) collective-permute-start(bf16[172,768]{1,0:T(8,128)(2,1)S(1)} %fusion.18), channel_id=1, source_target_pairs={{0,8},{1,9},{2,10},{3,11},{4,12},{5,13},{6,14},{7,15},{8,16},{9,17... | collective-permute-start | bytes 792584 | tf_op jit(solution)/shard_map/ppermute | solution.py:18
  131.2 7.5 %collective-permute-start.8 = (bf16[176,768]{1,0:T(8,128)(2,1)S(1)}, bf16[176,768]{1,0:T(8,128)(2,1)S(1)}, u32[]{:S(2)}, u32[]{:S(2)}) collective-permute-start(bf16[176,768]{1,0:T(8,128)(2,1)S(1)} %pad.8.g0_ref), channel_id=1, source_target_pairs={{0,24},{1,25},{2,26},{3,27},{4,28},{5,29},{6,30},{7,31},{8,0},{9,1... | collective-permute-start | bytes 811016 | tf_op jit(solution)/shard_map/ppermute | solution.py:18
  133.5 9.0 %collective-permute-start.7 = (bf16[176,768]{1,0:T(8,128)(2,1)S(1)}, bf16[176,768]{1,0:T(8,128)(2,1)S(1)}, u32[]{:S(2)}, u32[]{:S(2)}) collective-permute-start(bf16[176,768]{1,0:T(8,128)(2,1)S(1)} %pad.8.g0_ref), channel_id=1, source_target_pairs={{0,16},{1,17},{2,18},{3,19},{4,20},{5,21},{6,22},{7,23},{8,24},{9,... | collective-permute-start | bytes 811016 | tf_op jit(solution)/shard_map/ppermute | solution.py:18
  135.9 9.8 %collective-permute-start.6 = (bf16[176,768]{1,0:T(8,128)(2,1)S(1)}, bf16[176,768]{1,0:T(8,128)(2,1)S(1)}, u32[]{:S(2)}, u32[]{:S(2)}) collective-permute-start(bf16[176,768]{1,0:T(8,128)(2,1)S(1)} %pad.8.g0_ref), channel_id=1, source_target_pairs={{0,8},{1,9},{2,10},{3,11},{4,12},{5,13},{6,14},{7,15},{8,16},{9,17... | collective-permute-start | bytes 811016 | tf_op jit(solution)/shard_map/ppermute | solution.py:18
  (1 other events, 0.7 us)
Sparse Core Ops, SparseCore 0:
  9.4 58.3 all-gather.5
  85.0 45.4 all-gather.3

commit v6 on v5

--- a/solution.py
+++ b/solution.py
@@ -39,7 +39,10 @@
     )(x, y)
 
 
-def columns_kernel(kx_ref, v_ref, o0_ref, o1_ref, o2_ref, o3_ref, all_ref):
+HALF = 96
+
+
+def columns_kernel(where_ref, v_ref, o0_ref, o1_ref, o2_ref, o3_ref, all_ref):
     rows, columns = v_ref.shape
     width = columns // (NX * NY)
     for x in range(NX):
@@ -51,23 +54,27 @@
                 block = jnp.concatenate(
                     [v_ref[:, first:], jnp.zeros((rows, first + PAD - columns), v_ref.dtype)], axis=1
                 )
+            block = jnp.concatenate([block, jnp.zeros((PAD - rows, PAD), v_ref.dtype)], axis=0)
             all_ref[x, :, y * PAD : (y + 1) * PAD] = block
-    for d, o_ref in enumerate((o0_ref, o1_ref, o2_ref, o3_ref)):
-        o_ref[...] = all_ref[(kx_ref[0] + d) & (NX - 1)]
-
-
-def column_blocks(kx, v):
-    one = jax.ShapeDtypeStruct((v.shape[0], NY * PAD), v.dtype)
+    kx = where_ref[0]
+    first = pl.multiple_of(where_ref[1] * (PAD - HALF), 16)
+    o0_ref[...] = all_ref[kx]
+    for d, o_ref in enumerate((o1_ref, o2_ref, o3_ref)):
+        o_ref[...] = all_ref[(kx + d + 1) & (NX - 1), pl.ds(first, HALF), :]
+
+
+def column_blocks(where, v):
+    deep = NY * PAD
     vmem = pl.BlockSpec(memory_space=pltpu.VMEM)
     return pl.pallas_call(
         columns_kernel,
-        out_shape=[one] * NX,
+        out_shape=[jax.ShapeDtypeStruct((rows, deep), v.dtype) for rows in (PAD, HALF, HALF, HALF)],
         in_specs=[pl.BlockSpec(memory_space=pltpu.SMEM), vmem],
         out_specs=[vmem] * NX,
-        scratch_shapes=[pltpu.VMEM((NX,) + one.shape, v.dtype)],
+        scratch_shapes=[pltpu.VMEM((NX, PAD, deep), v.dtype)],
         compiler_params=pltpu.CompilerParams(vmem_limit_bytes=24 * 1024 * 1024),
         cost_estimate=pl.CostEstimate(flops=0, bytes_accessed=4_000_000, transcendentals=0),
-    )(kx, v)
+    )(where, v)
 
 
 def score_kernel(kx_ref, g0_ref, g1_ref, g2_ref, g3_ref, a_ref, s_ref, o_ref, lhs_ref):
@@ -128,12 +135,18 @@
     return lax.dynamic_update_slice(array, corner + zero.reshape(corner.shape), first)
 
 
+def both_halves(mine, core):
+    other = lax.ppermute(mine, "dp", [(n, n ^ 1) for n in range(2 * NZ)])
+    return jnp.where(core == 0, mine, other), jnp.where(core == 0, other, mine)
+
+
 def local(activations, out_grads_t, in_basis, out_basis_t, query_proj, eigvals, damping, lengths):
     bf, f32 = jnp.bfloat16, jnp.float32
     tokens, width = activations.shape[0], out_grads_t.shape[0]
     seqs, queries = lengths.shape[0], query_proj.shape[0]
     seq_len = tokens // seqs
     kx = lax.shift_right_logical(lax.axis_index("tensor"), 3)
+    core = lax.axis_index("dp") & 1
 
     both = packed(activations, out_grads_t)
     both = lax.all_gather(both, "tensor", axis_index_groups=YG)
@@ -143,33 +156,35 @@
     scaled = (query_proj.astype(f32) / (eigvals + damping[0])).astype(bf)
     scaled = jnp.pad(scaled, ((0, 0), (0, PAD - width), (0, 0)))
     pieces = scaled.reshape(queries, PAD, 2, 128).transpose(0, 2, 1, 3).reshape(8, PAD, 128)
-    blocks = column_blocks(kx.reshape(1), out_basis_t)
-    vs = [blocks[0]] + [shift_x(blocks[d], d) for d in range(1, NX)]
+    blocks = column_blocks(jnp.stack([kx, core]), out_basis_t)
+    near = [shift_x(blocks[d], d) for d in range(1, NX)]
+    tie = (near[0][:1, :1] + near[1][:1, :1] + near[2][:1, :1]) * 0
     pieces = lax.all_to_all(pieces, "dp", 0, 0, axis_index_groups=ZG)
-    rows = NY * 128
-    mixed = jnp.concatenate([in_basis.reshape(NX, rows, 128), pieces.reshape(NX, 2 * PAD, 128)], axis=1)
-    mixed = lax.all_to_all(mixed, "tensor", 0, 0, axis_index_groups=XG)
-    u4 = mixed[:, :rows]
-    tie = (vs[1][:1, :1] + vs[2][:1, :1] + vs[3][:1, :1]) * 0
-    pieces = after(mixed[:, rows:].reshape(NX, 2, PAD, 128), tie)
+    rows = NY * 128 // 2
+    mine = lax.dynamic_index_in_dim(in_basis.reshape(NX, 2, rows, 128), core, 1, keepdims=False)
+    mixed = jnp.concatenate([mine, pieces.reshape(NX, 2 * PAD, 128)], axis=1)
+    mixed = lax.all_to_all(after(mixed, tie), "tensor", 0, 0, axis_index_groups=XG)
+    u4 = jnp.stack(both_halves(mixed[:, :rows], core), axis=1)
+    pieces = mixed[:, rows:].reshape(NX, 2, PAD, 128)
     tiles = lax.all_gather(pieces, "dp").reshape(NZ, 2, NX, 2, PAD, 128)
 
     a_part = jnp.einsum("xyed,yte->xdt", u4.reshape(NX, NY, 128, 128), x8, preferred_element_type=f32).astype(bf)
     a_parts = lax.all_to_all(a_part, "tensor", 0, 0, axis_index_groups=XG)
 
+    near = after(jnp.stack(near), a_part[0, :1, :1] * 0)
+    v_low, v_high = both_halves(near, core)
+    vs = [blocks[0]] + [jnp.concatenate([v_low[n], v_high[n, 2 * HALF - PAD :]]) for n in range(NX - 1)]
     y8 = y8.transpose(0, 2, 1, 3).reshape(NY * PAD, tokens)
     g_parts = [jnp.dot(v, y8, preferred_element_type=f32).astype(bf) for v in vs]
-    tie = (g_parts[0][:1, :1] + g_parts[1][:1, :1] + g_parts[2][:1, :1] + g_parts[3][:1, :1]) * 0
     g_parts = [g_parts[0]] + [shift_x(g_parts[d], -d) for d in range(1, NX)]
 
-    at = after(add_parts(a_parts).astype(bf), tie)
+    at = after(add_parts(a_parts).astype(bf), v_low[0, :1, :1] * 0)
     at = jnp.broadcast_to(at, (NY, 128, tokens))
     at = lax.all_to_all(at, "tensor", 0, 0, axis_index_groups=YG)
 
     position = lax.broadcasted_iota(jnp.int32, (seqs, seq_len), 1)
     keep = (position < lengths[:, None]).astype(f32).reshape(1, tokens)
     g = (add_parts(g_parts) * keep).astype(bf)
-    g = jnp.pad(g, ((0, PAD - width), (0, 0)))
     gs = [g] + [shift_x(g, d) for d in range(1, NX)]
 
     tile = score_tiles(kx.reshape(1), gs, at.reshape(NY * 128, tokens), tiles)

time: 183 us -> 183 us (level)
  waiting for transfers between devices: 47.7 us -> 32.2 us
  starting transfers between devices: 41.1 us -> 55.1 us
  blocking collectives: 36.9 us -> 31.6 us
  other arithmetic: 3.61 us -> 8.69 us
    ppermute x9, waiting for transfers between devices: 40.9 us -> 25 us  [shift_x(): return lax.ppermute(array, 'tensor', perm)]
    all_to_all x1, blocking collectives: 23.6 us -> 15.5 us  [local(): lax.all_to_all(after(mixed, tie), 'tensor', 0, 0, axis_index_groups=XG)]
    ppermute x0 -> x2, starting transfers between devices: none -> 6.62 us  [both_halves(): other = lax.ppermute(mine, 'dp', [(n, n ^ 1) for n in range(2 * NZ)])]
    all_to_all x1, starting transfers between devices: 4.32 us -> 10.9 us  [local(): pieces = lax.all_to_all(pieces, 'dp', 0, 0, axis_index_groups=ZG)]
    all_to_all x1, waiting for transfers between devices: 5.81 us -> 0.01 us  [local(): at = lax.all_to_all(at, 'tensor', 0, 0, axis_index_groups=YG)]
    all_to_all x1, waiting for transfers between devices: 0.97 us -> 5.54 us  [local(): a_parts = lax.all_to_all(a_part, 'tensor', 0, 0, axis_index_groups=XG)]
    all_to_all x1, blocking collectives: 13.3 us -> 16.1 us  [local(): lax.all_to_all(tile, 'tensor', 0, 0, tiled=True).sum(0)[:seqs * queries]]
    slice x10 -> x8, local copies, waits for them, and re-layouts: 7.41 us -> 4.89 us  [the longest x3 2.36 us: local(): tie = (near[0][:1, :1] + near[1][:1, :1] + near[2][:1, :1]) * 0]
  transfers between devices with their start and end apart: 14 -> 16, of which waited for: 9 -> 7; matrix products, arithmetic and copies ran while one was open for 12% -> 15% of each run, Pallas kernels for 1% -> 1%
where the time goes in v6:
time: 183 us; the launch traced here: 179 us
  starting transfers between devices  55.1 us (30%)
  waiting for transfers between devices  32.2 us (18%)
  blocking collectives  31.6 us (17%)
  between operations  19.5 us (11%)
  local copies, waits for them, and re-layouts  14.6 us (8%)
  Pallas kernels  11.6 us (6%)
  other arithmetic  8.69 us (5%)
  matrix products  6.12 us (3%)
    ppermute x9, starting transfers between devices, shift_x(): return lax.ppermute(array, 'tensor', perm)  27.2 us
    ppermute x9, waiting for transfers between devices, shift_x(): return lax.ppermute(array, 'tensor', perm)  25 us
    all_to_all x1, blocking collectives, local(): lax.all_to_all(tile, 'tensor', 0, 0, tiled=True).sum(0)[:seqs * queries]  16.1 us
    all_to_all x1, blocking collectives, local(): lax.all_to_all(after(mixed, tie), 'tensor', 0, 0, axis_index_groups=XG)  15.5 us
    all_to_all x1, starting transfers between devices, local(): pieces = lax.all_to_all(pieces, 'dp', 0, 0, axis_index_groups=ZG)  10.9 us
    pallas_call x1, Pallas kernels, score_tiles(): pl.pallas_call(score_kernel, grid=(queries,), out_shape=jax.ShapeDtypeStr...  7.06 us
    all_to_all x1, starting transfers between devices, local(): at = lax.all_to_all(at, 'tensor', 0, 0, axis_index_groups=YG)  6.87 us
    ppermute x2, starting transfers between devices, both_halves(): other = lax.ppermute(mine, 'dp', [(n, n ^ 1) for n in range(2 * NZ)])  6.62 us
  transfers between devices with their start and end apart: 16, of which 7 were waited for; matrix products, arithmetic and copies ran while one was open for 15% of the time, Pallas kernels for 1%

profile of v6, /device:TPU:1, one launch (start us, length us, event | category | flops | bytes accessed | tf_op | source)
XLA Modules:
  0.0 179.5 jit_solution(4218531619782262668)
XLA Ops:
  12.2 10.9 %all-to-all-start = ((bf16[8,176,128]{2,1,0:T(8,128)(2,1)}), bf16[8,176,128]{2,1,0:T(8,128)(2,1)}, u32[]{:S(2)}, u32[]{:S(2)}) async-start(bf16[8,176,128]{2,1,0:T(8,128)(2,1)} %bitcast.11), calls=%async_computation | async-start | bytes 720896 | tf_op jit(solution)/shard_map/all_to_all | solution.py:162
  23.2 2.6 %shard_map.82 = (bf16[176,1408]{1,0:T(8,128)(2,1)S(1)}, bf16[96,1408]{1,0:T(8,128)(2,1)}, bf16[96,1408]{1,0:T(8,128)(2,1)}, bf16[96,1408]{1,0:T(8,128)(2,1)}) custom-call(s32[2]{0:T(128)S(1)} %pad_add_fusion.where_ref, bf16[172,5504]{1,0:T(8,128)(2,1)S(1)} %copy-done.1), custom_call_target="tpu_custom_call" | custom-call | bytes 4000000 | tf_op jit(solution)/shard_map/pallas_call | solution.py:69
  25.7 3.1 %collective-permute-start = (bf16[96,1408]{1,0:T(8,128)(2,1)}, bf16[96,1408]{1,0:T(8,128)(2,1)S(1)}, u32[]{:S(2)}, u32[]{:S(2)}) collective-permute-start(bf16[96,1408]{1,0:T(8,128)(2,1)} %get-tuple-element.10), channel_id=1, source_target_pairs={{0,8},{1,9},{2,10},{3,11},{4,12},{5,13},{6,14},{7,15},{8,16},{9,17... | collective-permute-start | bytes 811016 | tf_op jit(solution)/shard_map/ppermute | solution.py:18
  28.9 4.4 %collective-permute-start.1 = (bf16[96,1408]{1,0:T(8,128)(2,1)}, bf16[96,1408]{1,0:T(8,128)(2,1)}, u32[]{:S(2)}, u32[]{:S(2)}) collective-permute-start(bf16[96,1408]{1,0:T(8,128)(2,1)} %get-tuple-element.11), channel_id=1, source_target_pairs={{0,16},{1,17},{2,18},{3,19},{4,20},{5,21},{6,22},{7,23},{8,24},{9,... | collective-permute-start | bytes 811016 | tf_op jit(solution)/shard_map/ppermute | solution.py:18
  33.2 3.1 %collective-permute-start.2 = (bf16[96,1408]{1,0:T(8,128)(2,1)}, bf16[96,1408]{1,0:T(8,128)(2,1)S(1)}, u32[]{:S(2)}, u32[]{:S(2)}) collective-permute-start(bf16[96,1408]{1,0:T(8,128)(2,1)} %get-tuple-element.12), channel_id=1, source_target_pairs={{0,24},{1,25},{2,26},{3,27},{4,28},{5,29},{6,30},{7,31},{8,0},{9,1... | collective-permute-start | bytes 811016 | tf_op jit(solution)/shard_map/ppermute | solution.py:18
  37.5 5.5 %collective-permute-done.1 = bf16[96,1408]{1,0:T(8,128)(2,1)} collective-permute-done((bf16[96,1408]{1,0:T(8,128)(2,1)}, bf16[96,1408]{1,0:T(8,128)(2,1)}, u32[]{:S(2)}, u32[]{:S(2)}) %collective-permute-start.1) | collective-permute-done | bytes 270368 | tf_op jit(solution)/shard_map/ppermute | solution.py:18
  48.4 15.5 %all_to_all.29 = bf16[4,864,128]{2,1,0:T(8,128)(2,1)S(1)} all-to-all(bf16[4,864,128]{2,1,0:T(8,128)(2,1)S(1)} %dynamic_update_slice.9), channel_id=1, replica_groups={{0,8,16,24},{1,9,17,25},{2,10,18,26},{3,11,19,27},{4,12,20,28},{5,13,21..., dimensions={0} | all-to-all | bytes 1769472 | tf_op jit(solution)/shard_map/all_to_all | solution.py:166
  64.8 4.3 %collective-permute-start.3 = (bf16[4,512,128]{2,1,0:T(8,128)(2,1)S(1)}, bf16[4,512,128]{2,1,0:T(8,128)(2,1)}, u32[]{:S(2)}, u32[]{:S(2)}) collective-permute-start(bf16[4,512,128]{2,1,0:T(8,128)(2,1)S(1)} %slice.114), channel_id=1, source_target_pairs={{0,32},{32,0},{64,96},{96,64},{128,160},{160,128},{192,224},{224,1... | collective-permute-start | bytes 1572872 | tf_op jit(solution)/shard_map/ppermute | solution.py:139
  73.0 3.7 %bitcast_convert_fusion = bf16[4,128,768]{2,1,0:T(8,128)(2,1)} fusion(bf16[4,8,128,128]{3,2,1,0:T(8,128)(2,1)} %bitcast.90, bf16[8,1824,128]{2,1,0:T(8,128)(2,1)} %bitcast.88), kind=kOutput, calls=%fused_computation.10 | convolution fusion | flops 805699584 | bytes 3407872 | tf_op jit(solution)/shard_map/xyed,yte->xdt/dot_general | solution.py:171
  76.7 3.5 %all-to-all-start.2 = ((bf16[4,128,768]{2,1,0:T(8,128)(2,1)}), bf16[4,128,768]{2,1,0:T(8,128)(2,1)S(1)}, u32[]{:S(2)}, u32[]{:S(2)}) async-start(bf16[4,128,768]{2,1,0:T(8,128)(2,1)} %bitcast_convert_fusion), calls=%async_computation.2 | async-start | bytes 1572864 | tf_op jit(solution)/shard_map/all_to_all | solution.py:172
  84.4 2.3 %collective-permute-start.4 = (bf16[3,96,1408]{2,1,0:T(8,128)(2,1)S(1)}, bf16[3,96,1408]{2,1,0:T(8,128)(2,1)}, u32[]{:S(2)}, u32[]{:S(2)}) collective-permute-start(bf16[3,96,1408]{2,1,0:T(8,128)(2,1)S(1)} %dynamic_update_slice.10), channel_id=1, source_target_pairs={{0,32},{32,0},{64,96},{96,64},{128,160},{160,128},{192,224},{224,1... | collective-permute-start | bytes 2433032 | tf_op jit(solution)/shard_map/ppermute | solution.py:139
  86.7 5.5 %all-to-all-done.2 = bf16[4,128,768]{2,1,0:T(8,128)(2,1)S(1)} async-done(((bf16[4,128,768]{2,1,0:T(8,128)(2,1)}), bf16[4,128,768]{2,1,0:T(8,128)(2,1)S(1)}, u32[]{:S(2)}, u32[]{:S(2)}) %all-to-all-start.2) | async-done | bytes 786464 | tf_op jit(solution)/shard_map/all_to_all | solution.py:172
  92.8 2.2 %broadcast_select_fusion.1 = (bf16[3,96,1408]{2,1,0:T(8,128)(2,1)S(1)}, bf16[3,96,1408]{2,1,0:T(8,128)(2,1)}) fusion(bf16[3,96,1408]{2,1,0:T(8,128)(2,1)S(1)} %dynamic_update_slice.10, bf16[3,96,1408]{2,1,0:T(8,128)(2,1)} %collective-permute-done.4, pred[]{:T(512)S(6)} %eq.2), kind=kLoop, calls=%fused_computation.20 | loop fusion | flops 811008 | bytes 3244033 | tf_op jit(solution)/shard_map/jit(_where)/select_n | solution.py:140
  98.0 6.9 %all-to-all-start.3 = ((bf16[8,128,768]{2,1,0:T(8,128)(2,1)}), bf16[8,128,768]{2,1,0:T(8,128)(2,1)S(1)}, u32[]{:S(2)}, u32[]{:S(2)}) async-start(bf16[8,128,768]{2,1,0:T(8,128)(2,1)} %broadcast_in_dim.2), calls=%async_computation.3 | async-start | bytes 3145728 | tf_op jit(solution)/shard_map/all_to_all | solution.py:183
  108.8 2.8 %collective-permute-start.5 = (bf16[176,768]{1,0:T(8,128)(2,1)S(1)}, bf16[176,768]{1,0:T(8,128)(2,1)S(1)}, u32[]{:S(2)}, u32[]{:S(2)}) collective-permute-start(bf16[176,768]{1,0:T(8,128)(2,1)S(1)} %fusion.15), channel_id=1, source_target_pairs={{0,24},{1,25},{2,26},{3,27},{4,28},{5,29},{6,30},{7,31},{8,0},{9,1... | collective-permute-start | bytes 811016 | tf_op jit(solution)/shard_map/ppermute | solution.py:18
  112.2 3.2 %collective-permute-start.6 = (bf16[176,768]{1,0:T(8,128)(2,1)S(1)}, bf16[176,768]{1,0:T(8,128)(2,1)S(1)}, u32[]{:S(2)}, u32[]{:S(2)}) collective-permute-start(bf16[176,768]{1,0:T(8,128)(2,1)S(1)} %fusion.18), channel_id=1, source_target_pairs={{0,16},{1,17},{2,18},{3,19},{4,20},{5,21},{6,22},{7,23},{8,24},{9,... | collective-permute-start | bytes 811016 | tf_op jit(solution)/shard_map/ppermute | solution.py:18
  118.1 3.8 %collective-permute-done.6 = bf16[176,768]{1,0:T(8,128)(2,1)S(1)} collective-permute-done((bf16[176,768]{1,0:T(8,128)(2,1)S(1)}, bf16[176,768]{1,0:T(8,128)(2,1)S(1)}, u32[]{:S(2)}, u32[]{:S(2)}) %collective-permute-start.6) | collective-permute-done | bytes 270368 | tf_op jit(solution)/shard_map/ppermute | solution.py:18
  121.8 6.9 %collective-permute-done.7 = bf16[176,768]{1,0:T(8,128)(2,1)S(1)} collective-permute-done((bf16[176,768]{1,0:T(8,128)(2,1)S(1)}, bf16[176,768]{1,0:T(8,128)(2,1)S(1)}, u32[]{:S(2)}, u32[]{:S(2)}) %collective-permute-start.7) | collective-permute-done | bytes 270368 | tf_op jit(solution)/shard_map/ppermute | solution.py:18
  131.3 3.4 %collective-permute-start.8 = (bf16[176,768]{1,0:T(8,128)(2,1)S(1)}, bf16[176,768]{1,0:T(8,128)(2,1)S(1)}, u32[]{:S(2)}, u32[]{:S(2)}) collective-permute-start(bf16[176,768]{1,0:T(8,128)(2,1)S(1)} %multiply_convert_fusion.g0_ref), channel_id=1, source_target_pairs={{0,8},{1,9},{2,10},{3,11},{4,12},{5,13},{6,14},{7,15},{8,16},{9,17... | collective-permute-start | bytes 811016 | tf_op jit(solution)/shard_map/ppermute | solution.py:18
  134.7 3.5 %collective-permute-start.9 = (bf16[176,768]{1,0:T(8,128)(2,1)S(1)}, bf16[176,768]{1,0:T(8,128)(2,1)S(1)}, u32[]{:S(2)}, u32[]{:S(2)}) collective-permute-start(bf16[176,768]{1,0:T(8,128)(2,1)S(1)} %multiply_convert_fusion.g0_ref), channel_id=1, source_target_pairs={{0,16},{1,17},{2,18},{3,19},{4,20},{5,21},{6,22},{7,23},{8,24},{9,... | collective-permute-start | bytes 811016 | tf_op jit(solution)/shard_map/ppermute | solution.py:18
  138.2 2.1 %collective-permute-done.8.g1_ref = bf16[176,768]{1,0:T(8,128)(2,1)S(1)} collective-permute-done((bf16[176,768]{1,0:T(8,128)(2,1)S(1)}, bf16[176,768]{1,0:T(8,128)(2,1)S(1)}, u32[]{:S(2)}, u32[]{:S(2)}) %collective-permute-start.8) | collective-permute-done | bytes 270368 | tf_op jit(solution)/shard_map/ppermute | solution.py:18
  140.3 6.7 %collective-permute-done.9.g2_ref = bf16[176,768]{1,0:T(8,128)(2,1)S(1)} collective-permute-done((bf16[176,768]{1,0:T(8,128)(2,1)S(1)}, bf16[176,768]{1,0:T(8,128)(2,1)S(1)}, u32[]{:S(2)}, u32[]{:S(2)}) %collective-permute-start.9) | collective-permute-done | bytes 270368 | tf_op jit(solution)/shard_map/ppermute | solution.py:18
  148.7 7.1 %shard_map.84 = f32[32,128]{1,0:T(8,128)S(1)} custom-call(s32[1]{0:T(128)} %bitcast.kx_ref, bf16[176,768]{1,0:T(8,128)(2,1)S(1)} %multiply_convert_fusion.g0_ref, bf16[176,768]{1,0:T(8,128)(2,1)S(1)} %collective-permute-done.8.g1_ref, bf16[176,768]{1,0:T(8,128)(2,1)S(1)} %copy-done.3, bf16[176,768]{1,0:T(8,128)(2,1)S(1)} %collective-permute-done.10.g3_ref, ...), custom_call_target="tpu_custom_call" | custom-call | flops 4429185024 | bytes 9000000 | tf_op jit(solution)/shard_map/pallas_call | solution.py:111
  155.7 16.1 %all_to_all.30 = f32[32,1,128]{2,1,0:T(1,128)S(1)} all-to-all(f32[32,1,128]{2,1,0:T(1,128)S(1)} %bitcast.81), channel_id=1, replica_groups=mesh['dp'=16,'tensor'=32] {'tensor'}, dimensions={0} | all-to-all | bytes 32768 | tf_op jit(solution)/shard_map/all_to_all | solution.py:191
  (78 shorter events, 31.1 us)
Async XLA Ops:
  6.5 29.8 %copy-start = (bf16[4096,128]{1,0:T(8,128)(2,1)S(1)}, bf16[4096,128]{1,0:T(8,128)(2,1)}, u32[]{:S(2)}) copy-start(bf16[4096,128]{1,0:T(8,128)(2,1)} %param.10) | copy-start | bytes 3145732
  6.5 66.5 %all-gather.6.cloned.1.call-start = ((), (), s32[]{:S(2)}) async-start(), calls=%async_computation.6 | async-start | bytes 4202496 | tf_op jit(solution)/shard_map/all_gather | solution.py:152
  8.5 14.7 %copy-start.1 = (bf16[172,5504]{1,0:T(8,128)(2,1)S(1)}, bf16[172,5504]{1,0:T(8,128)(2,1)}, u32[]{:S(2)}) copy-start(bf16[172,5504]{1,0:T(8,128)(2,1)} %v_ref.1) | copy-start | bytes 5680132
  12.2 35.1 %all-to-all-start = ((bf16[8,176,128]{2,1,0:T(8,128)(2,1)}), bf16[8,176,128]{2,1,0:T(8,128)(2,1)}, u32[]{:S(2)}, u32[]{:S(2)}) async-start(bf16[8,176,128]{2,1,0:T(8,128)(2,1)} %bitcast.11), calls=%async_computation | async-start | bytes 720896 | tf_op jit(solution)/shard_map/all_to_all | solution.py:162
  23.0 124.7 %all-gather.4.cloned.1.call-start = ((), (), s32[]{:S(2)}) async-start(), calls=%async_computation.5 | async-start | bytes 6127616 | tf_op jit(solution)/shard_map/all_gather | solution.py:169
  25.7 11.1 %collective-permute-start = (bf16[96,1408]{1,0:T(8,128)(2,1)}, bf16[96,1408]{1,0:T(8,128)(2,1)S(1)}, u32[]{:S(2)}, u32[]{:S(2)}) collective-permute-start(bf16[96,1408]{1,0:T(8,128)(2,1)} %get-tuple-element.10), channel_id=1, source_target_pairs={{0,8},{1,9},{2,10},{3,11},{4,12},{5,13},{6,14},{7,15},{8,16},{9,17... | collective-permute-start | bytes 811016 | tf_op jit(solution)/shard_map/ppermute | solution.py:18
  28.9 14.1 %collective-permute-start.1 = (bf16[96,1408]{1,0:T(8,128)(2,1)}, bf16[96,1408]{1,0:T(8,128)(2,1)}, u32[]{:S(2)}, u32[]{:S(2)}) collective-permute-start(bf16[96,1408]{1,0:T(8,128)(2,1)} %get-tuple-element.11), channel_id=1, source_target_pairs={{0,16},{1,17},{2,18},{3,19},{4,20},{5,21},{6,22},{7,23},{8,24},{9,... | collective-permute-start | bytes 811016 | tf_op jit(solution)/shard_map/ppermute | solution.py:18
  33.2 12.2 %collective-permute-start.2 = (bf16[96,1408]{1,0:T(8,128)(2,1)}, bf16[96,1408]{1,0:T(8,128)(2,1)S(1)}, u32[]{:S(2)}, u32[]{:S(2)}) collective-permute-start(bf16[96,1408]{1,0:T(8,128)(2,1)} %get-tuple-element.12), channel_id=1, source_target_pairs={{0,24},{1,25},{2,26},{3,27},{4,28},{5,29},{6,30},{7,31},{8,0},{9,1... | collective-permute-start | bytes 811016 | tf_op jit(solution)/shard_map/ppermute | solution.py:18
  36.9 11.5 %copy-start.7 = (bf16[96,1408]{1,0:T(8,128)(2,1)}, bf16[96,1408]{1,0:T(8,128)(2,1)S(1)}, u32[]{:S(2)}) copy-start(bf16[96,1408]{1,0:T(8,128)(2,1)S(1)} %collective-permute-done) | copy-start | bytes 811012
  45.4 1.9 %copy-start.9 = (bf16[96,1408]{1,0:T(8,128)(2,1)}, bf16[96,1408]{1,0:T(8,128)(2,1)S(1)}, u32[]{:S(2)}) copy-start(bf16[96,1408]{1,0:T(8,128)(2,1)S(1)} %collective-permute-done.2) | copy-start | bytes 811012
  64.8 6.0 %collective-permute-start.3 = (bf16[4,512,128]{2,1,0:T(8,128)(2,1)S(1)}, bf16[4,512,128]{2,1,0:T(8,128)(2,1)}, u32[]{:S(2)}, u32[]{:S(2)}) collective-permute-start(bf16[4,512,128]{2,1,0:T(8,128)(2,1)S(1)} %slice.114), channel_id=1, source_target_pairs={{0,32},{32,0},{64,96},{96,64},{128,160},{160,128},{192,224},{224,1... | collective-permute-start | bytes 1572872 | tf_op jit(solution)/shard_map/ppermute | solution.py:139
  73.0 7.2 %copy-start.8 = (bf16[96,1408]{1,0:T(8,128)(2,1)S(1)}, bf16[96,1408]{1,0:T(8,128)(2,1)}, u32[]{:S(2)}) copy-start(bf16[96,1408]{1,0:T(8,128)(2,1)} %copy-done.7) | copy-start | bytes 811012
  76.7 15.5 %all-to-all-start.2 = ((bf16[4,128,768]{2,1,0:T(8,128)(2,1)}), bf16[4,128,768]{2,1,0:T(8,128)(2,1)S(1)}, u32[]{:S(2)}, u32[]{:S(2)}) async-start(bf16[4,128,768]{2,1,0:T(8,128)(2,1)} %bitcast_convert_fusion), calls=%async_computation.2 | async-start | bytes 1572864 | tf_op jit(solution)/shard_map/all_to_all | solution.py:172
  84.4 8.5 %collective-permute-start.4 = (bf16[3,96,1408]{2,1,0:T(8,128)(2,1)S(1)}, bf16[3,96,1408]{2,1,0:T(8,128)(2,1)}, u32[]{:S(2)}, u32[]{:S(2)}) collective-permute-start(bf16[3,96,1408]{2,1,0:T(8,128)(2,1)S(1)} %dynamic_update_slice.10), channel_id=1, source_target_pairs={{0,32},{32,0},{64,96},{96,64},{128,160},{160,128},{192,224},{224,1... | collective-permute-start | bytes 2433032 | tf_op jit(solution)/shard_map/ppermute | solution.py:139
  95.0 3.0 %copy-start.4 = (bf16[3,96,1408]{2,1,0:T(8,128)(2,1)}, bf16[3,96,1408]{2,1,0:T(8,128)(2,1)S(1)}, u32[]{:S(2)}) copy-start(bf16[3,96,1408]{2,1,0:T(8,128)(2,1)S(1)} %get-tuple-element.13) | copy-start | bytes 2433028
  98.0 49.7 %all-to-all-start.3 = ((bf16[8,128,768]{2,1,0:T(8,128)(2,1)}), bf16[8,128,768]{2,1,0:T(8,128)(2,1)S(1)}, u32[]{:S(2)}, u32[]{:S(2)}) async-start(bf16[8,128,768]{2,1,0:T(8,128)(2,1)} %broadcast_in_dim.2), calls=%async_computation.3 | async-start | bytes 3145728 | tf_op jit(solution)/shard_map/all_to_all | solution.py:183
  106.7 1.4 copy-start.5
  108.8 9.3 %collective-permute-start.5 = (bf16[176,768]{1,0:T(8,128)(2,1)S(1)}, bf16[176,768]{1,0:T(8,128)(2,1)S(1)}, u32[]{:S(2)}, u32[]{:S(2)}) collective-permute-start(bf16[176,768]{1,0:T(8,128)(2,1)S(1)} %fusion.15), channel_id=1, source_target_pairs={{0,24},{1,25},{2,26},{3,27},{4,28},{5,29},{6,30},{7,31},{8,0},{9,1... | collective-permute-start | bytes 811016 | tf_op jit(solution)/shard_map/ppermute | solution.py:18
  112.2 5.8 %copy-start.10 = (s32[6]{0:T(128)S(1)}, s32[6]{0:T(128)}, u32[]{:S(2)}) copy-start(s32[6]{0:T(128)} %param.15) | copy-start | bytes 76
  112.2 9.6 %collective-permute-start.6 = (bf16[176,768]{1,0:T(8,128)(2,1)S(1)}, bf16[176,768]{1,0:T(8,128)(2,1)S(1)}, u32[]{:S(2)}, u32[]{:S(2)}) collective-permute-start(bf16[176,768]{1,0:T(8,128)(2,1)S(1)} %fusion.18), channel_id=1, source_target_pairs={{0,16},{1,17},{2,18},{3,19},{4,20},{5,21},{6,22},{7,23},{8,24},{9,... | collective-permute-start | bytes 811016 | tf_op jit(solution)/shard_map/ppermute | solution.py:18
  116.0 12.7 %collective-permute-start.7 = (bf16[176,768]{1,0:T(8,128)(2,1)S(1)}, bf16[176,768]{1,0:T(8,128)(2,1)S(1)}, u32[]{:S(2)}, u32[]{:S(2)}) collective-permute-start(bf16[176,768]{1,0:T(8,128)(2,1)S(1)} %fusion.21), channel_id=1, source_target_pairs={{0,8},{1,9},{2,10},{3,11},{4,12},{5,13},{6,14},{7,15},{8,16},{9,17... | collective-permute-start | bytes 811016 | tf_op jit(solution)/shard_map/ppermute | solution.py:18
  129.4 8.8 %collective-permute-start.10 = (bf16[176,768]{1,0:T(8,128)(2,1)S(1)}, bf16[176,768]{1,0:T(8,128)(2,1)S(1)}, u32[]{:S(2)}, u32[]{:S(2)}) collective-permute-start(bf16[176,768]{1,0:T(8,128)(2,1)S(1)} %multiply_convert_fusion.g0_ref), channel_id=1, source_target_pairs={{0,24},{1,25},{2,26},{3,27},{4,28},{5,29},{6,30},{7,31},{8,0},{9,1... | collective-permute-start | bytes 811016 | tf_op jit(solution)/shard_map/ppermute | solution.py:18
  131.3 9.0 %collective-permute-start.8 = (bf16[176,768]{1,0:T(8,128)(2,1)S(1)}, bf16[176,768]{1,0:T(8,128)(2,1)S(1)}, u32[]{:S(2)}, u32[]{:S(2)}) collective-permute-start(bf16[176,768]{1,0:T(8,128)(2,1)S(1)} %multiply_convert_fusion.g0_ref), channel_id=1, source_target_pairs={{0,8},{1,9},{2,10},{3,11},{4,12},{5,13},{6,14},{7,15},{8,16},{9,17... | collective-permute-start | bytes 811016 | tf_op jit(solution)/shard_map/ppermute | solution.py:18
  134.7 12.3 %collective-permute-start.9 = (bf16[176,768]{1,0:T(8,128)(2,1)S(1)}, bf16[176,768]{1,0:T(8,128)(2,1)S(1)}, u32[]{:S(2)}, u32[]{:S(2)}) collective-permute-start(bf16[176,768]{1,0:T(8,128)(2,1)S(1)} %multiply_convert_fusion.g0_ref), channel_id=1, source_target_pairs={{0,16},{1,17},{2,18},{3,19},{4,20},{5,21},{6,22},{7,23},{8,24},{9,... | collective-permute-start | bytes 811016 | tf_op jit(solution)/shard_map/ppermute | solution.py:18
  (3 other events, 2.8 us)
Sparse Core Ops, SparseCore 0:
  9.4 58.3 all-gather.5
  69.9 47.4 all-gather.3

commit v7 on v6

--- a/solution.py
+++ b/solution.py
@@ -159,27 +159,27 @@
     blocks = column_blocks(jnp.stack([kx, core]), out_basis_t)
     near = [shift_x(blocks[d], d) for d in range(1, NX)]
     tie = (near[0][:1, :1] + near[1][:1, :1] + near[2][:1, :1]) * 0
+    near = jnp.stack(near)
+    v_low, v_high = both_halves(near, core)
+    vs = [blocks[0]] + [jnp.concatenate([v_low[n], v_high[n, 2 * HALF - PAD :]]) for n in range(NX - 1)]
+
     pieces = lax.all_to_all(pieces, "dp", 0, 0, axis_index_groups=ZG)
     rows = NY * 128 // 2
     mine = lax.dynamic_index_in_dim(in_basis.reshape(NX, 2, rows, 128), core, 1, keepdims=False)
     mixed = jnp.concatenate([mine, pieces.reshape(NX, 2 * PAD, 128)], axis=1)
     mixed = lax.all_to_all(after(mixed, tie), "tensor", 0, 0, axis_index_groups=XG)
     u4 = jnp.stack(both_halves(mixed[:, :rows], core), axis=1)
-    pieces = mixed[:, rows:].reshape(NX, 2, PAD, 128)
+    pieces = after(mixed[:, rows:].reshape(NX, 2, PAD, 128), v_low[0, :1, :1] * 0)
     tiles = lax.all_gather(pieces, "dp").reshape(NZ, 2, NX, 2, PAD, 128)
 
     a_part = jnp.einsum("xyed,yte->xdt", u4.reshape(NX, NY, 128, 128), x8, preferred_element_type=f32).astype(bf)
     a_parts = lax.all_to_all(a_part, "tensor", 0, 0, axis_index_groups=XG)
 
-    near = after(jnp.stack(near), a_part[0, :1, :1] * 0)
-    v_low, v_high = both_halves(near, core)
-    vs = [blocks[0]] + [jnp.concatenate([v_low[n], v_high[n, 2 * HALF - PAD :]]) for n in range(NX - 1)]
     y8 = y8.transpose(0, 2, 1, 3).reshape(NY * PAD, tokens)
     g_parts = [jnp.dot(v, y8, preferred_element_type=f32).astype(bf) for v in vs]
     g_parts = [g_parts[0]] + [shift_x(g_parts[d], -d) for d in range(1, NX)]
 
-    at = after(add_parts(a_parts).astype(bf), v_low[0, :1, :1] * 0)
-    at = jnp.broadcast_to(at, (NY, 128, tokens))
+    at = jnp.broadcast_to(add_parts(a_parts).astype(bf), (NY, 128, tokens))
     at = lax.all_to_all(at, "tensor", 0, 0, axis_index_groups=YG)
 
     position = lax.broadcasted_iota(jnp.int32, (seqs, seq_len), 1)

time: 183 us -> 176 us (0.962)
  waiting for transfers between devices: 32.2 us -> 26.5 us
  local copies, waits for them, and re-layouts: 14.6 us -> 17.8 us
  starting transfers between devices: 55.1 us -> 57.8 us
  other arithmetic: 8.69 us -> 6.5 us
  blocking collectives: 31.6 us -> 29.7 us
    ppermute x9, waiting for transfers between devices: 25 us -> 16.7 us  [shift_x(): return lax.ppermute(array, 'tensor', perm)]
    unnamed x22 -> x20, local copies, waits for them, and re-layouts: 2.24 us -> 5.99 us
    ppermute x2, starting transfers between devices: 6.62 us -> 9.98 us  [both_halves(): other = lax.ppermute(mine, 'dp', [(n, n ^ 1) for n in range(2 * NZ)])]
    all_to_all x1, waiting for transfers between devices: 0.01 us -> 2.16 us  [local(): pieces = lax.all_to_all(pieces, 'dp', 0, 0, axis_index_groups=ZG)]
    slice x4 -> x3, local copies, waits for them, and re-layouts: 2.49 us -> 0.63 us  [the longest x1 0.54 us: local(): v_low[0, :1, :1] * 0]
  transfers between devices with their start and end apart: 16 -> 16, of which waited for: 7 -> 7; matrix products, arithmetic and copies ran while one was open for 15% -> 13% of each run, Pallas kernels for 1% -> 1%
where the time goes in v7:
time: 176 us; the launch traced here: 172 us
  starting transfers between devices  57.8 us (33%)
  blocking collectives  29.7 us (17%)
  waiting for transfers between devices  26.5 us (15%)
  between operations  18.2 us (10%)
  local copies, waits for them, and re-layouts  17.8 us (10%)
  Pallas kernels  10.8 us (6%)
  other arithmetic  6.5 us (4%)
  matrix products  4.89 us (3%)
    ppermute x9, starting transfers between devices, shift_x(): return lax.ppermute(array, 'tensor', perm)  27.5 us
    ppermute x9, waiting for transfers between devices, shift_x(): return lax.ppermute(array, 'tensor', perm)  16.7 us
    all_to_all x1, blocking collectives, local(): lax.all_to_all(tile, 'tensor', 0, 0, tiled=True).sum(0)[:seqs * queries]  15.3 us
    all_to_all x1, blocking collectives, local(): a_parts = lax.all_to_all(a_part, 'tensor', 0, 0, axis_index_groups=XG)  14.4 us
    all_to_all x1, starting transfers between devices, local(): pieces = lax.all_to_all(pieces, 'dp', 0, 0, axis_index_groups=ZG)  10.1 us
    ppermute x2, starting transfers between devices, both_halves(): other = lax.ppermute(mine, 'dp', [(n, n ^ 1) for n in range(2 * NZ)])  9.98 us
    pallas_call x1, Pallas kernels, score_tiles(): pl.pallas_call(score_kernel, grid=(queries,), out_shape=jax.ShapeDtypeStr...  7.18 us
    all_to_all x1, starting transfers between devices, local(): at = lax.all_to_all(at, 'tensor', 0, 0, axis_index_groups=YG)  6.8 us
  transfers between devices with their start and end apart: 16, of which 7 were waited for; matrix products, arithmetic and copies ran while one was open for 13% of the time, Pallas kernels for 1%

profile of v7, /device:TPU:1, one launch (start us, length us, event | category | flops | bytes accessed | tf_op | source)
XLA Modules:
  0.0 172.2 jit_solution(14209491938220495932)
XLA Ops:
  11.9 3.9 %collective-permute-start = (bf16[96,1408]{1,0:T(8,128)(2,1)S(1)}, bf16[96,1408]{1,0:T(8,128)(2,1)S(1)}, u32[]{:S(2)}, u32[]{:S(2)}) collective-permute-start(bf16[96,1408]{1,0:T(8,128)(2,1)S(1)} %get-tuple-element.10), channel_id=1, source_target_pairs={{0,8},{1,9},{2,10},{3,11},{4,12},{5,13},{6,14},{7,15},{8,16},{9,17... | collective-permute-start | bytes 811016 | tf_op jit(solution)/shard_map/ppermute | solution.py:18
  15.8 4.4 %collective-permute-start.1 = (bf16[96,1408]{1,0:T(8,128)(2,1)S(1)}, bf16[96,1408]{1,0:T(8,128)(2,1)S(1)}, u32[]{:S(2)}, u32[]{:S(2)}) collective-permute-start(bf16[96,1408]{1,0:T(8,128)(2,1)S(1)} %get-tuple-element.11), channel_id=1, source_target_pairs={{0,16},{1,17},{2,18},{3,19},{4,20},{5,21},{6,22},{7,23},{8,24},{9,... | collective-permute-start | bytes 811016 | tf_op jit(solution)/shard_map/ppermute | solution.py:18
  20.2 3.1 %collective-permute-start.2 = (bf16[96,1408]{1,0:T(8,128)(2,1)S(1)}, bf16[96,1408]{1,0:T(8,128)(2,1)S(1)}, u32[]{:S(2)}, u32[]{:S(2)}) collective-permute-start(bf16[96,1408]{1,0:T(8,128)(2,1)S(1)} %get-tuple-element.12), channel_id=1, source_target_pairs={{0,24},{1,25},{2,26},{3,27},{4,28},{5,29},{6,30},{7,31},{8,0},{9,1... | collective-permute-start | bytes 811016 | tf_op jit(solution)/shard_map/ppermute | solution.py:18
  25.8 10.1 %all-to-all-start = ((bf16[8,176,128]{2,1,0:T(8,128)(2,1)}), bf16[8,176,128]{2,1,0:T(8,128)(2,1)S(1)}, u32[]{:S(2)}, u32[]{:S(2)}) async-start(bf16[8,176,128]{2,1,0:T(8,128)(2,1)} %bitcast.18), calls=%async_computation | async-start | bytes 720896 | tf_op jit(solution)/shard_map/all_to_all | solution.py:166
  36.9 3.7 %collective-permute-start.3 = (bf16[3,96,1408]{2,1,0:T(8,128)(2,1)}, bf16[3,96,1408]{2,1,0:T(8,128)(2,1)}, u32[]{:S(2)}, u32[]{:S(2)}) collective-permute-start(bf16[3,96,1408]{2,1,0:T(8,128)(2,1)} %pad_maximum_fusion.2), channel_id=1, source_target_pairs={{0,32},{32,0},{64,96},{96,64},{128,160},{160,128},{192,224},{224,1... | collective-permute-start | bytes 2433032 | tf_op jit(solution)/shard_map/ppermute | solution.py:139
  45.4 2.2 %all-to-all-done = bf16[8,176,128]{2,1,0:T(8,128)(2,1)S(1)} async-done(((bf16[8,176,128]{2,1,0:T(8,128)(2,1)}), bf16[8,176,128]{2,1,0:T(8,128)(2,1)S(1)}, u32[]{:S(2)}, u32[]{:S(2)}) %all-to-all-start) | async-done | bytes 360480 | tf_op jit(solution)/shard_map/all_to_all | solution.py:166
  49.8 3.5 %all-to-all-start.1 = ((bf16[4,864,128]{2,1,0:T(8,128)(2,1)}), bf16[4,864,128]{2,1,0:T(8,128)(2,1)S(1)}, u32[]{:S(2)}, u32[]{:S(2)}) async-start(bf16[4,864,128]{2,1,0:T(8,128)(2,1)} %dynamic_update_slice.7), calls=%async_computation.1 | async-start | bytes 1769472 | tf_op jit(solution)/shard_map/all_to_all | solution.py:170
  53.4 2.2 %broadcast_select_fusion.1 = (bf16[3,96,1408]{2,1,0:T(8,128)(2,1)S(1)}, bf16[3,96,1408]{2,1,0:T(8,128)(2,1)}) fusion(bf16[3,96,1408]{2,1,0:T(8,128)(2,1)} %collective-permute-done.3, pred[]{:T(512)S(6)} %eq.2, bf16[1,96,1408]{2,1,0:T(8,128)(2,1)S(1)} %bitcast.99, bf16[1,96,1408]{2,1,0:T(8,128)(2,1)S(1)} %bitcast.97, bf16[1,96,1408]{2,1,0:T(8,128)(2,1)S(1)} %bitcast.95), kind=kLoop, calls=%fused_computation.20 | loop fusion | flops 1622016 | bytes 3244033 | tf_op jit(solution)/shard_map/jit(_where)/select_n | solution.py:140
  57.1 6.0 %all-to-all-done.1 = bf16[4,864,128]{2,1,0:T(8,128)(2,1)S(1)} async-done(((bf16[4,864,128]{2,1,0:T(8,128)(2,1)}), bf16[4,864,128]{2,1,0:T(8,128)(2,1)S(1)}, u32[]{:S(2)}, u32[]{:S(2)}) %all-to-all-start.1) | async-done | bytes 884768 | tf_op jit(solution)/shard_map/all_to_all | solution.py:170
  65.2 6.3 %collective-permute-start.10 = (bf16[4,512,128]{2,1,0:T(8,128)(2,1)S(1)}, bf16[4,512,128]{2,1,0:T(8,128)(2,1)S(1)}, u32[]{:S(2)}, u32[]{:S(2)}) collective-permute-start(bf16[4,512,128]{2,1,0:T(8,128)(2,1)S(1)} %slice.111), channel_id=1, source_target_pairs={{0,32},{32,0},{64,96},{96,64},{128,160},{160,128},{192,224},{224,1... | collective-permute-start | bytes 1572872 | tf_op jit(solution)/shard_map/ppermute | solution.py:139
  73.4 2.5 %bitcast_convert_fusion = bf16[4,128,768]{2,1,0:T(8,128)(2,1)S(1)} fusion(bf16[4,8,128,128]{3,2,1,0:T(8,128)(2,1)S(1)} %bitcast.100, bf16[8,1824,128]{2,1,0:T(8,128)(2,1)} %bitcast.92), kind=kOutput, calls=%fused_computation.10 | convolution fusion | flops 805699584 | bytes 3407872 | tf_op jit(solution)/shard_map/xyed,yte->xdt/dot_general | solution.py:175
  75.8 14.4 %all_to_all.29 = bf16[4,128,768]{2,1,0:T(8,128)(2,1)S(1)} all-to-all(bf16[4,128,768]{2,1,0:T(8,128)(2,1)S(1)} %bitcast_convert_fusion), channel_id=1, replica_groups={{0,8,16,24},{1,9,17,25},{2,10,18,26},{3,11,19,27},{4,12,20,28},{5,13,21..., dimensions={0} | all-to-all | bytes 1572864 | tf_op jit(solution)/shard_map/all_to_all | solution.py:176
  91.6 6.8 %all-to-all-start.3 = ((bf16[8,128,768]{2,1,0:T(8,128)(2,1)}), bf16[8,128,768]{2,1,0:T(8,128)(2,1)S(1)}, u32[]{:S(2)}, u32[]{:S(2)}) async-start(bf16[8,128,768]{2,1,0:T(8,128)(2,1)} %broadcast_in_dim.2), calls=%async_computation.3 | async-start | bytes 3145728 | tf_op jit(solution)/shard_map/all_to_all | solution.py:183
  104.0 2.4 %collective-permute-start.5 = (bf16[176,768]{1,0:T(8,128)(2,1)S(1)}, bf16[176,768]{1,0:T(8,128)(2,1)S(1)}, u32[]{:S(2)}, u32[]{:S(2)}) collective-permute-start(bf16[176,768]{1,0:T(8,128)(2,1)S(1)} %fusion.18), channel_id=1, source_target_pairs={{0,16},{1,17},{2,18},{3,19},{4,20},{5,21},{6,22},{7,23},{8,24},{9,... | collective-permute-start | bytes 811016 | tf_op jit(solution)/shard_map/ppermute | solution.py:18
  107.0 2.9 %collective-permute-start.6 = (bf16[176,768]{1,0:T(8,128)(2,1)S(1)}, bf16[176,768]{1,0:T(8,128)(2,1)S(1)}, u32[]{:S(2)}, u32[]{:S(2)}) collective-permute-start(bf16[176,768]{1,0:T(8,128)(2,1)S(1)} %fusion.21), channel_id=1, source_target_pairs={{0,8},{1,9},{2,10},{3,11},{4,12},{5,13},{6,14},{7,15},{8,16},{9,17... | collective-permute-start | bytes 811016 | tf_op jit(solution)/shard_map/ppermute | solution.py:18
  110.6 3.6 %collective-permute-start.4 = (bf16[176,768]{1,0:T(8,128)(2,1)S(1)}, bf16[176,768]{1,0:T(8,128)(2,1)S(1)}, u32[]{:S(2)}, u32[]{:S(2)}) collective-permute-start(bf16[176,768]{1,0:T(8,128)(2,1)S(1)} %fusion.15), channel_id=1, source_target_pairs={{0,24},{1,25},{2,26},{3,27},{4,28},{5,29},{6,30},{7,31},{8,0},{9,1... | collective-permute-start | bytes 811016 | tf_op jit(solution)/shard_map/ppermute | solution.py:18
  114.2 6.8 %collective-permute-done.6 = bf16[176,768]{1,0:T(8,128)(2,1)S(1)} collective-permute-done((bf16[176,768]{1,0:T(8,128)(2,1)S(1)}, bf16[176,768]{1,0:T(8,128)(2,1)S(1)}, u32[]{:S(2)}, u32[]{:S(2)}) %collective-permute-start.6) | collective-permute-done | bytes 270368 | tf_op jit(solution)/shard_map/ppermute | solution.py:18
  121.7 2.1 %collective-permute-start.9 = (bf16[176,768]{1,0:T(8,128)(2,1)S(1)}, bf16[176,768]{1,0:T(8,128)(2,1)S(1)}, u32[]{:S(2)}, u32[]{:S(2)}) collective-permute-start(bf16[176,768]{1,0:T(8,128)(2,1)S(1)} %multiply_convert_fusion.g0_ref), channel_id=1, source_target_pairs={{0,24},{1,25},{2,26},{3,27},{4,28},{5,29},{6,30},{7,31},{8,0},{9,1... | collective-permute-start | bytes 811016 | tf_op jit(solution)/shard_map/ppermute | solution.py:18
  123.7 2.1 %collective-permute-start.8 = (bf16[176,768]{1,0:T(8,128)(2,1)S(1)}, bf16[176,768]{1,0:T(8,128)(2,1)S(1)}, u32[]{:S(2)}, u32[]{:S(2)}) collective-permute-start(bf16[176,768]{1,0:T(8,128)(2,1)S(1)} %multiply_convert_fusion.g0_ref), channel_id=1, source_target_pairs={{0,16},{1,17},{2,18},{3,19},{4,20},{5,21},{6,22},{7,23},{8,24},{9,... | collective-permute-start | bytes 811016 | tf_op jit(solution)/shard_map/ppermute | solution.py:18
  125.8 3.0 %collective-permute-start.7 = (bf16[176,768]{1,0:T(8,128)(2,1)S(1)}, bf16[176,768]{1,0:T(8,128)(2,1)S(1)}, u32[]{:S(2)}, u32[]{:S(2)}) collective-permute-start(bf16[176,768]{1,0:T(8,128)(2,1)S(1)} %multiply_convert_fusion.g0_ref), channel_id=1, source_target_pairs={{0,8},{1,9},{2,10},{3,11},{4,12},{5,13},{6,14},{7,15},{8,16},{9,17... | collective-permute-start | bytes 811016 | tf_op jit(solution)/shard_map/ppermute | solution.py:18
  130.4 2.3 %collective-permute-done.8.g2_ref = bf16[176,768]{1,0:T(8,128)(2,1)S(1)} collective-permute-done((bf16[176,768]{1,0:T(8,128)(2,1)S(1)}, bf16[176,768]{1,0:T(8,128)(2,1)S(1)}, u32[]{:S(2)}, u32[]{:S(2)}) %collective-permute-start.8) | collective-permute-done | bytes 270368 | tf_op jit(solution)/shard_map/ppermute | solution.py:18
  133.4 6.0 %collective-permute-done.7.g1_ref = bf16[176,768]{1,0:T(8,128)(2,1)S(1)} collective-permute-done((bf16[176,768]{1,0:T(8,128)(2,1)S(1)}, bf16[176,768]{1,0:T(8,128)(2,1)S(1)}, u32[]{:S(2)}, u32[]{:S(2)}) %collective-permute-start.7) | collective-permute-done | bytes 270368 | tf_op jit(solution)/shard_map/ppermute | solution.py:18
  142.1 7.2 %shard_map.84 = f32[32,128]{1,0:T(8,128)S(1)} custom-call(s32[1]{0:T(128)} %bitcast.kx_ref, bf16[176,768]{1,0:T(8,128)(2,1)S(1)} %multiply_convert_fusion.g0_ref, bf16[176,768]{1,0:T(8,128)(2,1)S(1)} %copy-done.5, bf16[176,768]{1,0:T(8,128)(2,1)S(1)} %copy-done.3, bf16[176,768]{1,0:T(8,128)(2,1)S(1)} %collective-permute-done.9.g3_ref, ...), custom_call_target="tpu_custom_call" | custom-call | flops 4429185024 | bytes 9000000 | tf_op jit(solution)/shard_map/pallas_call | solution.py:111
  149.3 15.3 %all_to_all.30 = f32[32,1,128]{2,1,0:T(1,128)S(1)} all-to-all(f32[32,1,128]{2,1,0:T(1,128)S(1)} %bitcast.83), channel_id=1, replica_groups=mesh['dp'=16,'tensor'=32] {'tensor'}, dimensions={0} | all-to-all | bytes 32768 | tf_op jit(solution)/shard_map/all_to_all | solution.py:191
  (73 shorter events, 31.3 us)
Async XLA Ops:
  6.5 34.0 %copy-start = (bf16[4096,128]{1,0:T(8,128)(2,1)S(1)}, bf16[4096,128]{1,0:T(8,128)(2,1)}, u32[]{:S(2)}) copy-start(bf16[4096,128]{1,0:T(8,128)(2,1)} %param.10) | copy-start | bytes 3145732
  6.5 18.3 %copy-start.8 = (bf16[4,172,256]{2,0,1:T(4,128)(2,1)S(1)}, bf16[4,172,256]{2,0,1:T(4,128)(2,1)}, u32[]{:S(2)}) copy-start(bf16[4,172,256]{2,0,1:T(4,128)(2,1)} %param.12) | copy-start | bytes 1056772
  6.5 66.8 %all-gather.6.cloned.1.call-start = ((), (), s32[]{:S(2)}) async-start(), calls=%async_computation.6 | async-start | bytes 4202496 | tf_op jit(solution)/shard_map/all_gather | solution.py:152
  8.6 1.5 copy-start.1
  11.9 24.0 %collective-permute-start = (bf16[96,1408]{1,0:T(8,128)(2,1)S(1)}, bf16[96,1408]{1,0:T(8,128)(2,1)S(1)}, u32[]{:S(2)}, u32[]{:S(2)}) collective-permute-start(bf16[96,1408]{1,0:T(8,128)(2,1)S(1)} %get-tuple-element.10), channel_id=1, source_target_pairs={{0,8},{1,9},{2,10},{3,11},{4,12},{5,13},{6,14},{7,15},{8,16},{9,17... | collective-permute-start | bytes 811016 | tf_op jit(solution)/shard_map/ppermute | solution.py:18
  15.8 20.0 %collective-permute-start.1 = (bf16[96,1408]{1,0:T(8,128)(2,1)S(1)}, bf16[96,1408]{1,0:T(8,128)(2,1)S(1)}, u32[]{:S(2)}, u32[]{:S(2)}) collective-permute-start(bf16[96,1408]{1,0:T(8,128)(2,1)S(1)} %get-tuple-element.11), channel_id=1, source_target_pairs={{0,16},{1,17},{2,18},{3,19},{4,20},{5,21},{6,22},{7,23},{8,24},{9,... | collective-permute-start | bytes 811016 | tf_op jit(solution)/shard_map/ppermute | solution.py:18
  20.2 15.7 %collective-permute-start.2 = (bf16[96,1408]{1,0:T(8,128)(2,1)S(1)}, bf16[96,1408]{1,0:T(8,128)(2,1)S(1)}, u32[]{:S(2)}, u32[]{:S(2)}) collective-permute-start(bf16[96,1408]{1,0:T(8,128)(2,1)S(1)} %get-tuple-element.12), channel_id=1, source_target_pairs={{0,24},{1,25},{2,26},{3,27},{4,28},{5,29},{6,30},{7,31},{8,0},{9,1... | collective-permute-start | bytes 811016 | tf_op jit(solution)/shard_map/ppermute | solution.py:18
  25.8 21.8 %all-to-all-start = ((bf16[8,176,128]{2,1,0:T(8,128)(2,1)}), bf16[8,176,128]{2,1,0:T(8,128)(2,1)S(1)}, u32[]{:S(2)}, u32[]{:S(2)}) async-start(bf16[8,176,128]{2,1,0:T(8,128)(2,1)} %bitcast.18), calls=%async_computation | async-start | bytes 720896 | tf_op jit(solution)/shard_map/all_to_all | solution.py:166
  36.9 16.5 %collective-permute-start.3 = (bf16[3,96,1408]{2,1,0:T(8,128)(2,1)}, bf16[3,96,1408]{2,1,0:T(8,128)(2,1)}, u32[]{:S(2)}, u32[]{:S(2)}) collective-permute-start(bf16[3,96,1408]{2,1,0:T(8,128)(2,1)} %pad_maximum_fusion.2), channel_id=1, source_target_pairs={{0,32},{32,0},{64,96},{96,64},{128,160},{160,128},{192,224},{224,1... | collective-permute-start | bytes 2433032 | tf_op jit(solution)/shard_map/ppermute | solution.py:139
  49.8 13.4 %all-to-all-start.1 = ((bf16[4,864,128]{2,1,0:T(8,128)(2,1)}), bf16[4,864,128]{2,1,0:T(8,128)(2,1)S(1)}, u32[]{:S(2)}, u32[]{:S(2)}) async-start(bf16[4,864,128]{2,1,0:T(8,128)(2,1)} %dynamic_update_slice.7), calls=%async_computation.1 | async-start | bytes 1769472 | tf_op jit(solution)/shard_map/all_to_all | solution.py:170
  53.3 86.9 %all-gather.4.cloned.1.call-start = ((), (), s32[]{:S(2)}) async-start(), calls=%async_computation.5 | async-start | bytes 6127616 | tf_op jit(solution)/shard_map/all_gather | solution.py:173
  55.6 0.9 copy-start.6
  64.4 0.8 copy-start.7
  65.2 7.8 %collective-permute-start.10 = (bf16[4,512,128]{2,1,0:T(8,128)(2,1)S(1)}, bf16[4,512,128]{2,1,0:T(8,128)(2,1)S(1)}, u32[]{:S(2)}, u32[]{:S(2)}) collective-permute-start(bf16[4,512,128]{2,1,0:T(8,128)(2,1)S(1)} %slice.111), channel_id=1, source_target_pairs={{0,32},{32,0},{64,96},{96,64},{128,160},{160,128},{192,224},{224,1... | collective-permute-start | bytes 1572872 | tf_op jit(solution)/shard_map/ppermute | solution.py:139
  91.6 48.6 %all-to-all-start.3 = ((bf16[8,128,768]{2,1,0:T(8,128)(2,1)}), bf16[8,128,768]{2,1,0:T(8,128)(2,1)S(1)}, u32[]{:S(2)}, u32[]{:S(2)}) async-start(bf16[8,128,768]{2,1,0:T(8,128)(2,1)} %broadcast_in_dim.2), calls=%async_computation.3 | async-start | bytes 3145728 | tf_op jit(solution)/shard_map/all_to_all | solution.py:183
  104.0 10.2 %collective-permute-start.5 = (bf16[176,768]{1,0:T(8,128)(2,1)S(1)}, bf16[176,768]{1,0:T(8,128)(2,1)S(1)}, u32[]{:S(2)}, u32[]{:S(2)}) collective-permute-start(bf16[176,768]{1,0:T(8,128)(2,1)S(1)} %fusion.18), channel_id=1, source_target_pairs={{0,16},{1,17},{2,18},{3,19},{4,20},{5,21},{6,22},{7,23},{8,24},{9,... | collective-permute-start | bytes 811016 | tf_op jit(solution)/shard_map/ppermute | solution.py:18
  107.0 7.1 %copy-start.9 = (s32[6]{0:T(128)S(1)}, s32[6]{0:T(128)}, u32[]{:S(2)}) copy-start(s32[6]{0:T(128)} %param.15) | copy-start | bytes 76
  107.0 14.0 %collective-permute-start.6 = (bf16[176,768]{1,0:T(8,128)(2,1)S(1)}, bf16[176,768]{1,0:T(8,128)(2,1)S(1)}, u32[]{:S(2)}, u32[]{:S(2)}) collective-permute-start(bf16[176,768]{1,0:T(8,128)(2,1)S(1)} %fusion.21), channel_id=1, source_target_pairs={{0,8},{1,9},{2,10},{3,11},{4,12},{5,13},{6,14},{7,15},{8,16},{9,17... | collective-permute-start | bytes 811016 | tf_op jit(solution)/shard_map/ppermute | solution.py:18
  110.6 10.4 %collective-permute-start.4 = (bf16[176,768]{1,0:T(8,128)(2,1)S(1)}, bf16[176,768]{1,0:T(8,128)(2,1)S(1)}, u32[]{:S(2)}, u32[]{:S(2)}) collective-permute-start(bf16[176,768]{1,0:T(8,128)(2,1)S(1)} %fusion.15), channel_id=1, source_target_pairs={{0,24},{1,25},{2,26},{3,27},{4,28},{5,29},{6,30},{7,31},{8,0},{9,1... | collective-permute-start | bytes 811016 | tf_op jit(solution)/shard_map/ppermute | solution.py:18
  121.7 8.8 %collective-permute-start.9 = (bf16[176,768]{1,0:T(8,128)(2,1)S(1)}, bf16[176,768]{1,0:T(8,128)(2,1)S(1)}, u32[]{:S(2)}, u32[]{:S(2)}) collective-permute-start(bf16[176,768]{1,0:T(8,128)(2,1)S(1)} %multiply_convert_fusion.g0_ref), channel_id=1, source_target_pairs={{0,24},{1,25},{2,26},{3,27},{4,28},{5,29},{6,30},{7,31},{8,0},{9,1... | collective-permute-start | bytes 811016 | tf_op jit(solution)/shard_map/ppermute | solution.py:18
  123.7 9.0 %collective-permute-start.8 = (bf16[176,768]{1,0:T(8,128)(2,1)S(1)}, bf16[176,768]{1,0:T(8,128)(2,1)S(1)}, u32[]{:S(2)}, u32[]{:S(2)}) collective-permute-start(bf16[176,768]{1,0:T(8,128)(2,1)S(1)} %multiply_convert_fusion.g0_ref), channel_id=1, source_target_pairs={{0,16},{1,17},{2,18},{3,19},{4,20},{5,21},{6,22},{7,23},{8,24},{9,... | collective-permute-start | bytes 811016 | tf_op jit(solution)/shard_map/ppermute | solution.py:18
  125.8 13.6 %collective-permute-start.7 = (bf16[176,768]{1,0:T(8,128)(2,1)S(1)}, bf16[176,768]{1,0:T(8,128)(2,1)S(1)}, u32[]{:S(2)}, u32[]{:S(2)}) collective-permute-start(bf16[176,768]{1,0:T(8,128)(2,1)S(1)} %multiply_convert_fusion.g0_ref), channel_id=1, source_target_pairs={{0,8},{1,9},{2,10},{3,11},{4,12},{5,13},{6,14},{7,15},{8,16},{9,17... | collective-permute-start | bytes 811016 | tf_op jit(solution)/shard_map/ppermute | solution.py:18
  140.2 1.0 copy-start.3
  141.1 1.0 copy-start.5
  (2 other events, 1.4 us)
Sparse Core Ops, SparseCore 0:
  9.4 58.3 all-gather.5
  69.9 47.4 all-gather.3

commit v8 on v7

--- a/solution.py
+++ b/solution.py
@@ -107,15 +107,15 @@
 def score_tiles(kx, gs, at, tiles):
     tokens = at.shape[1]
     queries = tiles.shape[0] // 2
-    whole = lambda q: (0, 0)
+    whole = pl.BlockSpec(memory_space=pltpu.VMEM)
     return pl.pallas_call(
         score_kernel,
         grid=(queries,),
         out_shape=jax.ShapeDtypeStruct((NX * NY, 128), jnp.float32),
         in_specs=[pl.BlockSpec(memory_space=pltpu.SMEM)]
-        + [pl.BlockSpec((PAD, tokens), whole)] * NX
-        + [pl.BlockSpec(at.shape, whole), pl.BlockSpec((2,) + tiles.shape[1:], lambda q: (q, 0, 0, 0, 0, 0))],
-        out_specs=pl.BlockSpec((NX * NY, 128), whole),
+        + [whole] * (NX + 1)
+        + [pl.BlockSpec((2,) + tiles.shape[1:], lambda q: (q, 0, 0, 0, 0, 0))],
+        out_specs=whole,
         scratch_shapes=[pltpu.VMEM((NX * PAD, NY * 128), jnp.bfloat16)],
         compiler_params=pltpu.CompilerParams(vmem_limit_bytes=48 * 1024 * 1024),
         cost_estimate=pl.CostEstimate(
@@ -175,11 +175,11 @@
     a_part = jnp.einsum("xyed,yte->xdt", u4.reshape(NX, NY, 128, 128), x8, preferred_element_type=f32).astype(bf)
     a_parts = lax.all_to_all(a_part, "tensor", 0, 0, axis_index_groups=XG)
 
-    y8 = y8.transpose(0, 2, 1, 3).reshape(NY * PAD, tokens)
+    y8 = after(y8.transpose(0, 2, 1, 3).reshape(NY * PAD, tokens), a_part[0, :1, :1] * 0)
     g_parts = [jnp.dot(v, y8, preferred_element_type=f32).astype(bf) for v in vs]
     g_parts = [g_parts[0]] + [shift_x(g_parts[d], -d) for d in range(1, NX)]
 
-    at = jnp.broadcast_to(add_parts(a_parts).astype(bf), (NY, 128, tokens))
+    at = jnp.broadcast_to(after(add_parts(a_parts).astype(bf), y8[:1, :1] * 0), (NY, 128, tokens))
     at = lax.all_to_all(at, "tensor", 0, 0, axis_index_groups=YG)
 
     position = lax.broadcasted_iota(jnp.int32, (seqs, seq_len), 1)

time: 176 us -> 184 us (1.045); the launches traced: 172 us -> 183 us
  blocking collectives: 29.7 us -> 18 us
  local copies, waits for them, and re-layouts: 17.8 us -> 24.9 us
  starting transfers between devices: 57.8 us -> 64.3 us
  waiting for transfers between devices: 26.5 us -> 31.7 us
  matrix products: 4.89 us -> 7.79 us
  between operations: 18.2 us -> 20.1 us
    all_to_all x1 -> x0, blocking collectives: 14.4 us -> none  [local(): a_parts = lax.all_to_all(a_part, 'tensor', 0, 0, axis_index_groups=XG)]
    all_to_all x0 -> x1, waiting for transfers between devices: none -> 4.71 us  [local(): a_parts = lax.all_to_all(a_part, 'tensor', 0, 0, axis_index_groups=XG)]
    all_to_all x0 -> x1, starting transfers between devices: none -> 3.49 us  [local(): a_parts = lax.all_to_all(a_part, 'tensor', 0, 0, axis_index_groups=XG)]
    ppermute x9, starting transfers between devices: 27.5 us -> 30.3 us  [shift_x(): return lax.ppermute(array, 'tensor', perm)]
    all_to_all x1, blocking collectives: 15.3 us -> 18 us  [local(): lax.all_to_all(tile, 'tensor', 0, 0, tiled=True).sum(0)[:seqs * queries]]
    dot_general x4, matrix products: 2.43 us -> 4.43 us  [local(): jnp.dot(v, y8, preferred_element_type=f32).astype(bf)]
    unnamed x20 -> x33, local copies, waits for them, and re-layouts: 5.99 us -> 7.81 us
  transfers between devices with their start and end apart: 16 -> 17, of which waited for: 7 -> 10; matrix products, arithmetic and copies ran while one was open for 13% -> 16% of each run, Pallas kernels for 1% -> 1%
where the time goes in v8:
time: 184 us; the launch traced here: 183 us
  starting transfers between devices  64.3 us (35%)
  waiting for transfers between devices  31.7 us (17%)
  local copies, waits for them, and re-layouts  24.9 us (14%)
  between operations  20.1 us (11%)
  blocking collectives  18 us (10%)
  Pallas kernels  10.9 us (6%)
  matrix products  7.79 us (4%)
  other arithmetic  5.61 us (3%)
    ppermute x9, starting transfers between devices, shift_x(): return lax.ppermute(array, 'tensor', perm)  30.3 us
    all_to_all x1, blocking collectives, local(): lax.all_to_all(tile, 'tensor', 0, 0, tiled=True).sum(0)[:seqs * queries]  18 us
    ppermute x9, waiting for transfers between devices, shift_x(): return lax.ppermute(array, 'tensor', perm)  17.4 us
    all_to_all x1, starting transfers between devices, local(): pieces = lax.all_to_all(pieces, 'dp', 0, 0, axis_index_groups=ZG)  10 us
    ppermute x2, starting transfers between devices, both_halves(): other = lax.ppermute(mine, 'dp', [(n, n ^ 1) for n in range(2 * NZ)])  10 us
    unnamed x33, local copies, waits for them, and re-layouts  7.81 us
    pallas_call x1, Pallas kernels, score_tiles(): pl.pallas_call(score_kernel, grid=(queries,), out_shape=jax.ShapeDtypeStr...  7.17 us
    all_to_all x1, starting transfers between devices, local(): at = lax.all_to_all(at, 'tensor', 0, 0, axis_index_groups=YG)  6.83 us
  transfers between devices with their start and end apart: 17, of which 10 were waited for; matrix products, arithmetic and copies ran while one was open for 16% of the time, Pallas kernels for 1%

profile of v8, /device:TPU:1, one launch (start us, length us, event | category | flops | bytes accessed | tf_op | source)
XLA Modules:
  0.0 183.2 jit_solution(11506751833563620641)
XLA Ops:
  11.9 3.9 %collective-permute-start = (bf16[96,1408]{1,0:T(8,128)(2,1)S(1)}, bf16[96,1408]{1,0:T(8,128)(2,1)S(1)}, u32[]{:S(2)}, u32[]{:S(2)}) collective-permute-start(bf16[96,1408]{1,0:T(8,128)(2,1)S(1)} %get-tuple-element.10), channel_id=1, source_target_pairs={{0,8},{1,9},{2,10},{3,11},{4,12},{5,13},{6,14},{7,15},{8,16},{9,17... | collective-permute-start | bytes 811016 | tf_op jit(solution)/shard_map/ppermute | solution.py:18
  15.8 4.4 %collective-permute-start.1 = (bf16[96,1408]{1,0:T(8,128)(2,1)S(1)}, bf16[96,1408]{1,0:T(8,128)(2,1)S(1)}, u32[]{:S(2)}, u32[]{:S(2)}) collective-permute-start(bf16[96,1408]{1,0:T(8,128)(2,1)S(1)} %get-tuple-element.11), channel_id=1, source_target_pairs={{0,16},{1,17},{2,18},{3,19},{4,20},{5,21},{6,22},{7,23},{8,24},{9,... | collective-permute-start | bytes 811016 | tf_op jit(solution)/shard_map/ppermute | solution.py:18
  20.2 3.1 %collective-permute-start.2 = (bf16[96,1408]{1,0:T(8,128)(2,1)S(1)}, bf16[96,1408]{1,0:T(8,128)(2,1)S(1)}, u32[]{:S(2)}, u32[]{:S(2)}) collective-permute-start(bf16[96,1408]{1,0:T(8,128)(2,1)S(1)} %get-tuple-element.12), channel_id=1, source_target_pairs={{0,24},{1,25},{2,26},{3,27},{4,28},{5,29},{6,30},{7,31},{8,0},{9,1... | collective-permute-start | bytes 811016 | tf_op jit(solution)/shard_map/ppermute | solution.py:18
  24.9 10.0 %all-to-all-start = ((bf16[8,176,128]{2,1,0:T(8,128)(2,1)}), bf16[8,176,128]{2,1,0:T(8,128)(2,1)S(1)}, u32[]{:S(2)}, u32[]{:S(2)}) async-start(bf16[8,176,128]{2,1,0:T(8,128)(2,1)} %bitcast.8), calls=%async_computation | async-start | bytes 720896 | tf_op jit(solution)/shard_map/all_to_all | solution.py:166
  36.0 3.7 %collective-permute-start.4 = (bf16[3,96,1408]{2,1,0:T(8,128)(2,1)}, bf16[3,96,1408]{2,1,0:T(8,128)(2,1)}, u32[]{:S(2)}, u32[]{:S(2)}) collective-permute-start(bf16[3,96,1408]{2,1,0:T(8,128)(2,1)} %pad_maximum_fusion.2), channel_id=1, source_target_pairs={{0,32},{32,0},{64,96},{96,64},{128,160},{160,128},{192,224},{224,1... | collective-permute-start | bytes 2433032 | tf_op jit(solution)/shard_map/ppermute | solution.py:139
  48.9 3.5 %all-to-all-start.1 = ((bf16[4,864,128]{2,1,0:T(8,128)(2,1)}), bf16[4,864,128]{2,1,0:T(8,128)(2,1)S(1)}, u32[]{:S(2)}, u32[]{:S(2)}) async-start(bf16[4,864,128]{2,1,0:T(8,128)(2,1)} %dynamic_update_slice.13), calls=%async_computation.1 | async-start | bytes 1769472 | tf_op jit(solution)/shard_map/all_to_all | solution.py:170
  52.5 2.3 %broadcast_select_fusion.1 = (bf16[3,96,1408]{2,1,0:T(8,128)(2,1)S(1)}, bf16[3,96,1408]{2,1,0:T(8,128)(2,1)}) fusion(bf16[3,96,1408]{2,1,0:T(8,128)(2,1)} %collective-permute-done.4, pred[]{:T(512)S(6)} %eq.2, bf16[1,96,1408]{2,1,0:T(8,128)(2,1)S(1)} %bitcast.85, bf16[1,96,1408]{2,1,0:T(8,128)(2,1)S(1)} %bitcast.83, bf16[1,96,1408]{2,1,0:T(8,128)(2,1)S(1)} %bitcast.81), kind=kLoop, calls=%fused_computation.13 | loop fusion | flops 1622016 | bytes 3244033 | tf_op jit(solution)/shard_map/jit(_where)/select_n | solution.py:140
  56.3 6.0 %all-to-all-done.1 = bf16[4,864,128]{2,1,0:T(8,128)(2,1)S(1)} async-done(((bf16[4,864,128]{2,1,0:T(8,128)(2,1)}), bf16[4,864,128]{2,1,0:T(8,128)(2,1)S(1)}, u32[]{:S(2)}, u32[]{:S(2)}) %all-to-all-start.1) | async-done | bytes 884768 | tf_op jit(solution)/shard_map/all_to_all | solution.py:170
  64.3 6.3 %collective-permute-start.3 = (bf16[4,512,128]{2,1,0:T(8,128)(2,1)S(1)}, bf16[4,512,128]{2,1,0:T(8,128)(2,1)S(1)}, u32[]{:S(2)}, u32[]{:S(2)}) collective-permute-start(bf16[4,512,128]{2,1,0:T(8,128)(2,1)S(1)} %slice.119), channel_id=1, source_target_pairs={{0,32},{32,0},{64,96},{96,64},{128,160},{160,128},{192,224},{224,1... | collective-permute-start | bytes 1572872 | tf_op jit(solution)/shard_map/ppermute | solution.py:139
  72.4 3.4 %bitcast_convert_fusion = bf16[4,128,768]{2,1,0:T(8,128)(2,1)} fusion(bf16[4,8,128,128]{3,2,1,0:T(8,128)(2,1)S(1)} %bitcast.86, bf16[8,1824,128]{2,1,0:T(8,128)(2,1)} %bitcast.78), kind=kOutput, calls=%fused_computation.3 | convolution fusion | flops 805699584 | bytes 3407872 | tf_op jit(solution)/shard_map/xyed,yte->xdt/dot_general | solution.py:175
  75.8 3.5 %all-to-all-start.2 = ((bf16[4,128,768]{2,1,0:T(8,128)(2,1)}), bf16[4,128,768]{2,1,0:T(8,128)(2,1)S(1)}, u32[]{:S(2)}, u32[]{:S(2)}) async-start(bf16[4,128,768]{2,1,0:T(8,128)(2,1)} %bitcast_convert_fusion), calls=%async_computation.2 | async-start | bytes 1572864 | tf_op jit(solution)/shard_map/all_to_all | solution.py:176
  86.6 4.7 %all-to-all-done.2 = bf16[4,128,768]{2,1,0:T(8,128)(2,1)S(1)} async-done(((bf16[4,128,768]{2,1,0:T(8,128)(2,1)}), bf16[4,128,768]{2,1,0:T(8,128)(2,1)S(1)}, u32[]{:S(2)}, u32[]{:S(2)}) %all-to-all-start.2) | async-done | bytes 786464 | tf_op jit(solution)/shard_map/all_to_all | solution.py:176
  93.8 6.8 %all-to-all-start.3 = ((bf16[8,128,768]{2,1,0:T(8,128)(2,1)}), bf16[8,128,768]{2,1,0:T(8,128)(2,1)S(1)}, u32[]{:S(2)}, u32[]{:S(2)}) async-start(bf16[8,128,768]{2,1,0:T(8,128)(2,1)} %broadcast_in_dim.2), calls=%async_computation.3 | async-start | bytes 3145728 | tf_op jit(solution)/shard_map/all_to_all | solution.py:183
  106.0 2.6 %convolution_convert_fusion = bf16[176,768]{1,0:T(8,128)(2,1)S(1)} fusion(bf16[1408,768]{1,0:T(8,128)(2,1)} %dynamic_update_slice.14, bf16[80,1408]{1,0:T(8,128)(2,1)} %get-tuple-element.21, bf16[96,1408]{1,0:T(8,128)(2,1)} %get-tuple-element.18), kind=kOutput, calls=%fused_computation.4 | convolution fusion | flops 381759488 | bytes 2928640 | tf_op jit(solution)/shard_map/dot_general | solution.py:179
  108.6 2.4 %collective-permute-start.7 = (bf16[176,768]{1,0:T(8,128)(2,1)S(1)}, bf16[176,768]{1,0:T(8,128)(2,1)S(1)}, u32[]{:S(2)}, u32[]{:S(2)}) collective-permute-start(bf16[176,768]{1,0:T(8,128)(2,1)S(1)} %convolution_convert_fusion), channel_id=1, source_target_pairs={{0,8},{1,9},{2,10},{3,11},{4,12},{5,13},{6,14},{7,15},{8,16},{9,17... | collective-permute-start | bytes 811016 | tf_op jit(solution)/shard_map/ppermute | solution.py:18
  111.7 3.6 %collective-permute-start.6 = (bf16[176,768]{1,0:T(8,128)(2,1)S(1)}, bf16[176,768]{1,0:T(8,128)(2,1)S(1)}, u32[]{:S(2)}, u32[]{:S(2)}) collective-permute-start(bf16[176,768]{1,0:T(8,128)(2,1)S(1)} %convolution_convert_fusion.1), channel_id=1, source_target_pairs={{0,16},{1,17},{2,18},{3,19},{4,20},{5,21},{6,22},{7,23},{8,24},{9,... | collective-permute-start | bytes 811016 | tf_op jit(solution)/shard_map/ppermute | solution.py:18
  115.9 2.6 %collective-permute-start.5 = (bf16[176,768]{1,0:T(8,128)(2,1)S(1)}, bf16[176,768]{1,0:T(8,128)(2,1)S(1)}, u32[]{:S(2)}, u32[]{:S(2)}) collective-permute-start(bf16[176,768]{1,0:T(8,128)(2,1)S(1)} %convolution_convert_fusion.2), channel_id=1, source_target_pairs={{0,24},{1,25},{2,26},{3,27},{4,28},{5,29},{6,30},{7,31},{8,0},{9,1... | collective-permute-start | bytes 811016 | tf_op jit(solution)/shard_map/ppermute | solution.py:18
  118.8 4.9 %collective-permute-done.6 = bf16[176,768]{1,0:T(8,128)(2,1)S(1)} collective-permute-done((bf16[176,768]{1,0:T(8,128)(2,1)S(1)}, bf16[176,768]{1,0:T(8,128)(2,1)S(1)}, u32[]{:S(2)}, u32[]{:S(2)}) %collective-permute-start.6) | collective-permute-done | bytes 270368 | tf_op jit(solution)/shard_map/ppermute | solution.py:18
  123.7 4.0 %collective-permute-done.5 = bf16[176,768]{1,0:T(8,128)(2,1)S(1)} collective-permute-done((bf16[176,768]{1,0:T(8,128)(2,1)S(1)}, bf16[176,768]{1,0:T(8,128)(2,1)S(1)}, u32[]{:S(2)}, u32[]{:S(2)}) %collective-permute-start.5) | collective-permute-done | bytes 270368 | tf_op jit(solution)/shard_map/ppermute | solution.py:18
  128.4 2.3 %collective-permute-start.8 = (bf16[176,768]{1,0:T(8,128)(2,1)S(1)}, bf16[176,768]{1,0:T(8,128)(2,1)S(1)}, u32[]{:S(2)}, u32[]{:S(2)}) collective-permute-start(bf16[176,768]{1,0:T(8,128)(2,1)S(1)} %multiply_convert_fusion.g0_ref), channel_id=1, source_target_pairs={{0,8},{1,9},{2,10},{3,11},{4,12},{5,13},{6,14},{7,15},{8,16},{9,17... | collective-permute-start | bytes 811016 | tf_op jit(solution)/shard_map/ppermute | solution.py:18
  130.7 6.1 %collective-permute-start.9 = (bf16[176,768]{1,0:T(8,128)(2,1)S(1)}, bf16[176,768]{1,0:T(8,128)(2,1)S(1)}, u32[]{:S(2)}, u32[]{:S(2)}) collective-permute-start(bf16[176,768]{1,0:T(8,128)(2,1)S(1)} %multiply_convert_fusion.g0_ref), channel_id=1, source_target_pairs={{0,16},{1,17},{2,18},{3,19},{4,20},{5,21},{6,22},{7,23},{8,24},{9,... | collective-permute-start | bytes 811016 | tf_op jit(solution)/shard_map/ppermute | solution.py:18
  139.0 7.2 %collective-permute-done.9.g2_ref = bf16[176,768]{1,0:T(8,128)(2,1)S(1)} collective-permute-done((bf16[176,768]{1,0:T(8,128)(2,1)S(1)}, bf16[176,768]{1,0:T(8,128)(2,1)S(1)}, u32[]{:S(2)}, u32[]{:S(2)}) %collective-permute-start.9) | collective-permute-done | bytes 270368 | tf_op jit(solution)/shard_map/ppermute | solution.py:18
  150.4 7.2 %shard_map.84 = f32[32,128]{1,0:T(8,128)S(1)} custom-call(s32[1]{0:T(128)} %bitcast.kx_ref, bf16[176,768]{1,0:T(8,128)(2,1)S(1)} %multiply_convert_fusion.g0_ref, bf16[176,768]{1,0:T(8,128)(2,1)S(1)} %collective-permute-done.8.g1_ref, bf16[176,768]{1,0:T(8,128)(2,1)S(1)} %copy-done.3, bf16[176,768]{1,0:T(8,128)(2,1)S(1)} %copy-done.5, ...), custom_call_target="tpu_custom_call" | custom-call | flops 4429185024 | bytes 9000000 | tf_op jit(solution)/shard_map/pallas_call | solution.py:111
  157.6 18.0 %all_to_all.29 = f32[32,1,128]{2,1,0:T(1,128)S(1)} all-to-all(f32[32,1,128]{2,1,0:T(1,128)S(1)} %bitcast.70), channel_id=1, replica_groups=mesh['dp'=16,'tensor'=32] {'tensor'}, dimensions={0} | all-to-all | bytes 32768 | tf_op jit(solution)/shard_map/all_to_all | solution.py:191
  (92 shorter events, 40.6 us)
Async XLA Ops:
  6.5 33.2 %copy-start = (bf16[4096,128]{1,0:T(8,128)(2,1)S(1)}, bf16[4096,128]{1,0:T(8,128)(2,1)}, u32[]{:S(2)}) copy-start(bf16[4096,128]{1,0:T(8,128)(2,1)} %param.10) | copy-start | bytes 3145732
  6.5 17.4 %copy-start.14 = (f32[172,256]{1,0:T(8,128)S(1)}, f32[172,256]{1,0:T(8,128)}, u32[]{:S(2)}) copy-start(f32[172,256]{1,0:T(8,128)} %param.13) | copy-start | bytes 528388
  6.5 65.9 %all-gather.6.cloned.1.call-start = ((), (), s32[]{:S(2)}) async-start(), calls=%async_computation.6 | async-start | bytes 4202496 | tf_op jit(solution)/shard_map/all_gather | solution.py:152
  10.2 13.8 %copy-start.10 = (bf16[4,172,256]{2,0,1:T(4,128)(2,1)S(1)}, bf16[4,172,256]{2,0,1:T(4,128)(2,1)}, u32[]{:S(2)}) copy-start(bf16[4,172,256]{2,0,1:T(4,128)(2,1)} %param.12) | copy-start | bytes 1056772
  11.9 23.1 %collective-permute-start = (bf16[96,1408]{1,0:T(8,128)(2,1)S(1)}, bf16[96,1408]{1,0:T(8,128)(2,1)S(1)}, u32[]{:S(2)}, u32[]{:S(2)}) collective-permute-start(bf16[96,1408]{1,0:T(8,128)(2,1)S(1)} %get-tuple-element.10), channel_id=1, source_target_pairs={{0,8},{1,9},{2,10},{3,11},{4,12},{5,13},{6,14},{7,15},{8,16},{9,17... | collective-permute-start | bytes 811016 | tf_op jit(solution)/shard_map/ppermute | solution.py:18
  15.8 19.1 %collective-permute-start.1 = (bf16[96,1408]{1,0:T(8,128)(2,1)S(1)}, bf16[96,1408]{1,0:T(8,128)(2,1)S(1)}, u32[]{:S(2)}, u32[]{:S(2)}) collective-permute-start(bf16[96,1408]{1,0:T(8,128)(2,1)S(1)} %get-tuple-element.11), channel_id=1, source_target_pairs={{0,16},{1,17},{2,18},{3,19},{4,20},{5,21},{6,22},{7,23},{8,24},{9,... | collective-permute-start | bytes 811016 | tf_op jit(solution)/shard_map/ppermute | solution.py:18
  20.2 14.8 %collective-permute-start.2 = (bf16[96,1408]{1,0:T(8,128)(2,1)S(1)}, bf16[96,1408]{1,0:T(8,128)(2,1)S(1)}, u32[]{:S(2)}, u32[]{:S(2)}) collective-permute-start(bf16[96,1408]{1,0:T(8,128)(2,1)S(1)} %get-tuple-element.12), channel_id=1, source_target_pairs={{0,24},{1,25},{2,26},{3,27},{4,28},{5,29},{6,30},{7,31},{8,0},{9,1... | collective-permute-start | bytes 811016 | tf_op jit(solution)/shard_map/ppermute | solution.py:18
  24.9 21.7 %all-to-all-start = ((bf16[8,176,128]{2,1,0:T(8,128)(2,1)}), bf16[8,176,128]{2,1,0:T(8,128)(2,1)S(1)}, u32[]{:S(2)}, u32[]{:S(2)}) async-start(bf16[8,176,128]{2,1,0:T(8,128)(2,1)} %bitcast.8), calls=%async_computation | async-start | bytes 720896 | tf_op jit(solution)/shard_map/all_to_all | solution.py:166
  36.0 16.5 %collective-permute-start.4 = (bf16[3,96,1408]{2,1,0:T(8,128)(2,1)}, bf16[3,96,1408]{2,1,0:T(8,128)(2,1)}, u32[]{:S(2)}, u32[]{:S(2)}) collective-permute-start(bf16[3,96,1408]{2,1,0:T(8,128)(2,1)} %pad_maximum_fusion.2), channel_id=1, source_target_pairs={{0,32},{32,0},{64,96},{96,64},{128,160},{160,128},{192,224},{224,1... | collective-permute-start | bytes 2433032 | tf_op jit(solution)/shard_map/ppermute | solution.py:139
  48.9 13.3 %all-to-all-start.1 = ((bf16[4,864,128]{2,1,0:T(8,128)(2,1)}), bf16[4,864,128]{2,1,0:T(8,128)(2,1)S(1)}, u32[]{:S(2)}, u32[]{:S(2)}) async-start(bf16[4,864,128]{2,1,0:T(8,128)(2,1)} %dynamic_update_slice.13), calls=%async_computation.1 | async-start | bytes 1769472 | tf_op jit(solution)/shard_map/all_to_all | solution.py:170
  52.4 96.1 %all-gather.4.cloned.1.call-start = ((), (), s32[]{:S(2)}) async-start(), calls=%async_computation.5 | async-start | bytes 6127616 | tf_op jit(solution)/shard_map/all_gather | solution.py:173
  64.3 7.8 %collective-permute-start.3 = (bf16[4,512,128]{2,1,0:T(8,128)(2,1)S(1)}, bf16[4,512,128]{2,1,0:T(8,128)(2,1)S(1)}, u32[]{:S(2)}, u32[]{:S(2)}) collective-permute-start(bf16[4,512,128]{2,1,0:T(8,128)(2,1)S(1)} %slice.119), channel_id=1, source_target_pairs={{0,32},{32,0},{64,96},{96,64},{128,160},{160,128},{192,224},{224,1... | collective-permute-start | bytes 1572872 | tf_op jit(solution)/shard_map/ppermute | solution.py:139
  75.8 15.5 %all-to-all-start.2 = ((bf16[4,128,768]{2,1,0:T(8,128)(2,1)}), bf16[4,128,768]{2,1,0:T(8,128)(2,1)S(1)}, u32[]{:S(2)}, u32[]{:S(2)}) async-start(bf16[4,128,768]{2,1,0:T(8,128)(2,1)} %bitcast_convert_fusion), calls=%async_computation.2 | async-start | bytes 1572864 | tf_op jit(solution)/shard_map/all_to_all | solution.py:176
  93.8 54.7 %all-to-all-start.3 = ((bf16[8,128,768]{2,1,0:T(8,128)(2,1)}), bf16[8,128,768]{2,1,0:T(8,128)(2,1)S(1)}, u32[]{:S(2)}, u32[]{:S(2)}) async-start(bf16[8,128,768]{2,1,0:T(8,128)(2,1)} %broadcast_in_dim.2), calls=%async_computation.3 | async-start | bytes 3145728 | tf_op jit(solution)/shard_map/all_to_all | solution.py:183
  106.0 5.0 %copy-start.11 = (bf16[96,1408]{1,0:T(8,128)(2,1)S(1)}, bf16[96,1408]{1,0:T(8,128)(2,1)}, u32[]{:S(2)}) copy-start(bf16[96,1408]{1,0:T(8,128)(2,1)} %get-tuple-element.19) | copy-start | bytes 811012
  106.0 5.1 %copy-start.13 = (bf16[80,1408]{1,0:T(8,128)(2,1)S(1)}, bf16[80,1408]{1,0:T(8,128)(2,1)}, u32[]{:S(2)}) copy-start(bf16[80,1408]{1,0:T(8,128)(2,1)} %get-tuple-element.22) | copy-start | bytes 675844
  108.6 6.7 %copy-start.12 = (bf16[80,1408]{1,0:T(8,128)(2,1)S(1)}, bf16[80,1408]{1,0:T(8,128)(2,1)}, u32[]{:S(2)}) copy-start(bf16[80,1408]{1,0:T(8,128)(2,1)} %get-tuple-element.20) | copy-start | bytes 675844
  108.6 10.2 %collective-permute-start.7 = (bf16[176,768]{1,0:T(8,128)(2,1)S(1)}, bf16[176,768]{1,0:T(8,128)(2,1)S(1)}, u32[]{:S(2)}, u32[]{:S(2)}) collective-permute-start(bf16[176,768]{1,0:T(8,128)(2,1)S(1)} %convolution_convert_fusion), channel_id=1, source_target_pairs={{0,8},{1,9},{2,10},{3,11},{4,12},{5,13},{6,14},{7,15},{8,16},{9,17... | collective-permute-start | bytes 811016 | tf_op jit(solution)/shard_map/ppermute | solution.py:18
  111.7 6.9 %copy-start.15 = (s32[6]{0:T(128)S(1)}, s32[6]{0:T(128)}, u32[]{:S(2)}) copy-start(s32[6]{0:T(128)} %param.15) | copy-start | bytes 76
  111.7 12.0 %collective-permute-start.6 = (bf16[176,768]{1,0:T(8,128)(2,1)S(1)}, bf16[176,768]{1,0:T(8,128)(2,1)S(1)}, u32[]{:S(2)}, u32[]{:S(2)}) collective-permute-start(bf16[176,768]{1,0:T(8,128)(2,1)S(1)} %convolution_convert_fusion.1), channel_id=1, source_target_pairs={{0,16},{1,17},{2,18},{3,19},{4,20},{5,21},{6,22},{7,23},{8,24},{9,... | collective-permute-start | bytes 811016 | tf_op jit(solution)/shard_map/ppermute | solution.py:18
  115.9 11.8 %collective-permute-start.5 = (bf16[176,768]{1,0:T(8,128)(2,1)S(1)}, bf16[176,768]{1,0:T(8,128)(2,1)S(1)}, u32[]{:S(2)}, u32[]{:S(2)}) collective-permute-start(bf16[176,768]{1,0:T(8,128)(2,1)S(1)} %convolution_convert_fusion.2), channel_id=1, source_target_pairs={{0,24},{1,25},{2,26},{3,27},{4,28},{5,29},{6,30},{7,31},{8,0},{9,1... | collective-permute-start | bytes 811016 | tf_op jit(solution)/shard_map/ppermute | solution.py:18
  128.4 10.6 %collective-permute-start.8 = (bf16[176,768]{1,0:T(8,128)(2,1)S(1)}, bf16[176,768]{1,0:T(8,128)(2,1)S(1)}, u32[]{:S(2)}, u32[]{:S(2)}) collective-permute-start(bf16[176,768]{1,0:T(8,128)(2,1)S(1)} %multiply_convert_fusion.g0_ref), channel_id=1, source_target_pairs={{0,8},{1,9},{2,10},{3,11},{4,12},{5,13},{6,14},{7,15},{8,16},{9,17... | collective-permute-start | bytes 811016 | tf_op jit(solution)/shard_map/ppermute | solution.py:18
  130.7 15.5 %collective-permute-start.9 = (bf16[176,768]{1,0:T(8,128)(2,1)S(1)}, bf16[176,768]{1,0:T(8,128)(2,1)S(1)}, u32[]{:S(2)}, u32[]{:S(2)}) collective-permute-start(bf16[176,768]{1,0:T(8,128)(2,1)S(1)} %multiply_convert_fusion.g0_ref), channel_id=1, source_target_pairs={{0,16},{1,17},{2,18},{3,19},{4,20},{5,21},{6,22},{7,23},{8,24},{9,... | collective-permute-start | bytes 811016 | tf_op jit(solution)/shard_map/ppermute | solution.py:18
  136.8 11.0 %collective-permute-start.10 = (bf16[176,768]{1,0:T(8,128)(2,1)S(1)}, bf16[176,768]{1,0:T(8,128)(2,1)S(1)}, u32[]{:S(2)}, u32[]{:S(2)}) collective-permute-start(bf16[176,768]{1,0:T(8,128)(2,1)S(1)} %multiply_convert_fusion.g0_ref), channel_id=1, source_target_pairs={{0,24},{1,25},{2,26},{3,27},{4,28},{5,29},{6,30},{7,31},{8,0},{9,1... | collective-permute-start | bytes 811016 | tf_op jit(solution)/shard_map/ppermute | solution.py:18
  (9 other events, 12.9 us)
Sparse Core Ops, SparseCore 0:
  9.4 58.3 all-gather.5
  69.9 47.5 all-gather.3

commit v9 on v7

--- a/solution.py
+++ b/solution.py
@@ -77,6 +77,33 @@
     )(where, v)
 
 
+def join_kernel(where_ref, n1_ref, n2_ref, n3_ref, other_ref, o1_ref, o2_ref, o3_ref):
+    skip = 2 * HALF - PAD
+    for n, (n_ref, o_ref) in enumerate(((n1_ref, o1_ref), (n2_ref, o2_ref), (n3_ref, o3_ref))):
+
+        @pl.when(where_ref[1] == 0)
+        def _():
+            o_ref[:HALF] = n_ref[...]
+            o_ref[HALF:] = other_ref[n, skip:]
+
+        @pl.when(where_ref[1] != 0)
+        def _():
+            o_ref[:HALF] = other_ref[n]
+            o_ref[HALF:] = n_ref[skip:]
+
+
+def joined(where, near, other):
+    vmem = pl.BlockSpec(memory_space=pltpu.VMEM)
+    return pl.pallas_call(
+        join_kernel,
+        out_shape=[jax.ShapeDtypeStruct((PAD, other.shape[2]), other.dtype)] * (NX - 1),
+        in_specs=[pl.BlockSpec(memory_space=pltpu.SMEM)] + [vmem] * NX,
+        out_specs=[vmem] * (NX - 1),
+        compiler_params=pltpu.CompilerParams(vmem_limit_bytes=16 * 1024 * 1024),
+        cost_estimate=pl.CostEstimate(flops=0, bytes_accessed=3_000_000, transcendentals=0),
+    )(where, *near, other)
+
+
 def score_kernel(kx_ref, g0_ref, g1_ref, g2_ref, g3_ref, a_ref, s_ref, o_ref, lhs_ref):
     q = pl.program_id(0)
     queries = pl.num_programs(0)
@@ -156,12 +183,12 @@
     scaled = (query_proj.astype(f32) / (eigvals + damping[0])).astype(bf)
     scaled = jnp.pad(scaled, ((0, 0), (0, PAD - width), (0, 0)))
     pieces = scaled.reshape(queries, PAD, 2, 128).transpose(0, 2, 1, 3).reshape(8, PAD, 128)
-    blocks = column_blocks(jnp.stack([kx, core]), out_basis_t)
+    where = jnp.stack([kx, core])
+    blocks = column_blocks(where, out_basis_t)
     near = [shift_x(blocks[d], d) for d in range(1, NX)]
     tie = (near[0][:1, :1] + near[1][:1, :1] + near[2][:1, :1]) * 0
-    near = jnp.stack(near)
-    v_low, v_high = both_halves(near, core)
-    vs = [blocks[0]] + [jnp.concatenate([v_low[n], v_high[n, 2 * HALF - PAD :]]) for n in range(NX - 1)]
+    other = lax.ppermute(jnp.stack(near), "dp", [(n, n ^ 1) for n in range(2 * NZ)])
+    vs = [blocks[0]] + list(joined(where, near, other))
 
     pieces = lax.all_to_all(pieces, "dp", 0, 0, axis_index_groups=ZG)
     rows = NY * 128 // 2
@@ -169,7 +196,7 @@
     mixed = jnp.concatenate([mine, pieces.reshape(NX, 2 * PAD, 128)], axis=1)
     mixed = lax.all_to_all(after(mixed, tie), "tensor", 0, 0, axis_index_groups=XG)
     u4 = jnp.stack(both_halves(mixed[:, :rows], core), axis=1)
-    pieces = after(mixed[:, rows:].reshape(NX, 2, PAD, 128), v_low[0, :1, :1] * 0)
+    pieces = after(mixed[:, rows:].reshape(NX, 2, PAD, 128), vs[1][:1, :1] * 0)
     tiles = lax.all_gather(pieces, "dp").reshape(NZ, 2, NX, 2, PAD, 128)
 
     a_part = jnp.einsum("xyed,yte->xdt", u4.reshape(NX, NY, 128, 128), x8, preferred_element_type=f32).astype(bf)

time: 176 us -> 179 us (1.017)
  local copies, waits for them, and re-layouts: 17.8 us -> 20.4 us
    ppermute x0 -> x1, starting transfers between devices: none -> 3.67 us  [local(): lax.ppermute(jnp.stack(near), 'dp', [(n, n ^ 1) for n in range(2 * NZ)])]
    ppermute x2 -> x1, starting transfers between devices: 9.98 us -> 6.34 us  [both_halves(): other = lax.ppermute(mine, 'dp', [(n, n ^ 1) for n in range(2 * NZ)])]
    squeeze x2 -> x0, local copies, waits for them, and re-layouts: 2.42 us -> none  [the longest x1 1.22 us: local(): v_low[n]]
    select_n x1 -> x0, other arithmetic: 2.25 us -> none  [both_halves(): jnp.where(core == 0, mine, other)]
    unnamed x20 -> x26, local copies, waits for them, and re-layouts: 5.99 us -> 6.6 us
  transfers between devices with their start and end apart: 16 -> 16, of which waited for: 7 -> 7; matrix products, arithmetic and copies ran while one was open for 13% -> 14% of each run, Pallas kernels for 1% -> 1%
where the time goes in v9:
time: 179 us; the launch traced here: 177 us
  starting transfers between devices  58.6 us (33%)
  blocking collectives  30.8 us (17%)
  waiting for transfers between devices  25.8 us (14%)
  local copies, waits for them, and re-layouts  20.4 us (11%)
  between operations  18.1 us (10%)
  Pallas kernels  11.4 us (6%)
  other arithmetic  6.49 us (4%)
  matrix products  5.14 us (3%)
    ppermute x9, starting transfers between devices, shift_x(): return lax.ppermute(array, 'tensor', perm)  27.5 us
    ppermute x9, waiting for transfers between devices, shift_x(): return lax.ppermute(array, 'tensor', perm)  17.7 us
    all_to_all x1, blocking collectives, local(): lax.all_to_all(tile, 'tensor', 0, 0, tiled=True).sum(0)[:seqs * queries]  16.4 us
    all_to_all x1, blocking collectives, local(): a_parts = lax.all_to_all(a_part, 'tensor', 0, 0, axis_index_groups=XG)  14.4 us
    all_to_all x1, starting transfers between devices, local(): pieces = lax.all_to_all(pieces, 'dp', 0, 0, axis_index_groups=ZG)  10.1 us
    pallas_call x1, Pallas kernels, score_tiles(): pl.pallas_call(score_kernel, grid=(queries,), out_shape=jax.ShapeDtypeStr...  7.06 us
    all_to_all x1, starting transfers between devices, local(): at = lax.all_to_all(at, 'tensor', 0, 0, axis_index_groups=YG)  6.8 us
    unnamed x26, local copies, waits for them, and re-layouts  6.6 us
  transfers between devices with their start and end apart: 16, of which 7 were waited for; matrix products, arithmetic and copies ran while one was open for 14% of the time, Pallas kernels for 1%

profile of v9, /device:TPU:1, one launch (start us, length us, event | category | flops | bytes accessed | tf_op | source)
XLA Modules:
  0.0 176.8 jit_solution(13326629808869905327)
XLA Ops:
  6.5 2.0 %shard_map.83 = bf16[1824,128]{1,0:T(8,128)(2,1)} custom-call(bf16[768,128]{1,0:T(8,128)(2,1)} %x_ref.1, bf16[172,768]{1,0:T(8,128)(2,1)} %y_ref.1), custom_call_target="tpu_custom_call" | custom-call | bytes 1000000 | tf_op jit(solution)/shard_map/pallas_call | solution.py:33
  11.9 3.9 %collective-permute-start = (bf16[96,1408]{1,0:T(8,128)(2,1)S(1)}, bf16[96,1408]{1,0:T(8,128)(2,1)S(1)}, u32[]{:S(2)}, u32[]{:S(2)}) collective-permute-start(bf16[96,1408]{1,0:T(8,128)(2,1)S(1)} %get-tuple-element.13), channel_id=1, source_target_pairs={{0,8},{1,9},{2,10},{3,11},{4,12},{5,13},{6,14},{7,15},{8,16},{9,17... | collective-permute-start | bytes 811016 | tf_op jit(solution)/shard_map/ppermute | solution.py:18
  15.8 4.4 %collective-permute-start.1 = (bf16[96,1408]{1,0:T(8,128)(2,1)S(1)}, bf16[96,1408]{1,0:T(8,128)(2,1)S(1)}, u32[]{:S(2)}, u32[]{:S(2)}) collective-permute-start(bf16[96,1408]{1,0:T(8,128)(2,1)S(1)} %get-tuple-element.14), channel_id=1, source_target_pairs={{0,16},{1,17},{2,18},{3,19},{4,20},{5,21},{6,22},{7,23},{8,24},{9,... | collective-permute-start | bytes 811016 | tf_op jit(solution)/shard_map/ppermute | solution.py:18
  20.2 3.1 %collective-permute-start.2 = (bf16[96,1408]{1,0:T(8,128)(2,1)S(1)}, bf16[96,1408]{1,0:T(8,128)(2,1)S(1)}, u32[]{:S(2)}, u32[]{:S(2)}) collective-permute-start(bf16[96,1408]{1,0:T(8,128)(2,1)S(1)} %get-tuple-element.15), channel_id=1, source_target_pairs={{0,24},{1,25},{2,26},{3,27},{4,28},{5,29},{6,30},{7,31},{8,0},{9,1... | collective-permute-start | bytes 811016 | tf_op jit(solution)/shard_map/ppermute | solution.py:18
  25.8 10.1 %all-to-all-start = ((bf16[8,176,128]{2,1,0:T(8,128)(2,1)}), bf16[8,176,128]{2,1,0:T(8,128)(2,1)S(1)}, u32[]{:S(2)}, u32[]{:S(2)}) async-start(bf16[8,176,128]{2,1,0:T(8,128)(2,1)} %bitcast.82), calls=%async_computation | async-start | bytes 720896 | tf_op jit(solution)/shard_map/all_to_all | solution.py:193
  36.9 3.7 %collective-permute-start.3 = (bf16[3,96,1408]{2,1,0:T(8,128)(2,1)}, bf16[3,96,1408]{2,1,0:T(8,128)(2,1)S(1)}, u32[]{:S(2)}, u32[]{:S(2)}) collective-permute-start(bf16[3,96,1408]{2,1,0:T(8,128)(2,1)} %pad_maximum_fusion.2), channel_id=1, source_target_pairs={{0,32},{32,0},{64,96},{96,64},{128,160},{160,128},{192,224},{224,1... | collective-permute-start | bytes 2433032 | tf_op jit(solution)/shard_map/ppermute | solution.py:190
  47.6 2.0 %pad_maximum_fusion.1 = bf16[4,864,128]{2,1,0:T(8,128)(2,1)} fusion(bf16[4,352,128]{2,1,0:T(8,128)(2,1)S(1)} %bitcast.81, bf16[4,512,128]{2,1,0:T(8,128)(2,1)} %dynamic-slice_bitcast_fusion), kind=kLoop, calls=%fused_computation.17 | loop fusion | flops 1769472 | bytes 1769472 | tf_op jit(solution)/shard_map/concatenate | solution.py:196
  50.9 4.2 %all-to-all-start.1 = ((bf16[4,864,128]{2,1,0:T(8,128)(2,1)}), bf16[4,864,128]{2,1,0:T(8,128)(2,1)}, u32[]{:S(2)}, u32[]{:S(2)}) async-start(bf16[4,864,128]{2,1,0:T(8,128)(2,1)} %dynamic_update_slice.7), calls=%async_computation.1 | async-start | bytes 1769472 | tf_op jit(solution)/shard_map/all_to_all | solution.py:197
  59.5 5.5 %all-to-all-done.1 = bf16[4,864,128]{2,1,0:T(8,128)(2,1)} async-done(((bf16[4,864,128]{2,1,0:T(8,128)(2,1)}), bf16[4,864,128]{2,1,0:T(8,128)(2,1)}, u32[]{:S(2)}, u32[]{:S(2)}) %all-to-all-start.1) | async-done | bytes 884768 | tf_op jit(solution)/shard_map/all_to_all | solution.py:197
  69.1 6.3 %collective-permute-start.10 = (bf16[4,512,128]{2,1,0:T(8,128)(2,1)S(1)}, bf16[4,512,128]{2,1,0:T(8,128)(2,1)S(1)}, u32[]{:S(2)}, u32[]{:S(2)}) collective-permute-start(bf16[4,512,128]{2,1,0:T(8,128)(2,1)S(1)} %slice.81), channel_id=1, source_target_pairs={{0,32},{32,0},{64,96},{96,64},{128,160},{160,128},{192,224},{224,1... | collective-permute-start | bytes 1572872 | tf_op jit(solution)/shard_map/ppermute | solution.py:166
  79.3 2.8 %bitcast_convert_fusion = bf16[4,128,768]{2,1,0:T(8,128)(2,1)S(1)} fusion(bf16[4,8,128,128]{3,2,1,0:T(8,128)(2,1)} %bitcast.87, bf16[8,1824,128]{2,1,0:T(8,128)(2,1)} %bitcast.85), kind=kOutput, calls=%fused_computation.10 | convolution fusion | flops 805699584 | bytes 3407872 | tf_op jit(solution)/shard_map/xyed,yte->xdt/dot_general | solution.py:202
  82.1 14.4 %all_to_all.29 = bf16[4,128,768]{2,1,0:T(8,128)(2,1)S(1)} all-to-all(bf16[4,128,768]{2,1,0:T(8,128)(2,1)S(1)} %bitcast_convert_fusion), channel_id=1, replica_groups={{0,8,16,24},{1,9,17,25},{2,10,18,26},{3,11,19,27},{4,12,20,28},{5,13,21..., dimensions={0} | all-to-all | bytes 1572864 | tf_op jit(solution)/shard_map/all_to_all | solution.py:203
  97.9 6.8 %all-to-all-start.3 = ((bf16[8,128,768]{2,1,0:T(8,128)(2,1)}), bf16[8,128,768]{2,1,0:T(8,128)(2,1)S(1)}, u32[]{:S(2)}, u32[]{:S(2)}) async-start(bf16[8,128,768]{2,1,0:T(8,128)(2,1)} %broadcast_in_dim.2), calls=%async_computation.3 | async-start | bytes 3145728 | tf_op jit(solution)/shard_map/all_to_all | solution.py:210
  108.2 2.9 %collective-permute-start.4 = (bf16[176,768]{1,0:T(8,128)(2,1)S(1)}, bf16[176,768]{1,0:T(8,128)(2,1)S(1)}, u32[]{:S(2)}, u32[]{:S(2)}) collective-permute-start(bf16[176,768]{1,0:T(8,128)(2,1)S(1)} %fusion.15), channel_id=1, source_target_pairs={{0,24},{1,25},{2,26},{3,27},{4,28},{5,29},{6,30},{7,31},{8,0},{9,1... | collective-permute-start | bytes 811016 | tf_op jit(solution)/shard_map/ppermute | solution.py:18
  111.8 2.5 %collective-permute-start.6 = (bf16[176,768]{1,0:T(8,128)(2,1)S(1)}, bf16[176,768]{1,0:T(8,128)(2,1)S(1)}, u32[]{:S(2)}, u32[]{:S(2)}) collective-permute-start(bf16[176,768]{1,0:T(8,128)(2,1)S(1)} %fusion.21), channel_id=1, source_target_pairs={{0,8},{1,9},{2,10},{3,11},{4,12},{5,13},{6,14},{7,15},{8,16},{9,17... | collective-permute-start | bytes 811016 | tf_op jit(solution)/shard_map/ppermute | solution.py:18
  114.9 2.6 %collective-permute-start.5 = (bf16[176,768]{1,0:T(8,128)(2,1)S(1)}, bf16[176,768]{1,0:T(8,128)(2,1)S(1)}, u32[]{:S(2)}, u32[]{:S(2)}) collective-permute-start(bf16[176,768]{1,0:T(8,128)(2,1)S(1)} %fusion.18), channel_id=1, source_target_pairs={{0,16},{1,17},{2,18},{3,19},{4,20},{5,21},{6,22},{7,23},{8,24},{9,... | collective-permute-start | bytes 811016 | tf_op jit(solution)/shard_map/ppermute | solution.py:18
  118.1 3.0 %collective-permute-done.6 = bf16[176,768]{1,0:T(8,128)(2,1)S(1)} collective-permute-done((bf16[176,768]{1,0:T(8,128)(2,1)S(1)}, bf16[176,768]{1,0:T(8,128)(2,1)S(1)}, u32[]{:S(2)}, u32[]{:S(2)}) %collective-permute-start.6) | collective-permute-done | bytes 270368 | tf_op jit(solution)/shard_map/ppermute | solution.py:18
  121.1 5.1 %collective-permute-done.5 = bf16[176,768]{1,0:T(8,128)(2,1)S(1)} collective-permute-done((bf16[176,768]{1,0:T(8,128)(2,1)S(1)}, bf16[176,768]{1,0:T(8,128)(2,1)S(1)}, u32[]{:S(2)}, u32[]{:S(2)}) %collective-permute-start.5) | collective-permute-done | bytes 270368 | tf_op jit(solution)/shard_map/ppermute | solution.py:18
  128.4 3.3 %collective-permute-start.8 = (bf16[176,768]{1,0:T(8,128)(2,1)S(1)}, bf16[176,768]{1,0:T(8,128)(2,1)S(1)}, u32[]{:S(2)}, u32[]{:S(2)}) collective-permute-start(bf16[176,768]{1,0:T(8,128)(2,1)S(1)} %multiply_convert_fusion.g0_ref), channel_id=1, source_target_pairs={{0,16},{1,17},{2,18},{3,19},{4,20},{5,21},{6,22},{7,23},{8,24},{9,... | collective-permute-start | bytes 811016 | tf_op jit(solution)/shard_map/ppermute | solution.py:18
  131.7 2.8 %collective-permute-start.7 = (bf16[176,768]{1,0:T(8,128)(2,1)S(1)}, bf16[176,768]{1,0:T(8,128)(2,1)S(1)}, u32[]{:S(2)}, u32[]{:S(2)}) collective-permute-start(bf16[176,768]{1,0:T(8,128)(2,1)S(1)} %multiply_convert_fusion.g0_ref), channel_id=1, source_target_pairs={{0,8},{1,9},{2,10},{3,11},{4,12},{5,13},{6,14},{7,15},{8,16},{9,17... | collective-permute-start | bytes 811016 | tf_op jit(solution)/shard_map/ppermute | solution.py:18
  134.5 2.9 %collective-permute-done.8.g2_ref = bf16[176,768]{1,0:T(8,128)(2,1)S(1)} collective-permute-done((bf16[176,768]{1,0:T(8,128)(2,1)S(1)}, bf16[176,768]{1,0:T(8,128)(2,1)S(1)}, u32[]{:S(2)}, u32[]{:S(2)}) %collective-permute-start.8) | collective-permute-done | bytes 270368 | tf_op jit(solution)/shard_map/ppermute | solution.py:18
  137.4 6.7 %collective-permute-done.7.g1_ref = bf16[176,768]{1,0:T(8,128)(2,1)S(1)} collective-permute-done((bf16[176,768]{1,0:T(8,128)(2,1)S(1)}, bf16[176,768]{1,0:T(8,128)(2,1)S(1)}, u32[]{:S(2)}, u32[]{:S(2)}) %collective-permute-start.7) | collective-permute-done | bytes 270368 | tf_op jit(solution)/shard_map/ppermute | solution.py:18
  145.7 7.1 %shard_map.85 = f32[32,128]{1,0:T(8,128)S(1)} custom-call(s32[1]{0:T(128)} %bitcast.kx_ref, bf16[176,768]{1,0:T(8,128)(2,1)S(1)} %multiply_convert_fusion.g0_ref, bf16[176,768]{1,0:T(8,128)(2,1)S(1)} %copy-done.9, bf16[176,768]{1,0:T(8,128)(2,1)S(1)} %collective-permute-done.8.g2_ref, bf16[176,768]{1,0:T(8,128)(2,1)S(1)} %collective-permute-done.9.g3_ref, ...), custom_call_target="tpu_custom_call" | custom-call | flops 4429185024 | bytes 9000000 | tf_op jit(solution)/shard_map/pallas_call | solution.py:138
  152.8 16.4 %all_to_all.30 = f32[32,1,128]{2,1,0:T(1,128)S(1)} all-to-all(f32[32,1,128]{2,1,0:T(1,128)S(1)} %bitcast.75), channel_id=1, replica_groups=mesh['dp'=16,'tensor'=32] {'tensor'}, dimensions={0} | all-to-all | bytes 32768 | tf_op jit(solution)/shard_map/all_to_all | solution.py:218
  (78 shorter events, 34.2 us)
Async XLA Ops:
  6.5 34.0 %copy-start = (bf16[4096,128]{1,0:T(8,128)(2,1)S(1)}, bf16[4096,128]{1,0:T(8,128)(2,1)}, u32[]{:S(2)}) copy-start(bf16[4096,128]{1,0:T(8,128)(2,1)} %param.10) | copy-start | bytes 3145732
  6.5 18.3 %copy-start.11 = (bf16[4,172,256]{2,0,1:T(4,128)(2,1)S(1)}, bf16[4,172,256]{2,0,1:T(4,128)(2,1)}, u32[]{:S(2)}) copy-start(bf16[4,172,256]{2,0,1:T(4,128)(2,1)} %param.12) | copy-start | bytes 1056772
  6.5 72.8 %all-gather.6.cloned.1.call-start = ((), (), s32[]{:S(2)}) async-start(), calls=%async_computation.6 | async-start | bytes 4202496 | tf_op jit(solution)/shard_map/all_gather | solution.py:179
  8.6 1.5 copy-start.1
  11.9 24.0 %collective-permute-start = (bf16[96,1408]{1,0:T(8,128)(2,1)S(1)}, bf16[96,1408]{1,0:T(8,128)(2,1)S(1)}, u32[]{:S(2)}, u32[]{:S(2)}) collective-permute-start(bf16[96,1408]{1,0:T(8,128)(2,1)S(1)} %get-tuple-element.13), channel_id=1, source_target_pairs={{0,8},{1,9},{2,10},{3,11},{4,12},{5,13},{6,14},{7,15},{8,16},{9,17... | collective-permute-start | bytes 811016 | tf_op jit(solution)/shard_map/ppermute | solution.py:18
  15.8 20.0 %collective-permute-start.1 = (bf16[96,1408]{1,0:T(8,128)(2,1)S(1)}, bf16[96,1408]{1,0:T(8,128)(2,1)S(1)}, u32[]{:S(2)}, u32[]{:S(2)}) collective-permute-start(bf16[96,1408]{1,0:T(8,128)(2,1)S(1)} %get-tuple-element.14), channel_id=1, source_target_pairs={{0,16},{1,17},{2,18},{3,19},{4,20},{5,21},{6,22},{7,23},{8,24},{9,... | collective-permute-start | bytes 811016 | tf_op jit(solution)/shard_map/ppermute | solution.py:18
  20.2 15.7 %collective-permute-start.2 = (bf16[96,1408]{1,0:T(8,128)(2,1)S(1)}, bf16[96,1408]{1,0:T(8,128)(2,1)S(1)}, u32[]{:S(2)}, u32[]{:S(2)}) collective-permute-start(bf16[96,1408]{1,0:T(8,128)(2,1)S(1)} %get-tuple-element.15), channel_id=1, source_target_pairs={{0,24},{1,25},{2,26},{3,27},{4,28},{5,29},{6,30},{7,31},{8,0},{9,1... | collective-permute-start | bytes 811016 | tf_op jit(solution)/shard_map/ppermute | solution.py:18
  25.8 21.8 %all-to-all-start = ((bf16[8,176,128]{2,1,0:T(8,128)(2,1)}), bf16[8,176,128]{2,1,0:T(8,128)(2,1)S(1)}, u32[]{:S(2)}, u32[]{:S(2)}) async-start(bf16[8,176,128]{2,1,0:T(8,128)(2,1)} %bitcast.82), calls=%async_computation | async-start | bytes 720896 | tf_op jit(solution)/shard_map/all_to_all | solution.py:193
  36.9 18.3 %collective-permute-start.3 = (bf16[3,96,1408]{2,1,0:T(8,128)(2,1)}, bf16[3,96,1408]{2,1,0:T(8,128)(2,1)S(1)}, u32[]{:S(2)}, u32[]{:S(2)}) collective-permute-start(bf16[3,96,1408]{2,1,0:T(8,128)(2,1)} %pad_maximum_fusion.2), channel_id=1, source_target_pairs={{0,32},{32,0},{64,96},{96,64},{128,160},{160,128},{192,224},{224,1... | collective-permute-start | bytes 2433032 | tf_op jit(solution)/shard_map/ppermute | solution.py:190
  50.9 14.1 %all-to-all-start.1 = ((bf16[4,864,128]{2,1,0:T(8,128)(2,1)}), bf16[4,864,128]{2,1,0:T(8,128)(2,1)}, u32[]{:S(2)}, u32[]{:S(2)}) async-start(bf16[4,864,128]{2,1,0:T(8,128)(2,1)} %dynamic_update_slice.7), calls=%async_computation.1 | async-start | bytes 1769472 | tf_op jit(solution)/shard_map/all_to_all | solution.py:197
  55.1 89.7 %all-gather.4.cloned.1.call-start = ((), (), s32[]{:S(2)}) async-start(), calls=%async_computation.5 | async-start | bytes 6127616 | tf_op jit(solution)/shard_map/all_gather | solution.py:200
  69.1 7.9 %collective-permute-start.10 = (bf16[4,512,128]{2,1,0:T(8,128)(2,1)S(1)}, bf16[4,512,128]{2,1,0:T(8,128)(2,1)S(1)}, u32[]{:S(2)}, u32[]{:S(2)}) collective-permute-start(bf16[4,512,128]{2,1,0:T(8,128)(2,1)S(1)} %slice.81), channel_id=1, source_target_pairs={{0,32},{32,0},{64,96},{96,64},{128,160},{160,128},{192,224},{224,1... | collective-permute-start | bytes 1572872 | tf_op jit(solution)/shard_map/ppermute | solution.py:166
  96.6 8.1 %copy-start.12 = (s32[6]{0:T(128)S(1)}, s32[6]{0:T(128)}, u32[]{:S(2)}) copy-start(s32[6]{0:T(128)} %param.15) | copy-start | bytes 76
  97.9 46.9 %all-to-all-start.3 = ((bf16[8,128,768]{2,1,0:T(8,128)(2,1)}), bf16[8,128,768]{2,1,0:T(8,128)(2,1)S(1)}, u32[]{:S(2)}, u32[]{:S(2)}) async-start(bf16[8,128,768]{2,1,0:T(8,128)(2,1)} %broadcast_in_dim.2), calls=%async_computation.3 | async-start | bytes 3145728 | tf_op jit(solution)/shard_map/all_to_all | solution.py:210
  106.5 1.0 copy-start.7
  107.3 3.8 %copy-start.5 = (bf16[176,1408]{1,0:T(8,128)(2,1)S(1)}, bf16[176,1408]{1,0:T(8,128)(2,1)}, u32[]{:S(2)}) copy-start(bf16[176,1408]{1,0:T(8,128)(2,1)} %copy-done.4) | copy-start | bytes 1486852
  108.2 6.1 %copy-start.3 = (bf16[176,1408]{1,0:T(8,128)(2,1)S(1)}, bf16[176,1408]{1,0:T(8,128)(2,1)}, u32[]{:S(2)}) copy-start(bf16[176,1408]{1,0:T(8,128)(2,1)} %copy-done.2) | copy-start | bytes 1486852
  108.2 9.9 %collective-permute-start.4 = (bf16[176,768]{1,0:T(8,128)(2,1)S(1)}, bf16[176,768]{1,0:T(8,128)(2,1)S(1)}, u32[]{:S(2)}, u32[]{:S(2)}) collective-permute-start(bf16[176,768]{1,0:T(8,128)(2,1)S(1)} %fusion.15), channel_id=1, source_target_pairs={{0,24},{1,25},{2,26},{3,27},{4,28},{5,29},{6,30},{7,31},{8,0},{9,1... | collective-permute-start | bytes 811016 | tf_op jit(solution)/shard_map/ppermute | solution.py:18
  111.8 9.4 %collective-permute-start.6 = (bf16[176,768]{1,0:T(8,128)(2,1)S(1)}, bf16[176,768]{1,0:T(8,128)(2,1)S(1)}, u32[]{:S(2)}, u32[]{:S(2)}) collective-permute-start(bf16[176,768]{1,0:T(8,128)(2,1)S(1)} %fusion.21), channel_id=1, source_target_pairs={{0,8},{1,9},{2,10},{3,11},{4,12},{5,13},{6,14},{7,15},{8,16},{9,17... | collective-permute-start | bytes 811016 | tf_op jit(solution)/shard_map/ppermute | solution.py:18
  114.9 11.4 %collective-permute-start.5 = (bf16[176,768]{1,0:T(8,128)(2,1)S(1)}, bf16[176,768]{1,0:T(8,128)(2,1)S(1)}, u32[]{:S(2)}, u32[]{:S(2)}) collective-permute-start(bf16[176,768]{1,0:T(8,128)(2,1)S(1)} %fusion.18), channel_id=1, source_target_pairs={{0,16},{1,17},{2,18},{3,19},{4,20},{5,21},{6,22},{7,23},{8,24},{9,... | collective-permute-start | bytes 811016 | tf_op jit(solution)/shard_map/ppermute | solution.py:18
  126.4 8.1 %collective-permute-start.9 = (bf16[176,768]{1,0:T(8,128)(2,1)S(1)}, bf16[176,768]{1,0:T(8,128)(2,1)S(1)}, u32[]{:S(2)}, u32[]{:S(2)}) collective-permute-start(bf16[176,768]{1,0:T(8,128)(2,1)S(1)} %multiply_convert_fusion.g0_ref), channel_id=1, source_target_pairs={{0,24},{1,25},{2,26},{3,27},{4,28},{5,29},{6,30},{7,31},{8,0},{9,1... | collective-permute-start | bytes 811016 | tf_op jit(solution)/shard_map/ppermute | solution.py:18
  128.4 9.0 %collective-permute-start.8 = (bf16[176,768]{1,0:T(8,128)(2,1)S(1)}, bf16[176,768]{1,0:T(8,128)(2,1)S(1)}, u32[]{:S(2)}, u32[]{:S(2)}) collective-permute-start(bf16[176,768]{1,0:T(8,128)(2,1)S(1)} %multiply_convert_fusion.g0_ref), channel_id=1, source_target_pairs={{0,16},{1,17},{2,18},{3,19},{4,20},{5,21},{6,22},{7,23},{8,24},{9,... | collective-permute-start | bytes 811016 | tf_op jit(solution)/shard_map/ppermute | solution.py:18
  131.7 12.3 %collective-permute-start.7 = (bf16[176,768]{1,0:T(8,128)(2,1)S(1)}, bf16[176,768]{1,0:T(8,128)(2,1)S(1)}, u32[]{:S(2)}, u32[]{:S(2)}) collective-permute-start(bf16[176,768]{1,0:T(8,128)(2,1)S(1)} %multiply_convert_fusion.g0_ref), channel_id=1, source_target_pairs={{0,8},{1,9},{2,10},{3,11},{4,12},{5,13},{6,14},{7,15},{8,16},{9,17... | collective-permute-start | bytes 811016 | tf_op jit(solution)/shard_map/ppermute | solution.py:18
  144.8 1.0 copy-start.9
  (5 other events, 3.8 us)
Sparse Core Ops, SparseCore 0:
  9.4 58.3 all-gather.5
  69.9 49.1 all-gather.3

commit v10 on v7

--- a/solution.py
+++ b/solution.py
@@ -77,18 +77,18 @@
     )(where, v)
 
 
-def score_kernel(kx_ref, g0_ref, g1_ref, g2_ref, g3_ref, a_ref, s_ref, o_ref, lhs_ref):
+def score_kernel(kx_ref, g_ref, a_ref, s_ref, o_ref, lhs_ref):
     q = pl.program_id(0)
     queries = pl.num_programs(0)
-    tokens = g0_ref.shape[1]
+    tokens = a_ref.shape[1]
     for d in range(NX):
         fx = (kx_ref[0] - d) & (NX - 1)
         for y in range(NY):
             lhs_ref[d * PAD : (d + 1) * PAD, y * 128 : (y + 1) * 128] = s_ref[y % 2, y // 2 % 2, fx, y // 4]
     t = jnp.dot(lhs_ref[...], a_ref[...], preferred_element_type=jnp.float32)
     acc = jnp.zeros((8, tokens), jnp.float32)
-    for d, g_ref in enumerate((g0_ref, g1_ref, g2_ref, g3_ref)):
-        part = t[d * PAD : (d + 1) * PAD] * g_ref[...].astype(jnp.float32)
+    for d in range(NX):
+        part = t[d * PAD : (d + 1) * PAD] * g_ref[d].astype(jnp.float32)
         acc += part.reshape(PAD // 8, 8, tokens).sum(0)
     per_token = jnp.sum(acc, axis=0, keepdims=True)
     lane = lax.broadcasted_iota(jnp.int32, o_ref.shape, 1)
@@ -104,7 +104,7 @@
     o_ref[...] = out
 
 
-def score_tiles(kx, gs, at, tiles):
+def score_tiles(kx, g4, at, tiles):
     tokens = at.shape[1]
     queries = tiles.shape[0] // 2
     whole = lambda q: (0, 0)
@@ -113,7 +113,7 @@
         grid=(queries,),
         out_shape=jax.ShapeDtypeStruct((NX * NY, 128), jnp.float32),
         in_specs=[pl.BlockSpec(memory_space=pltpu.SMEM)]
-        + [pl.BlockSpec((PAD, tokens), whole)] * NX
+        + [pl.BlockSpec((NX, PAD, tokens), lambda q: (0, 0, 0))]
         + [pl.BlockSpec(at.shape, whole), pl.BlockSpec((2,) + tiles.shape[1:], lambda q: (q, 0, 0, 0, 0, 0))],
         out_specs=pl.BlockSpec((NX * NY, 128), whole),
         scratch_shapes=[pltpu.VMEM((NX * PAD, NY * 128), jnp.bfloat16)],
@@ -121,7 +121,7 @@
         cost_estimate=pl.CostEstimate(
             flops=2 * NX * queries * PAD * NY * 128 * tokens, bytes_accessed=9_000_000, transcendentals=0
         ),
-    )(kx, *gs, at, tiles)
+    )(kx, g4, at, tiles)
 
 
 def add_parts(parts):
@@ -187,7 +187,7 @@
     g = (add_parts(g_parts) * keep).astype(bf)
     gs = [g] + [shift_x(g, d) for d in range(1, NX)]
 
-    tile = score_tiles(kx.reshape(1), gs, at.reshape(NY * 128, tokens), tiles)
+    tile = score_tiles(kx.reshape(1), jnp.stack(gs), at.reshape(NY * 128, tokens), tiles)
     totals = lax.all_to_all(tile, "tensor", 0, 0, tiled=True).sum(0)[: seqs * queries]
     norm_factor = (in_basis.shape[0] * out_basis_t.shape[1] * seq_len) ** (-0.5)
     return totals.reshape(seqs, queries) * norm_factor

time: 176 us -> 175 us (level)
  local copies, waits for them, and re-layouts: 17.8 us -> 15.8 us
    unnamed x20 -> x14, local copies, waits for them, and re-layouts: 5.99 us -> 3.9 us
  transfers between devices with their start and end apart: 16 -> 16, of which waited for: 7 -> 7; matrix products, arithmetic and copies ran while one was open for 13% -> 14% of each run, Pallas kernels for 1% -> 1%
where the time goes in v10:
time: 175 us; the launch traced here: 172 us
  starting transfers between devices  57.8 us (33%)
  blocking collectives  29.7 us (17%)
  waiting for transfers between devices  27 us (15%)
  between operations  18.3 us (10%)
  local copies, waits for them, and re-layouts  15.8 us (9%)
  Pallas kernels  10.8 us (6%)
  other arithmetic  7.62 us (4%)
  matrix products  4.9 us (3%)
    ppermute x9, starting transfers between devices, shift_x(): return lax.ppermute(array, 'tensor', perm)  27.5 us
    ppermute x9, waiting for transfers between devices, shift_x(): return lax.ppermute(array, 'tensor', perm)  17.4 us
    all_to_all x1, blocking collectives, local(): lax.all_to_all(tile, 'tensor', 0, 0, tiled=True).sum(0)[:seqs * queries]  15.3 us
    all_to_all x1, blocking collectives, local(): a_parts = lax.all_to_all(a_part, 'tensor', 0, 0, axis_index_groups=XG)  14.4 us
    all_to_all x1, starting transfers between devices, local(): pieces = lax.all_to_all(pieces, 'dp', 0, 0, axis_index_groups=ZG)  10.1 us
    ppermute x2, starting transfers between devices, both_halves(): other = lax.ppermute(mine, 'dp', [(n, n ^ 1) for n in range(2 * NZ)])  9.97 us
    pallas_call x1, Pallas kernels, score_tiles(): pl.pallas_call(score_kernel, grid=(queries,), out_shape=jax.ShapeDtypeStr...  7.18 us
    all_to_all x1, starting transfers between devices, local(): at = lax.all_to_all(at, 'tensor', 0, 0, axis_index_groups=YG)  6.78 us
  transfers between devices with their start and end apart: 16, of which 7 were waited for; matrix products, arithmetic and copies ran while one was open for 14% of the time, Pallas kernels for 1%

profile of v10, /device:TPU:1, one launch (start us, length us, event | category | flops | bytes accessed | tf_op | source)
XLA Modules:
  0.0 171.9 jit_solution(6863757022642234087)
XLA Ops:
  11.9 3.9 %collective-permute-start = (bf16[96,1408]{1,0:T(8,128)(2,1)S(1)}, bf16[96,1408]{1,0:T(8,128)(2,1)S(1)}, u32[]{:S(2)}, u32[]{:S(2)}) collective-permute-start(bf16[96,1408]{1,0:T(8,128)(2,1)S(1)} %get-tuple-element.10), channel_id=1, source_target_pairs={{0,8},{1,9},{2,10},{3,11},{4,12},{5,13},{6,14},{7,15},{8,16},{9,17... | collective-permute-start | bytes 811016 | tf_op jit(solution)/shard_map/ppermute | solution.py:18
  15.8 4.4 %collective-permute-start.1 = (bf16[96,1408]{1,0:T(8,128)(2,1)S(1)}, bf16[96,1408]{1,0:T(8,128)(2,1)S(1)}, u32[]{:S(2)}, u32[]{:S(2)}) collective-permute-start(bf16[96,1408]{1,0:T(8,128)(2,1)S(1)} %get-tuple-element.11), channel_id=1, source_target_pairs={{0,16},{1,17},{2,18},{3,19},{4,20},{5,21},{6,22},{7,23},{8,24},{9,... | collective-permute-start | bytes 811016 | tf_op jit(solution)/shard_map/ppermute | solution.py:18
  20.2 3.1 %collective-permute-start.2 = (bf16[96,1408]{1,0:T(8,128)(2,1)S(1)}, bf16[96,1408]{1,0:T(8,128)(2,1)S(1)}, u32[]{:S(2)}, u32[]{:S(2)}) collective-permute-start(bf16[96,1408]{1,0:T(8,128)(2,1)S(1)} %get-tuple-element.12), channel_id=1, source_target_pairs={{0,24},{1,25},{2,26},{3,27},{4,28},{5,29},{6,30},{7,31},{8,0},{9,1... | collective-permute-start | bytes 811016 | tf_op jit(solution)/shard_map/ppermute | solution.py:18
  25.8 10.1 %all-to-all-start = ((bf16[8,176,128]{2,1,0:T(8,128)(2,1)}), bf16[8,176,128]{2,1,0:T(8,128)(2,1)S(1)}, u32[]{:S(2)}, u32[]{:S(2)}) async-start(bf16[8,176,128]{2,1,0:T(8,128)(2,1)} %bitcast.22), calls=%async_computation | async-start | bytes 720896 | tf_op jit(solution)/shard_map/all_to_all | solution.py:166
  36.9 3.7 %collective-permute-start.3 = (bf16[3,96,1408]{2,1,0:T(8,128)(2,1)}, bf16[3,96,1408]{2,1,0:T(8,128)(2,1)}, u32[]{:S(2)}, u32[]{:S(2)}) collective-permute-start(bf16[3,96,1408]{2,1,0:T(8,128)(2,1)} %pad_maximum_fusion.3), channel_id=1, source_target_pairs={{0,32},{32,0},{64,96},{96,64},{128,160},{160,128},{192,224},{224,1... | collective-permute-start | bytes 2433032 | tf_op jit(solution)/shard_map/ppermute | solution.py:139
  45.5 2.1 %all-to-all-done = bf16[8,176,128]{2,1,0:T(8,128)(2,1)S(1)} async-done(((bf16[8,176,128]{2,1,0:T(8,128)(2,1)}), bf16[8,176,128]{2,1,0:T(8,128)(2,1)S(1)}, u32[]{:S(2)}, u32[]{:S(2)}) %all-to-all-start) | async-done | bytes 360480 | tf_op jit(solution)/shard_map/all_to_all | solution.py:166
  49.8 3.5 %all-to-all-start.1 = ((bf16[4,864,128]{2,1,0:T(8,128)(2,1)}), bf16[4,864,128]{2,1,0:T(8,128)(2,1)S(1)}, u32[]{:S(2)}, u32[]{:S(2)}) async-start(bf16[4,864,128]{2,1,0:T(8,128)(2,1)} %dynamic_update_slice.7), calls=%async_computation.1 | async-start | bytes 1769472 | tf_op jit(solution)/shard_map/all_to_all | solution.py:170
  53.4 2.2 %broadcast_select_fusion.1 = (bf16[3,96,1408]{2,1,0:T(8,128)(2,1)S(1)}, bf16[3,96,1408]{2,1,0:T(8,128)(2,1)}) fusion(bf16[3,96,1408]{2,1,0:T(8,128)(2,1)} %collective-permute-done.3, pred[]{:T(512)S(6)} %eq.2, bf16[1,96,1408]{2,1,0:T(8,128)(2,1)S(1)} %bitcast.103, bf16[1,96,1408]{2,1,0:T(8,128)(2,1)S(1)} %bitcast.101, bf16[1,96,1408]{2,1,0:T(8,128)(2,1)S(1)} %bitcast.99), kind=kLoop, calls=%fused_computation.21 | loop fusion | flops 1622016 | bytes 3244033 | tf_op jit(solution)/shard_map/jit(_where)/select_n | solution.py:140
  57.2 6.0 %all-to-all-done.1 = bf16[4,864,128]{2,1,0:T(8,128)(2,1)S(1)} async-done(((bf16[4,864,128]{2,1,0:T(8,128)(2,1)}), bf16[4,864,128]{2,1,0:T(8,128)(2,1)S(1)}, u32[]{:S(2)}, u32[]{:S(2)}) %all-to-all-start.1) | async-done | bytes 884768 | tf_op jit(solution)/shard_map/all_to_all | solution.py:170
  65.3 6.3 %collective-permute-start.10 = (bf16[4,512,128]{2,1,0:T(8,128)(2,1)S(1)}, bf16[4,512,128]{2,1,0:T(8,128)(2,1)S(1)}, u32[]{:S(2)}, u32[]{:S(2)}) collective-permute-start(bf16[4,512,128]{2,1,0:T(8,128)(2,1)S(1)} %slice.111), channel_id=1, source_target_pairs={{0,32},{32,0},{64,96},{96,64},{128,160},{160,128},{192,224},{224,1... | collective-permute-start | bytes 1572872 | tf_op jit(solution)/shard_map/ppermute | solution.py:139
  73.4 2.5 %bitcast_convert_fusion = bf16[4,128,768]{2,1,0:T(8,128)(2,1)S(1)} fusion(bf16[4,8,128,128]{3,2,1,0:T(8,128)(2,1)S(1)} %bitcast.104, bf16[8,1824,128]{2,1,0:T(8,128)(2,1)} %bitcast.96), kind=kOutput, calls=%fused_computation.10 | convolution fusion | flops 805699584 | bytes 3407872 | tf_op jit(solution)/shard_map/xyed,yte->xdt/dot_general | solution.py:175
  75.8 14.4 %all_to_all.29 = bf16[4,128,768]{2,1,0:T(8,128)(2,1)S(1)} all-to-all(bf16[4,128,768]{2,1,0:T(8,128)(2,1)S(1)} %bitcast_convert_fusion), channel_id=1, replica_groups={{0,8,16,24},{1,9,17,25},{2,10,18,26},{3,11,19,27},{4,12,20,28},{5,13,21..., dimensions={0} | all-to-all | bytes 1572864 | tf_op jit(solution)/shard_map/all_to_all | solution.py:176
  91.6 6.8 %all-to-all-start.3 = ((bf16[8,128,768]{2,1,0:T(8,128)(2,1)}), bf16[8,128,768]{2,1,0:T(8,128)(2,1)S(1)}, u32[]{:S(2)}, u32[]{:S(2)}) async-start(bf16[8,128,768]{2,1,0:T(8,128)(2,1)} %broadcast_in_dim.2), calls=%async_computation.3 | async-start | bytes 3145728 | tf_op jit(solution)/shard_map/all_to_all | solution.py:183
  104.0 2.4 %collective-permute-start.5 = (bf16[176,768]{1,0:T(8,128)(2,1)S(1)}, bf16[176,768]{1,0:T(8,128)(2,1)S(1)}, u32[]{:S(2)}, u32[]{:S(2)}) collective-permute-start(bf16[176,768]{1,0:T(8,128)(2,1)S(1)} %fusion.18), channel_id=1, source_target_pairs={{0,16},{1,17},{2,18},{3,19},{4,20},{5,21},{6,22},{7,23},{8,24},{9,... | collective-permute-start | bytes 811016 | tf_op jit(solution)/shard_map/ppermute | solution.py:18
  107.0 2.9 %collective-permute-start.6 = (bf16[176,768]{1,0:T(8,128)(2,1)S(1)}, bf16[176,768]{1,0:T(8,128)(2,1)S(1)}, u32[]{:S(2)}, u32[]{:S(2)}) collective-permute-start(bf16[176,768]{1,0:T(8,128)(2,1)S(1)} %fusion.21), channel_id=1, source_target_pairs={{0,8},{1,9},{2,10},{3,11},{4,12},{5,13},{6,14},{7,15},{8,16},{9,17... | collective-permute-start | bytes 811016 | tf_op jit(solution)/shard_map/ppermute | solution.py:18
  110.6 3.6 %collective-permute-start.4 = (bf16[176,768]{1,0:T(8,128)(2,1)S(1)}, bf16[176,768]{1,0:T(8,128)(2,1)S(1)}, u32[]{:S(2)}, u32[]{:S(2)}) collective-permute-start(bf16[176,768]{1,0:T(8,128)(2,1)S(1)} %fusion.15), channel_id=1, source_target_pairs={{0,24},{1,25},{2,26},{3,27},{4,28},{5,29},{6,30},{7,31},{8,0},{9,1... | collective-permute-start | bytes 811016 | tf_op jit(solution)/shard_map/ppermute | solution.py:18
  114.2 6.7 %collective-permute-done.6 = bf16[176,768]{1,0:T(8,128)(2,1)S(1)} collective-permute-done((bf16[176,768]{1,0:T(8,128)(2,1)S(1)}, bf16[176,768]{1,0:T(8,128)(2,1)S(1)}, u32[]{:S(2)}, u32[]{:S(2)}) %collective-permute-start.6) | collective-permute-done | bytes 270368 | tf_op jit(solution)/shard_map/ppermute | solution.py:18
  121.6 2.1 %collective-permute-start.9 = (bf16[176,768]{1,0:T(8,128)(2,1)S(1)}, bf16[176,768]{1,0:T(8,128)(2,1)S(1)}, u32[]{:S(2)}, u32[]{:S(2)}) collective-permute-start(bf16[176,768]{1,0:T(8,128)(2,1)S(1)} %multiply_convert_fusion), channel_id=1, source_target_pairs={{0,24},{1,25},{2,26},{3,27},{4,28},{5,29},{6,30},{7,31},{8,0},{9,1... | collective-permute-start | bytes 811016 | tf_op jit(solution)/shard_map/ppermute | solution.py:18
  123.7 2.1 %collective-permute-start.8 = (bf16[176,768]{1,0:T(8,128)(2,1)S(1)}, bf16[176,768]{1,0:T(8,128)(2,1)S(1)}, u32[]{:S(2)}, u32[]{:S(2)}) collective-permute-start(bf16[176,768]{1,0:T(8,128)(2,1)S(1)} %multiply_convert_fusion), channel_id=1, source_target_pairs={{0,16},{1,17},{2,18},{3,19},{4,20},{5,21},{6,22},{7,23},{8,24},{9,... | collective-permute-start | bytes 811016 | tf_op jit(solution)/shard_map/ppermute | solution.py:18
  125.9 3.0 %collective-permute-start.7 = (bf16[176,768]{1,0:T(8,128)(2,1)S(1)}, bf16[176,768]{1,0:T(8,128)(2,1)S(1)}, u32[]{:S(2)}, u32[]{:S(2)}) collective-permute-start(bf16[176,768]{1,0:T(8,128)(2,1)S(1)} %multiply_convert_fusion), channel_id=1, source_target_pairs={{0,8},{1,9},{2,10},{3,11},{4,12},{5,13},{6,14},{7,15},{8,16},{9,17... | collective-permute-start | bytes 811016 | tf_op jit(solution)/shard_map/ppermute | solution.py:18
  130.4 2.3 %collective-permute-done.8 = bf16[176,768]{1,0:T(8,128)(2,1)S(1)} collective-permute-done((bf16[176,768]{1,0:T(8,128)(2,1)S(1)}, bf16[176,768]{1,0:T(8,128)(2,1)S(1)}, u32[]{:S(2)}, u32[]{:S(2)}) %collective-permute-start.8) | collective-permute-done | bytes 270368 | tf_op jit(solution)/shard_map/ppermute | solution.py:18
  132.7 6.7 %collective-permute-done.7 = bf16[176,768]{1,0:T(8,128)(2,1)S(1)} collective-permute-done((bf16[176,768]{1,0:T(8,128)(2,1)S(1)}, bf16[176,768]{1,0:T(8,128)(2,1)S(1)}, u32[]{:S(2)}, u32[]{:S(2)}) %collective-permute-start.7) | collective-permute-done | bytes 270368 | tf_op jit(solution)/shard_map/ppermute | solution.py:18
  141.9 7.2 %shard_map.84 = f32[32,128]{1,0:T(8,128)S(1)} custom-call(s32[1]{0:T(128)} %bitcast.kx_ref, bf16[4,176,768]{2,1,0:T(8,128)(2,1)S(1)} %copy-done.2, bf16[1024,768]{1,0:T(8,128)(2,1)S(1)} %bitcast.86, bf16[8,2,4,2,176,128]{5,4,3,2,1,0:T(8,128)(2,1)} %bitcast.109), custom_call_target="tpu_custom_call" | custom-call | flops 4429185024 | bytes 9000000 | tf_op jit(solution)/shard_map/pallas_call | solution.py:111
  149.0 15.3 %all_to_all.30 = f32[32,1,128]{2,1,0:T(1,128)S(1)} all-to-all(f32[32,1,128]{2,1,0:T(1,128)S(1)} %bitcast.87), channel_id=1, replica_groups=mesh['dp'=16,'tensor'=32] {'tensor'}, dimensions={0} | all-to-all | bytes 32768 | tf_op jit(solution)/shard_map/all_to_all | solution.py:191
  (68 shorter events, 30.4 us)
Async XLA Ops:
  6.5 34.0 %copy-start = (bf16[4096,128]{1,0:T(8,128)(2,1)S(1)}, bf16[4096,128]{1,0:T(8,128)(2,1)}, u32[]{:S(2)}) copy-start(bf16[4096,128]{1,0:T(8,128)(2,1)} %param.10) | copy-start | bytes 3145732
  6.5 18.3 %copy-start.5 = (bf16[4,172,256]{2,0,1:T(4,128)(2,1)S(1)}, bf16[4,172,256]{2,0,1:T(4,128)(2,1)}, u32[]{:S(2)}) copy-start(bf16[4,172,256]{2,0,1:T(4,128)(2,1)} %param.12) | copy-start | bytes 1056772
  6.5 66.8 %all-gather.6.cloned.1.call-start = ((), (), s32[]{:S(2)}) async-start(), calls=%async_computation.6 | async-start | bytes 4202496 | tf_op jit(solution)/shard_map/all_gather | solution.py:152
  8.6 1.5 copy-start.1
  11.9 24.0 %collective-permute-start = (bf16[96,1408]{1,0:T(8,128)(2,1)S(1)}, bf16[96,1408]{1,0:T(8,128)(2,1)S(1)}, u32[]{:S(2)}, u32[]{:S(2)}) collective-permute-start(bf16[96,1408]{1,0:T(8,128)(2,1)S(1)} %get-tuple-element.10), channel_id=1, source_target_pairs={{0,8},{1,9},{2,10},{3,11},{4,12},{5,13},{6,14},{7,15},{8,16},{9,17... | collective-permute-start | bytes 811016 | tf_op jit(solution)/shard_map/ppermute | solution.py:18
  15.8 20.0 %collective-permute-start.1 = (bf16[96,1408]{1,0:T(8,128)(2,1)S(1)}, bf16[96,1408]{1,0:T(8,128)(2,1)S(1)}, u32[]{:S(2)}, u32[]{:S(2)}) collective-permute-start(bf16[96,1408]{1,0:T(8,128)(2,1)S(1)} %get-tuple-element.11), channel_id=1, source_target_pairs={{0,16},{1,17},{2,18},{3,19},{4,20},{5,21},{6,22},{7,23},{8,24},{9,... | collective-permute-start | bytes 811016 | tf_op jit(solution)/shard_map/ppermute | solution.py:18
  20.2 15.7 %collective-permute-start.2 = (bf16[96,1408]{1,0:T(8,128)(2,1)S(1)}, bf16[96,1408]{1,0:T(8,128)(2,1)S(1)}, u32[]{:S(2)}, u32[]{:S(2)}) collective-permute-start(bf16[96,1408]{1,0:T(8,128)(2,1)S(1)} %get-tuple-element.12), channel_id=1, source_target_pairs={{0,24},{1,25},{2,26},{3,27},{4,28},{5,29},{6,30},{7,31},{8,0},{9,1... | collective-permute-start | bytes 811016 | tf_op jit(solution)/shard_map/ppermute | solution.py:18
  25.8 21.8 %all-to-all-start = ((bf16[8,176,128]{2,1,0:T(8,128)(2,1)}), bf16[8,176,128]{2,1,0:T(8,128)(2,1)S(1)}, u32[]{:S(2)}, u32[]{:S(2)}) async-start(bf16[8,176,128]{2,1,0:T(8,128)(2,1)} %bitcast.22), calls=%async_computation | async-start | bytes 720896 | tf_op jit(solution)/shard_map/all_to_all | solution.py:166
  36.9 16.5 %collective-permute-start.3 = (bf16[3,96,1408]{2,1,0:T(8,128)(2,1)}, bf16[3,96,1408]{2,1,0:T(8,128)(2,1)}, u32[]{:S(2)}, u32[]{:S(2)}) collective-permute-start(bf16[3,96,1408]{2,1,0:T(8,128)(2,1)} %pad_maximum_fusion.3), channel_id=1, source_target_pairs={{0,32},{32,0},{64,96},{96,64},{128,160},{160,128},{192,224},{224,1... | collective-permute-start | bytes 2433032 | tf_op jit(solution)/shard_map/ppermute | solution.py:139
  49.8 13.4 %all-to-all-start.1 = ((bf16[4,864,128]{2,1,0:T(8,128)(2,1)}), bf16[4,864,128]{2,1,0:T(8,128)(2,1)S(1)}, u32[]{:S(2)}, u32[]{:S(2)}) async-start(bf16[4,864,128]{2,1,0:T(8,128)(2,1)} %dynamic_update_slice.7), calls=%async_computation.1 | async-start | bytes 1769472 | tf_op jit(solution)/shard_map/all_to_all | solution.py:170
  53.3 87.3 %all-gather.4.cloned.1.call-start = ((), (), s32[]{:S(2)}) async-start(), calls=%async_computation.5 | async-start | bytes 6127616 | tf_op jit(solution)/shard_map/all_gather | solution.py:173
  55.6 0.9 copy-start.3
  64.4 0.8 copy-start.4
  65.3 7.8 %collective-permute-start.10 = (bf16[4,512,128]{2,1,0:T(8,128)(2,1)S(1)}, bf16[4,512,128]{2,1,0:T(8,128)(2,1)S(1)}, u32[]{:S(2)}, u32[]{:S(2)}) collective-permute-start(bf16[4,512,128]{2,1,0:T(8,128)(2,1)S(1)} %slice.111), channel_id=1, source_target_pairs={{0,32},{32,0},{64,96},{96,64},{128,160},{160,128},{192,224},{224,1... | collective-permute-start | bytes 1572872 | tf_op jit(solution)/shard_map/ppermute | solution.py:139
  91.6 49.0 %all-to-all-start.3 = ((bf16[8,128,768]{2,1,0:T(8,128)(2,1)}), bf16[8,128,768]{2,1,0:T(8,128)(2,1)S(1)}, u32[]{:S(2)}, u32[]{:S(2)}) async-start(bf16[8,128,768]{2,1,0:T(8,128)(2,1)} %broadcast_in_dim.2), calls=%async_computation.3 | async-start | bytes 3145728 | tf_op jit(solution)/shard_map/all_to_all | solution.py:183
  104.0 10.2 %collective-permute-start.5 = (bf16[176,768]{1,0:T(8,128)(2,1)S(1)}, bf16[176,768]{1,0:T(8,128)(2,1)S(1)}, u32[]{:S(2)}, u32[]{:S(2)}) collective-permute-start(bf16[176,768]{1,0:T(8,128)(2,1)S(1)} %fusion.18), channel_id=1, source_target_pairs={{0,16},{1,17},{2,18},{3,19},{4,20},{5,21},{6,22},{7,23},{8,24},{9,... | collective-permute-start | bytes 811016 | tf_op jit(solution)/shard_map/ppermute | solution.py:18
  107.0 7.1 %copy-start.6 = (s32[6]{0:T(128)S(1)}, s32[6]{0:T(128)}, u32[]{:S(2)}) copy-start(s32[6]{0:T(128)} %param.15) | copy-start | bytes 76
  107.0 14.0 %collective-permute-start.6 = (bf16[176,768]{1,0:T(8,128)(2,1)S(1)}, bf16[176,768]{1,0:T(8,128)(2,1)S(1)}, u32[]{:S(2)}, u32[]{:S(2)}) collective-permute-start(bf16[176,768]{1,0:T(8,128)(2,1)S(1)} %fusion.21), channel_id=1, source_target_pairs={{0,8},{1,9},{2,10},{3,11},{4,12},{5,13},{6,14},{7,15},{8,16},{9,17... | collective-permute-start | bytes 811016 | tf_op jit(solution)/shard_map/ppermute | solution.py:18
  110.6 10.4 %collective-permute-start.4 = (bf16[176,768]{1,0:T(8,128)(2,1)S(1)}, bf16[176,768]{1,0:T(8,128)(2,1)S(1)}, u32[]{:S(2)}, u32[]{:S(2)}) collective-permute-start(bf16[176,768]{1,0:T(8,128)(2,1)S(1)} %fusion.15), channel_id=1, source_target_pairs={{0,24},{1,25},{2,26},{3,27},{4,28},{5,29},{6,30},{7,31},{8,0},{9,1... | collective-permute-start | bytes 811016 | tf_op jit(solution)/shard_map/ppermute | solution.py:18
  121.6 8.8 %collective-permute-start.9 = (bf16[176,768]{1,0:T(8,128)(2,1)S(1)}, bf16[176,768]{1,0:T(8,128)(2,1)S(1)}, u32[]{:S(2)}, u32[]{:S(2)}) collective-permute-start(bf16[176,768]{1,0:T(8,128)(2,1)S(1)} %multiply_convert_fusion), channel_id=1, source_target_pairs={{0,24},{1,25},{2,26},{3,27},{4,28},{5,29},{6,30},{7,31},{8,0},{9,1... | collective-permute-start | bytes 811016 | tf_op jit(solution)/shard_map/ppermute | solution.py:18
  123.7 9.0 %collective-permute-start.8 = (bf16[176,768]{1,0:T(8,128)(2,1)S(1)}, bf16[176,768]{1,0:T(8,128)(2,1)S(1)}, u32[]{:S(2)}, u32[]{:S(2)}) collective-permute-start(bf16[176,768]{1,0:T(8,128)(2,1)S(1)} %multiply_convert_fusion), channel_id=1, source_target_pairs={{0,16},{1,17},{2,18},{3,19},{4,20},{5,21},{6,22},{7,23},{8,24},{9,... | collective-permute-start | bytes 811016 | tf_op jit(solution)/shard_map/ppermute | solution.py:18
  125.9 13.6 %collective-permute-start.7 = (bf16[176,768]{1,0:T(8,128)(2,1)S(1)}, bf16[176,768]{1,0:T(8,128)(2,1)S(1)}, u32[]{:S(2)}, u32[]{:S(2)}) collective-permute-start(bf16[176,768]{1,0:T(8,128)(2,1)S(1)} %multiply_convert_fusion), channel_id=1, source_target_pairs={{0,8},{1,9},{2,10},{3,11},{4,12},{5,13},{6,14},{7,15},{8,16},{9,17... | collective-permute-start | bytes 811016 | tf_op jit(solution)/shard_map/ppermute | solution.py:18
  140.6 1.2 copy-start.2
Sparse Core Ops, SparseCore 0:
  9.4 58.3 all-gather.5
  69.9 47.4 all-gather.3
